TPU v7x, 32 devices: a whole 2x2x4 slice. The times are simulated.
32 devices in a mesh: fsdp: 8 (over y, x, core), seq: 4 (over z).
Axes of the slice: x: 2, y: 2, z: 4, core: 2. Of those that a mesh axis runs over, the one named last changes fastest.
Arguments:
- source_copy: bfloat16 [8, 1024, 512], P('fsdp', 'seq'), may hold values from -6 to 6
- target_embed: bfloat16 [8, 1024, 512], P('fsdp', 'seq'), may hold values from -6 to 6
- glance_mask: int32 [8, 1024], P('fsdp', 'seq'), may hold values 0 or 1
- segment_ids: int32 [8, 1024], P('fsdp', 'seq'), may hold values from 0 to 6, as said below
- pad_mask: int32 [8, 1024], P('fsdp', 'seq'), may hold values from 0 to 1, as said below
- encoder_out: bfloat16 [8, 1024, 512], P('fsdp', 'seq'), may hold values from -6 to 6
- out_grad: bfloat16 [8, 1024, 512], P('fsdp', 'seq'), may hold values from -6 to 6
- self_query: bfloat16 [512, 512], P(('fsdp', 'seq')), may hold values from -0.25 to 0.25
- self_key: bfloat16 [512, 512], P(('fsdp', 'seq')), may hold values from -0.25 to 0.25
- self_value: bfloat16 [512, 512], P(('fsdp', 'seq')), may hold values from -0.25 to 0.25
- self_output: bfloat16 [512, 512], P(('fsdp', 'seq')), may hold values from -1 to 1
- norm1_gain: bfloat16 [512], P(('fsdp', 'seq')), may hold values from 0.5 to 1.5
- norm1_shift: bfloat16 [512], P(('fsdp', 'seq')), may hold values from -3 to 3
- cross_query: bfloat16 [512, 512], P(('fsdp', 'seq')), may hold values from -0.25 to 0.25
- cross_key: bfloat16 [512, 512], P(('fsdp', 'seq')), may hold values from -0.25 to 0.25
- cross_value: bfloat16 [512, 512], P(('fsdp', 'seq')), may hold values from -0.25 to 0.25
- cross_output: bfloat16 [512, 512], P(('fsdp', 'seq')), may hold values from -1 to 1
- norm2_gain: bfloat16 [512], P(('fsdp', 'seq')), may hold values from 0.5 to 1.5
- norm2_shift: bfloat16 [512], P(('fsdp', 'seq')), may hold values from -3 to 3
- inner_weight: bfloat16 [512, 2048], P(('fsdp', 'seq')), may hold values from -0.25 to 0.25
- outer_weight: bfloat16 [2048, 512], P(('fsdp', 'seq')), may hold values from -0.125 to 0.125
- norm3_gain: bfloat16 [512], P(('fsdp', 'seq')), may hold values from 0.5 to 1.5
- norm3_shift: bfloat16 [512], P(('fsdp', 'seq')), may hold values from -3 to 3
Outputs:
- layer_out: bfloat16 [8, 1024, 512], P('fsdp', 'seq')
- input_grad: float32 [8, 1024, 512], P('fsdp', 'seq')
- encoder_grad: float32 [8, 1024, 512], P('fsdp', 'seq')
- grad_self_query: float32 [512, 512], P(('fsdp', 'seq'))
- grad_self_key: float32 [512, 512], P(('fsdp', 'seq'))
- grad_self_value: float32 [512, 512], P(('fsdp', 'seq'))
- grad_self_output: float32 [512, 512], P(('fsdp', 'seq'))
- grad_norm1_gain: float32 [512], P(('fsdp', 'seq'))
- grad_norm1_shift: float32 [512], P(('fsdp', 'seq'))
- grad_cross_query: float32 [512, 512], P(('fsdp', 'seq'))
- grad_cross_key: float32 [512, 512], P(('fsdp', 'seq'))
- grad_cross_value: float32 [512, 512], P(('fsdp', 'seq'))
- grad_cross_output: float32 [512, 512], P(('fsdp', 'seq'))
- grad_norm2_gain: float32 [512], P(('fsdp', 'seq'))
- grad_norm2_shift: float32 [512], P(('fsdp', 'seq'))
- grad_inner_weight: float32 [512, 2048], P(('fsdp', 'seq'))
- grad_outer_weight: float32 [2048, 512], P(('fsdp', 'seq'))
- grad_norm3_gain: float32 [512], P(('fsdp', 'seq'))
- grad_norm3_shift: float32 [512], P(('fsdp', 'seq'))
Inputs may be any that keep to these rules, and one draw needn't show every extreme that they name: `segment_ids`: within a row the numbers start at 0, rise by at most one from a position to the next and reach 6; in every row one document starts at or before position 128 and ends at or after position 896. `pad_mask`: in each row the zeros form a tail of the row, inside the row's last document, which holds a real position.
All inputs are finite; a program needn't handle non-finite values. No bound on the sum of `glance_mask` on one device may be relied on, other than what follows from the above.
Results may differ from a plain program's by a relative error of at most 0.025.
Values may be sent and summed in bfloat16 or wider, within the bound.
No kernel may reach another device: no remote copies, remote signals or barrier semaphores. Data moves between devices by JAX's collectives and lax.ppermute only.
A program may use at most 128 MiB of HBM per device.

v0:
```python
import functools

import jax
import jax.numpy as jnp
from jax import lax
from jax.experimental import pallas as pl
from jax.experimental.pallas import tpu as pltpu
from jax.sharding import PartitionSpec as P

HEADS = 8
HEAD = 64
PAIR = 2 * HEAD
SLOT = HEAD + 16


norm_eps = 1e-05
mask_fill = -1e30

BF = jnp.bfloat16
F32 = jnp.float32
VM = pltpu.VMEM
WHOLE = pl.BlockSpec(memory_space=pltpu.VMEM)
SCALARS = pl.BlockSpec(memory_space=pltpu.SMEM)
APART = pl.BlockSpec(memory_space=pl.ANY)


def shape(*dims, dtype=BF):
    return jax.ShapeDtypeStruct(dims, dtype)


def low(values):
    return values.astype(BF)


def dot(left, right):
    return jnp.dot(left, right, preferred_element_type=F32)


def dot_t(left, right):
    return lax.dot_general(left, right, (((1,), (1,)), ((), ())), preferred_element_type=F32)


def head_cols(block, head):
    pair = block[:, head // 2 * PAIR : (head // 2 + 1) * PAIR]
    lane = lax.broadcasted_iota(jnp.int32, pair.shape, 1)
    return jnp.where((lane >= HEAD) == (head % 2 == 1), pair, jnp.zeros_like(pair))


def head_rows(block, head):
    mine = block[head * HEAD : (head + 1) * HEAD, :]
    rest = jnp.zeros_like(mine)
    return jnp.concatenate([mine, rest] if head % 2 == 0 else [rest, mine], axis=0)


def chunk_of(pos, seq, c, e, d):
    return (pos[0] ^ (2 * e + c)) * seq + (pos[1] ^ d)


def in_order(pos, parts, target, col, sub=1):
    width = target.shape[1]
    for c, sides in enumerate(parts):
        if len(sides) == 1:
            sides = [sides[0].at[e] for e in range(sides[0].shape[0])]
        for e, part in enumerate(sides):
            for d in range(part.shape[0]):
                rows = part.shape[1]
                first = chunk_of(pos, part.shape[0], c, e, d) * (rows * sub)
                for r in range(sub):
                    start = pl.multiple_of(first + r * rows, rows)
                    target[pl.ds(start, rows), :] = part[
                        d, :, col + r * width : col + (r + 1) * width
                    ]


def by_distance(pos, source, parts, col, sub=1):
    width = source.shape[1]
    for c, part in enumerate(parts):
        for e in range(part.shape[0]):
            for d in range(part.shape[1]):
                rows = part.shape[2]
                first = chunk_of(pos, part.shape[1], c, e, d) * (rows * sub)
                for r in range(sub):
                    start = pl.multiple_of(first + r * rows, rows)
                    part[e, d, :, col + r * width : col + (r + 1) * width] = source[
                        pl.ds(start, rows), :
                    ]


def normalise(flow):
    centre = jnp.mean(flow, axis=1, keepdims=True)
    centered = flow - centre
    spread = jnp.mean(centered * centered, axis=1, keepdims=True)
    inverse = lax.rsqrt(spread + norm_eps)
    return centered * inverse, inverse


def normalise_back(grad, unit, inverse, gain):
    scaled = grad * gain
    mean_one = jnp.mean(scaled, axis=1, keepdims=True)
    mean_two = jnp.mean(scaled * unit, axis=1, keepdims=True)
    grad_flow = inverse * (scaled - mean_one - unit * mean_two)
    return (
        grad_flow,
        jnp.sum(grad * unit, axis=0, keepdims=True),
        jnp.sum(grad, axis=0, keepdims=True),
    )


def set_bias(key_rows, query_row, bias):
    count = query_row.shape[1]
    for d in range(len(key_rows)):
        column = jnp.broadcast_to(key_rows[d], (128, count)).T
        column = jnp.concatenate([column] * (count // 128), axis=1)
        bias[d * count : (d + 1) * count, :] = jnp.where(column == query_row, 0.0, mask_fill)


def set_values(values, slots, first):
    turned = values.T
    count = values.shape[0]
    cols = slice(first, first + count)
    for head in range(HEADS):
        slots[head * SLOT : head * SLOT + HEAD, cols] = turned[head * HEAD : (head + 1) * HEAD, :]
        slots[head * SLOT + HEAD : (head + 1) * SLOT, cols] = jnp.ones((SLOT - HEAD, count), BF)


def finish_head(head, exp_scores, slots, mixed_out, inverse_out):
    summed = dot(slots[head * SLOT : (head + 1) * SLOT, :], exp_scores)
    inverse = 1.0 / summed[HEAD : HEAD + 1, :]
    mixed_out[head * HEAD : (head + 1) * HEAD, :] = low(summed[:HEAD, :] * inverse)
    inverse_out[head : head + 1, :] = inverse


def attend(query, keys, slots, bias, exps, exps_out, sem, mixed_out, inverse_out):
    count = query.shape[0]

    def scores_of(head):
        pair_keys = keys[:, head // 2 * PAIR : (head // 2 + 1) * PAIR]
        return dot_t(pair_keys, head_cols(query, head)) + bias[...]

    scores, before = scores_of(0), None
    for head in range(HEADS):
        after = scores_of(head + 1) if head + 1 < HEADS else None
        if head > 0:
            finish_head(head - 1, before, slots, mixed_out, inverse_out)
        top = jnp.max(scores, axis=0, keepdims=True)
        before = low(jnp.exp(scores - top))
        exps[head // 2, :, head % 2 * count : (head % 2 + 1) * count] = before
        if head % 2 == 1:
            pltpu.make_async_copy(
                exps.at[head // 2], exps_out.at[head // 2], sem.at[head // 2]
            ).start()
        scores = after
    finish_head(HEADS - 1, before, slots, mixed_out, inverse_out)
    for pair in range(HEADS // 2):
        pltpu.make_async_copy(exps.at[pair], exps_out.at[pair], sem.at[pair]).wait()


def fetch(exps_in, exps, sem, pair):
    return pltpu.make_async_copy(exps_in.at[pair], exps.at[pair], sem.at[pair])


def attend_back(
    query, keys_t, values, mixed_t, grad_t, grad, exps_in, exps, sem, query_t_out, kv_out
):
    count, feat = query.shape

    def head_dot(head):
        rows = slice(head * HEAD, (head + 1) * HEAD)
        both = grad_t[rows, :].astype(F32) * mixed_t[rows, :].astype(F32)
        return jnp.sum(both, axis=0, keepdims=True)

    def grad_probs(pair):
        heads = (2 * pair, 2 * pair + 1)
        both = jnp.concatenate([head_rows(grad_t, head) for head in heads], axis=1)
        return dot(values[:, pair * PAIR : (pair + 1) * PAIR], both)

    def pair_cols(block, pair):
        return jnp.concatenate([head_cols(block, 2 * pair), head_cols(block, 2 * pair + 1)], axis=0)

    row_dots = [head_dot(head) for head in range(HEADS)]
    grad_prob = grad_probs(0)
    for pair in range(HEADS // 2):
        after = grad_probs(pair + 1) if pair + 1 < HEADS // 2 else None
        fetch(exps_in, exps, sem, pair).wait()
        cols = slice(pair * PAIR, (pair + 1) * PAIR)
        exp_scores = exps[pair]
        row_dot = jnp.concatenate([row_dots[2 * pair], row_dots[2 * pair + 1]], axis=1)
        grad_scores = low(exp_scores.astype(F32) * (grad_prob - row_dot))
        kv_out[:, feat + pair * PAIR : feat + (pair + 1) * PAIR] = low(
            dot(exp_scores, pair_cols(grad, pair))
        )
        kv_out[:, cols] = low(dot(grad_scores, pair_cols(query, pair)))
        for head in (2 * pair, 2 * pair + 1):
            rows = slice(head * HEAD, (head + 1) * HEAD)
            mine = grad_scores[:, head % 2 * count : (head % 2 + 1) * count]
            query_t_out[rows, :] = low(dot(keys_t[rows, :], mine) * HEAD ** (-0.5))
        grad_prob = after


def over_sums(grad_t, inverse):
    return low(
        jnp.concatenate(
            [
                grad_t[head * HEAD : (head + 1) * HEAD, :] * inverse[head : head + 1, :]
                for head in range(HEADS)
            ],
            axis=0,
        )
    )


def send_out(pairs, sem):
    copies = [pltpu.make_async_copy(a, b, sem.at[i]) for i, (a, b) in enumerate(pairs)]
    for copy in copies:
        copy.start()
    return copies


def self_attend_body(n_blocks, n_parts, pos, *refs):
    blocks, refs = refs[:n_blocks], refs[n_blocks:]
    near, far, refs = refs[:n_parts], refs[n_parts : 2 * n_parts], refs[2 * n_parts :]
    (ids, q_out, v_out, kt_out, mixed_out, inverse_out, kid_out, exps_out) = refs[:8]
    weight, keys, slots, bias, exps, sem, values, keys_t, out_sem = refs[8:]
    count, feat = q_out.shape
    in_order(pos, (near, far), weight, 0)
    query = low(dot(blocks[0][:count, :], weight[:, :feat]))
    query = query * BF(HEAD ** (-0.5))
    q_out[...] = query
    for d, block in enumerate(blocks):
        rows = slice(d * count, (d + 1) * count)
        key = low(dot(block[:count, :], weight[:, feat : 2 * feat]))
        value = low(dot(block[:count, :], weight[:, 2 * feat :]))
        keys[rows, :] = key
        keys_t[:, rows] = key.T
        values[rows, :] = value
        set_values(value, slots, d * count)
        kid_out[d : d + 1, :] = block[count : count + 1, :count].astype(F32)
    copies = send_out(((keys_t, kt_out), (values, v_out)), out_sem)
    set_bias([kid_out[d : d + 1, :] for d in range(n_blocks)], ids[...].astype(F32), bias)
    attend(query, keys, slots, bias, exps, exps_out, sem, mixed_out, inverse_out)
    for copy in copies:
        copy.wait()


def attend_scratch(keys, feat, count):
    return [
        VM((keys, feat), BF),
        VM((HEADS * SLOT, keys), BF),
        VM((keys, count), F32),
        VM((HEADS // 2, keys, 2 * count), BF),
        pltpu.SemaphoreType.DMA((HEADS // 2,)),
        VM((keys, feat), BF),
        VM((feat, keys), BF),
        pltpu.SemaphoreType.DMA((2,)),
    ]


SMALL = ("stack", "join", "add_far", "add_mid", "add_near", "add_one", "add_line")
ROOM = {"self_attend": 22, "cross_attend": 24, "feed": 28, "cross_back": 28, "self_back": 22}


def kernel_call(
    body, outs, out_specs, in_specs, scratch, name, flops, size, after=(), held_in=(), held_out=()
):
    n_in = len(in_specs)
    small = name in SMALL

    def space(place, held):
        return pltpu.VMEM if small or place in held else pltpu.HBM

    def run(*refs):
        body(*refs[:n_in], *refs[n_in + len(after) :])

    single = not isinstance(outs, (tuple, list))
    outs = tuple(
        space(place, held_out)(out.shape, out.dtype)
        for place, out in enumerate([outs] if single else outs)
    )
    outs = outs[0] if single else outs
    call = pl.pallas_call(
        run if after else body,
        out_shape=outs,
        in_specs=in_specs + [APART] * len(after),
        out_specs=out_specs,
        scratch_shapes=scratch,
        compiler_params=pltpu.CompilerParams(vmem_limit_bytes=(4 if small else ROOM.get(name, 12)) * 2**20),
        cost_estimate=pl.CostEstimate(flops=flops, bytes_accessed=size, transcendentals=0),
        name=name,
    )

    def go(*operands):
        operands = [
            x
            if spec is SCALARS
            else pltpu.with_memory_space_constraint(x, space(place, held_in))
            for place, (x, spec) in enumerate(zip(operands, in_specs, strict=True))
        ]
        return call(*operands, *after)

    return go


def self_attend(pos, blocks, ids, near, far, count, feat, after):
    keys = count * len(blocks)
    return kernel_call(
        functools.partial(self_attend_body, len(blocks), len(near)),
        (
            shape(count, feat),
            shape(keys, feat),
            shape(feat, keys),
            shape(feat, count),
            shape(HEADS, count, dtype=F32),
            shape(len(blocks), count, dtype=F32),
            shape(HEADS // 2, keys, 2 * count),
        ),
        [WHOLE] + [APART] * 2 + [WHOLE] * 3 + [APART],
        [SCALARS] + [WHOLE] * (len(blocks) + 2 * len(near) + 1),
        [VM((feat, 3 * feat), BF)] + attend_scratch(keys, feat, count),
        "self_attend",
        12 * 10**9,
        20 * 10**6,
        after,
    )(pos, *blocks, *near, *far, ids)


def cross_attend_body(n_blocks, n_parts, pos, *refs):
    blocks, refs = refs[:n_blocks], refs[n_blocks:]
    near, far, refs = refs[:n_parts], refs[n_parts : 2 * n_parts], refs[2 * n_parts :]
    (ids, kid, mixed, mixed_one) = refs[:4]
    (vec_out, unit_out, inv_out, q_out, v_out, kt_out, mixed_out, inverse_out) = refs[4:12]
    (unit_two_out, inv_two_out, exps_out) = refs[12:15]
    weight, keys, slots, bias, exps, sem, values, keys_t, out_sem = refs[15:]
    count, feat = q_out.shape
    in_order(pos, (near, far), weight, 0)
    vec_out[...] = weight[:, 5 * feat :].astype(F32).T[:8, :]
    flow = mixed[:count, :].astype(F32) + dot(mixed_one[...].T, weight[:, :feat])
    unit, inverse = normalise(flow)
    unit_out[...] = unit
    inv_out[...] = jnp.broadcast_to(inverse, inv_out.shape)
    normed = unit * vec_out[0:1, :] + vec_out[1:2, :]
    query = low(dot(low(normed), weight[:, feat : 2 * feat])) * BF(HEAD ** (-0.5))
    q_out[...] = query
    for d, block in enumerate(blocks):
        rows = slice(d * count, (d + 1) * count)
        key = low(dot(block[...], weight[:, 2 * feat : 3 * feat]))
        value = low(dot(block[...], weight[:, 3 * feat : 4 * feat]))
        keys[rows, :] = key
        keys_t[:, rows] = key.T
        values[rows, :] = value
        set_values(value, slots, d * count)
    copies = send_out(((keys_t, kt_out), (values, v_out)), out_sem)
    set_bias([kid[d : d + 1, :] for d in range(n_blocks)], ids[...].astype(F32), bias)
    attend(query, keys, slots, bias, exps, exps_out, sem, mixed_out, inverse_out)
    flow = unit_out[...] * vec_out[0:1, :] + vec_out[1:2, :]
    flow = flow + dot(mixed_out[...].T, weight[:, 4 * feat : 5 * feat])
    unit, inverse = normalise(flow)
    unit_two_out[...] = unit
    inv_two_out[...] = jnp.broadcast_to(inverse, inv_two_out.shape)
    for copy in copies:
        copy.wait()


def cross_attend(pos, blocks, ids, kid, mixed, mixed_one, near, far, after):
    count, feat = blocks[0].shape
    keys = count * len(blocks)
    return kernel_call(
        functools.partial(cross_attend_body, len(blocks), len(near)),
        (
            shape(8, feat, dtype=F32),
            shape(count, feat, dtype=F32),
            shape(count, 128, dtype=F32),
            shape(count, feat),
            shape(keys, feat),
            shape(feat, keys),
            shape(feat, count),
            shape(HEADS, count, dtype=F32),
            shape(count, feat, dtype=F32),
            shape(count, 128, dtype=F32),
            shape(HEADS // 2, keys, 2 * count),
        ),
        [WHOLE] * 4 + [APART] * 2 + [WHOLE] * 4 + [APART],
        [SCALARS] + [WHOLE] * (len(blocks) + 2 * len(near) + 4),
        [VM((feat, 5 * feat + 128), BF)] + attend_scratch(keys, feat, count),
        "cross_attend",
        14 * 10**9,
        20 * 10**6,
        after,
        held_out=(8, 9),
    )(pos, *blocks, *near, *far, ids, kid, mixed, mixed_one)


def feed_body(pos, unit_in, inv_in, vec, grad_in, pad, three, *refs):
    (layer_out, flow_out, vec_grad_out, keep_out, away_out) = refs[:5]
    w_out, g_in, g_out = refs[5:]
    feat, wide = g_in.shape
    sub = wide // feat
    w_in = three.at[:, :wide]
    rows = keep_out.shape[2]
    for first in range(0, feat, rows):
        for r in range(sub):
            w_out[first * sub + r * rows : first * sub + (r + 1) * rows, :] = three[
                first : first + rows, wide + r * feat : wide + (r + 1) * feat
            ]
    real = jnp.broadcast_to(pad[...].astype(F32), (128, pad.shape[1])).T[:, :1]
    unit_two = unit_in[...]
    normed_two = unit_two * vec[2:3, :] + vec[3:4, :]
    normed_low = low(normed_two)
    inner = dot(normed_low, w_in[...])
    cube = 0.044715 * inner * inner
    bend = jnp.tanh((2.0 / jnp.pi) ** 0.5 * inner * (1.0 + cube))
    active = low(0.5 * inner * (1.0 + bend))
    slope = 0.5 * (1.0 + bend) + 0.5 * inner * (1.0 - bend * bend) * (2.0 / jnp.pi) ** 0.5 * (
        1.0 + 3.0 * cube
    )
    flow = normed_two + dot(active, w_out[...])
    unit, inverse = normalise(flow)
    layer_out[...] = low((unit * vec[4:5, :] + vec[5:6, :]) * real)
    top = grad_in[...].astype(F32) * real
    grad_flow, grad_gain, grad_shift = normalise_back(top, unit, inverse, vec[4:5, :])
    vec_grad_out[...] = jnp.zeros_like(vec_grad_out)
    vec_grad_out[4:5, :] = grad_gain
    vec_grad_out[5:6, :] = grad_shift
    grad_y = low(grad_flow)
    grad_inner = low(slope * dot_t(grad_y, w_out[...]))
    grad_normed = grad_flow + dot_t(grad_inner, w_in[...])
    grad_flow, grad_gain, grad_shift = normalise_back(
        grad_normed, unit_two, inv_in[:, :1], vec[2:3, :]
    )
    vec_grad_out[2:3, :] = grad_gain
    vec_grad_out[3:4, :] = grad_shift
    flow_out[...] = grad_flow
    g_out[...] = low(dot(active.T, grad_y))
    by_distance(pos, g_out, (keep_out, away_out), wide, sub)
    g_in[...] = low(dot(normed_low.T, grad_inner))
    by_distance(pos, g_in, (keep_out, away_out), 0)


def feed(pos, unit, inverse, vec, out_grad, pad, three, whole):
    count, feat = unit.shape
    wide = three.shape[1] // 2
    return kernel_call(
        feed_body,
        (
            shape(count, feat),
            shape(count, feat, dtype=F32),
            shape(8, feat, dtype=F32),
            shape(*whole),
            shape(*whole),
        ),
        [WHOLE] * 5,
        [SCALARS] + [WHOLE] * 6,
        [VM((wide, feat), BF), VM((feat, wide), BF), VM((wide, feat), BF)],
        "feed",
        6 * 10**9,
        20 * 10**6,
        held_in=(1, 2),
        held_out=(1, 2, 3, 4),
    )(pos, unit, inverse, vec, out_grad, pad, three)


def cross_back_body(n_blocks, n_parts, pos, line, *refs):
    blocks, refs = refs[:n_blocks], refs[n_blocks:]
    near, far, refs = refs[:n_parts], refs[n_parts : 2 * n_parts], refs[2 * n_parts :]
    (flow_in, mixed_two, inverse_two, query, keys_t, values, exps_in) = refs[:7]
    (unit_in, inv_in, vec, vec_grad, mixed_one, inverse_one) = refs[7:13]
    refs = refs[13:]
    flow_out, one_t_out, keep_out, away_out, parts_out = refs[:5]
    weight, grads, kv, query_t, exps, sem = refs[5:]
    count, feat = query.shape
    for pair in range(HEADS // 2):
        fetch(exps_in, exps, sem, pair).start()
    in_order(pos, (near, far), weight, 0)
    grad_y = low(flow_in[...])
    grad_t = over_sums(dot_t(weight[:, 4 * feat : 5 * feat], grad_y), inverse_two)
    grads[:, 4 * feat : 5 * feat] = low(dot(mixed_two[...], grad_y))
    attend_back(
        query, keys_t, values, mixed_two, grad_t, grad_t.T, exps_in, exps, sem, query_t, kv
    )
    grad_query = query_t[...].T
    grad_normed = flow_in[...] + dot_t(grad_query, weight[:, feat : 2 * feat])
    unit = unit_in[...]
    grad_flow, grad_gain, grad_shift = normalise_back(grad_normed, unit, inv_in[:, :1], vec[0:1, :])
    flow_out[...] = grad_flow
    grad_y = low(grad_flow)
    one_t_out[...] = over_sums(dot_t(weight[:, :feat], grad_y), inverse_one)
    grads[:, :feat] = low(dot(mixed_one[...], grad_y))
    normed = low(unit * vec[0:1, :] + vec[1:2, :])
    grads[:, feat : 2 * feat] = low(dot(normed.T, grad_query))
    turned = jnp.concatenate([block[...].T for block in blocks], axis=1)
    grads[:, 2 * feat : 4 * feat] = low(dot(turned, kv[...]))
    rows = jnp.concatenate(
        [grad_gain, grad_shift, vec_grad[2:8, :], jnp.zeros((120, feat), F32)], axis=0
    )
    grads[:, 5 * feat :] = low(rows.T)
    by_distance(pos, grads, (keep_out, away_out), 0)
    for d in range(n_blocks):
        part = dot_t(kv[d * count : (d + 1) * count, :], weight[:, 2 * feat : 4 * feat])
        place = pl.multiple_of((line[0] ^ d) * count, count)
        parts_out[pl.ds(place, count), :] = low(part)


def back_scratch(keys, feat, count):
    return [
        VM((keys, 2 * feat), BF),
        VM((feat, count), BF),
        VM((HEADS // 2, keys, 2 * count), BF),
        pltpu.SemaphoreType.DMA((HEADS // 2,)),
    ]


def cross_back(pos, line, blocks, near, far, after, *args):
    count, feat = blocks[0].shape
    keys = count * len(blocks)
    whole = near[0].shape if len(near) == 1 else (len(near),) + near[0].shape
    return kernel_call(
        functools.partial(cross_back_body, len(blocks), len(near)),
        (
            shape(count, feat, dtype=F32),
            shape(feat, count),
            shape(*whole),
            shape(*whole),
        )
        + (shape(keys, feat),),
        [WHOLE] * 5,
        [SCALARS] * 2 + [WHOLE] * (len(blocks) + 2 * len(near) + 6) + [APART] + [WHOLE] * 6,
        [VM((feat, 5 * feat + 128), BF)] * 2 + back_scratch(keys, feat, count),
        "cross_back",
        15 * 10**9,
        20 * 10**6,
        after,
        held_in=(2 + len(blocks) + 2 * len(near),),
        held_out=range(4),
    )(pos, line, *blocks, *near, *far, *args)


def self_back_body(
    n_blocks, n_parts, pos, line, flow_in, one_t, mixed_one, query, keys_t, values, exps_in, *refs
):
    near, far, refs = refs[:n_parts], refs[n_parts : 2 * n_parts], refs[2 * n_parts :]
    (own_out, query_t_out, kv_out, parts_out) = refs[:4]
    weight, exps, sem = refs[4:]
    count, feat = query.shape
    for pair in range(HEADS // 2):
        fetch(exps_in, exps, sem, pair).start()
    in_order(pos, (near, far), weight, 0)
    grad_t = one_t[...]
    attend_back(
        query,
        keys_t,
        values,
        mixed_one,
        grad_t,
        grad_t.T,
        exps_in,
        exps,
        sem,
        query_t_out,
        kv_out,
    )
    for d in range(n_blocks):
        part = dot_t(kv_out[d * count : (d + 1) * count, :], weight[:, feat:])
        place = pl.multiple_of((line[0] ^ d) * count, count)
        parts_out[pl.ds(place, count), :] = low(part)
    own_out[...] = flow_in[...] + dot_t(query_t_out[...].T, weight[:, :feat])


def self_back(pos, line, n_blocks, near, far, after, *args):
    count, feat = args[3].shape
    keys = count * n_blocks
    return kernel_call(
        functools.partial(self_back_body, n_blocks, len(near)),
        (
            shape(count, feat, dtype=F32),
            shape(feat, count),
            shape(keys, 2 * feat),
            shape(keys, feat),
        ),
        [WHOLE] * 4,
        [SCALARS] * 2 + [WHOLE] * 6 + [APART] + [WHOLE] * (2 * len(near)),
        [VM((feat, 3 * feat), BF)] + back_scratch(keys, feat, count)[2:],
        "self_back",
        12 * 10**9,
        20 * 10**6,
        after,
        held_in=(2, 3),
        held_out=(1, 2),
    )(pos, line, *args, *near, *far)


def self_grads_body(n_blocks, pos, *refs):
    blocks = refs[:n_blocks]
    query_t, kv, keep_out, away_out, grads = refs[n_blocks:]
    feat, count = query_t.shape
    turned = jnp.concatenate([block[:count, :].T for block in blocks], axis=1)
    grads[:, :feat] = low(dot_t(turned[:, :count], query_t[...]))
    grads[:, feat:] = low(dot(turned, kv[...]))
    by_distance(pos, grads, (keep_out, away_out), 0)


def self_grads(pos, blocks, query_t, kv, part_shape, after):
    feat = query_t.shape[0]
    return kernel_call(
        functools.partial(self_grads_body, len(blocks)),
        (shape(*part_shape), shape(*part_shape)),
        [WHOLE] * 2,
        [SCALARS] + [WHOLE] * (len(blocks) + 2),
        [VM((feat, 3 * feat), BF)],
        "self_grads",
        5 * 10**9,
        8 * 10**6,
        after,
        held_in=(1 + len(blocks), 2 + len(blocks)),
        held_out=(0, 1),
    )(pos, *blocks, query_t, kv)


def pack_body(sub, source, target, glance, ids, pad, encoder, *refs):
    refs, encoder_out = refs[:-1], refs[-1]
    encoder_out[...] = encoder[...]
    weights, (vectors, inner, outer, three, early, mixed) = refs[:8], refs[8:]
    rows, feat = weights[0].shape
    count = glance.shape[1]
    wide = inner.shape[1]
    three[:, :wide] = inner[...]
    for r in range(sub):
        three[:, wide + r * feat : wide + (r + 1) * feat] = outer[r * rows : (r + 1) * rows, :]
    for place, weight in enumerate(weights):
        early[:, place * feat : (place + 1) * feat] = weight[...]
    lines = vectors[...].astype(F32)
    lines = jnp.concatenate([lines, jnp.zeros((128 - lines.shape[0], lines.shape[1]), F32)], axis=0)
    early[:, 8 * feat :] = low(lines.T)[:rows, :]
    taken = jnp.broadcast_to(glance[...].astype(F32), (128, count)).T[:, :1]
    mixed[:count, :] = jnp.where(taken > 0.5, target[0], source[0])
    key_ids = jnp.where(pad[...] == 1, ids[...], -1).astype(F32)
    key_ids = jnp.concatenate([key_ids, jnp.zeros((1, feat - count), F32)], axis=1)
    mixed[count:, :] = low(jnp.broadcast_to(key_ids, (16, feat)))


def join_body(n, *refs):
    for i in range(n):
        refs[n][i] = refs[i][...]


def join(parts, *after):
    return kernel_call(
        functools.partial(join_body, len(parts)),
        shape(len(parts), *parts[0].shape),
        WHOLE,
        [WHOLE] * len(parts),
        [],
        "join",
        10**9,
        2 * 10**6,
        after,
    )(*parts)


def stack_body(n, cuts, *refs):
    parts, outs = refs[:n], refs[n:]
    for out, (first, last) in zip(outs, cuts, strict=True):
        for i in range(n):
            out[i] = parts[i][:, first:last]


def stack(parts, cuts, *after):
    rows = parts[0].shape[0]
    return kernel_call(
        functools.partial(stack_body, len(parts), cuts),
        tuple(shape(len(parts), rows, last - first) for first, last in cuts),
        [WHOLE] * len(cuts),
        [WHOLE] * len(parts),
        [],
        "stack",
        2 * 10**10,
        2 * 10**6,
        after,
    )(*parts)


def hold_body(*refs):
    pass


def hold(block, *after, space=None):
    out = shape(*block.shape, dtype=block.dtype)
    if space is not None:
        block = pltpu.with_memory_space_constraint(block, space)
        out = space(block.shape, block.dtype)
    return pl.pallas_call(
        hold_body,
        out_shape=out,
        in_specs=[APART] * (1 + len(after)),
        out_specs=APART,
        input_output_aliases={0: 0},
        name="hold",
    )(block, *after)


def swap(block, axis_name, size, bits):
    return lax.ppermute(block, axis_name, [(i, i ^ bits) for i in range(size)])


def stages(size):
    bits = size.bit_length() - 1
    return [2] * (bits // 2) + [1] * (bits % 2)


def spread(block, axis_name, size, unit, width):
    return [block] + [swap(block, axis_name, size, unit * far) for far in range(1, 1 << width)]


def spread_line(block, axis_name, size, unit, width):
    if width < 2:
        return spread(block, axis_name, size, unit, width)
    far = swap(block, axis_name, size, 2 * unit)
    return [block, swap(block, axis_name, size, unit), far, swap(far, axis_name, size, unit)]


def over_line(block, seq, way):
    blocks = [block]
    unit = 1
    for width in stages(seq):
        got = [way(b, "seq", seq, unit, width) for b in blocks]
        blocks = [g[far] for far in range(1 << width) for g in got]
        unit <<= width
    return blocks


def add_far_body(cut, keep, away, x_send, y_send, x_rest, y_rest):
    for e in range(4):
        both = low(keep[e].astype(F32) + away[e].astype(F32))
        (x_send if e % 2 == 1 else x_rest)[e // 2] = both[:, :, :cut]
        (y_send if e >= 2 else y_rest)[e % 2] = both[:, :, cut:]


def add_one_body(keep, away, *outs):
    for e in range(4):
        outs[e][...] = low(keep[e].astype(F32) + away[e].astype(F32))


def add_line_body(own, first, second, third, *outs):
    for d in range(4):
        total = own[d].astype(F32) + first[d].astype(F32)
        outs[d][...] = low(total + second[d].astype(F32) + third[d].astype(F32))


def add_mid_body(x_rest, x_got, y_rest, y_got, y_send, x_send, x_own, y_own):
    x_own[...] = x_rest[0].astype(F32) + x_got[0].astype(F32)
    y_send[...] = low(x_rest[1].astype(F32) + x_got[1].astype(F32))
    y_own[...] = y_rest[0].astype(F32) + y_got[0].astype(F32)
    x_send[...] = low(y_rest[1].astype(F32) + y_got[1].astype(F32))


def add_near_body(cut, x_own, x_got, y_own, y_got, own, odd, even):
    for d in range(4):
        left = x_own[d] + x_got[d].astype(F32)
        right = y_own[d] + y_got[d].astype(F32)
        if d == 0:
            own[:, :cut] = left
            own[:, cut:] = right
        elif d == 2:
            even[:, :cut] = low(left)
            even[:, cut:] = low(right)
        else:
            odd[d // 2, :, :cut] = low(left)
            odd[d // 2, :, cut:] = low(right)


def add_call(body, outs, operands, after, name):
    return kernel_call(
        body,
        outs,
        [WHOLE] * len(outs),
        [WHOLE] * len(operands),
        [],
        name,
        10**9,
        4 * 10**6,
        after,
    )(*operands)


def far_step(keep, away, after, fsdp):
    cols = keep.shape[3]
    cut = cols // 256 * 128
    dims = keep.shape[1:3]
    outs = [shape(2, *dims, width) for width in (cut, cols - cut) * 2]
    x_send, y_send, x_rest, y_rest = add_call(
        functools.partial(add_far_body, cut), outs, (keep, away), after, "add_far"
    )
    return (x_send, swap(x_send, "fsdp", fsdp, 2), swap(y_send, "fsdp", fsdp, 4), x_rest, y_rest)


def mid_step(far, after, fsdp):
    _, x_got, y_got, x_rest, y_rest = far
    x_dims, y_dims = x_rest.shape[1:], y_rest.shape[1:]
    outs = [shape(*x_dims), shape(*y_dims), shape(*x_dims, dtype=F32), shape(*y_dims, dtype=F32)]
    y_send, x_send, x_own, y_own = add_call(
        add_mid_body, outs, (x_rest, x_got, y_rest, y_got), after, "add_mid"
    )
    return (y_send, swap(y_send, "fsdp", fsdp, 4), swap(x_send, "fsdp", fsdp, 2), x_own, y_own)


def near_step(mid, after):
    _, x_got, y_got, x_own, y_own = mid
    cut = x_own.shape[2]
    rows, cols = x_own.shape[1], cut + y_own.shape[2]
    outs = [shape(rows, cols, dtype=F32), shape(2, rows, cols), shape(rows, cols)]
    return add_call(
        functools.partial(add_near_body, cut), outs, (x_own, x_got, y_own, y_got), after, "add_near"
    )


def finish_line(near, seq, *after):
    own, odd, even = near
    got = swap(odd, "seq", seq, 1)
    if after:
        got = hold(got, *after, space=pltpu.VMEM)
    even = low(even.astype(F32) + got[1].astype(F32))
    return own.astype(F32) + got[0].astype(F32), swap(even, "seq", seq, 2)


def bit_of(axis_name, bit):
    return (lax.axis_index(axis_name) & bit) != 0


def double(block, axis_name, size, bit, place):
    other = swap(block, axis_name, size, bit)
    high = bit_of(axis_name, bit)
    return jnp.where(
        high, jnp.stack([other, block], axis=place), jnp.stack([block, other], axis=place)
    )


def bits_below(size):
    return [1 << k for k in range(size.bit_length() - 1)]


def gather_blocks(shard, fsdp, seq, turned):
    block = shard
    for bit in bits_below(seq):
        block = double(block, "seq", seq, bit, 1)
    upper = bits_below(fsdp)[1:]
    done = []
    for bit in upper[::-1] if turned else upper:
        place = 1 + sum(b > bit for b in done)
        block = double(block, "fsdp", fsdp, bit, place)
        done.append(bit)
    if fsdp > 1:
        block = double(block, "fsdp", fsdp, 1, 1 + len(upper))
    return block.reshape(shard.shape[0], fsdp * seq * shard.shape[1], shard.shape[2])


def halve(block, axis_name, size, bit, place):
    high = bit_of(axis_name, bit).astype(jnp.int32)
    away = lax.dynamic_index_in_dim(block, 1 - high, place, keepdims=False)
    kept = lax.dynamic_index_in_dim(block, high, place, keepdims=False)
    other = swap(away, axis_name, size, bit)
    return (kept.astype(jnp.float32) + other.astype(jnp.float32)).astype(jnp.bfloat16)


def scatter_blocks(whole, fsdp, seq, turned):
    w, depth, cols = whole.shape
    n_up = len(bits_below(fsdp)) - 1
    n_seq = len(bits_below(seq))
    rows = depth // (fsdp * seq)
    block = whole.reshape((w,) + (2,) * (n_up + 1 + n_seq) + (rows, cols))
    block = halve(block, "fsdp", fsdp, 1, 1 + n_up)
    upper = bits_below(fsdp)[1:]
    left = list(upper)
    for bit in upper[::-1] if turned else upper:
        place = 1 + sum(b > bit for b in left)
        block = halve(block, "fsdp", fsdp, bit, place)
        left.remove(bit)
    for bit in bits_below(seq)[::-1]:
        block = halve(block, "seq", seq, bit, 1)
    return block.astype(jnp.float32)


def whole_parts(shard, fsdp, seq):
    whole = gather_blocks(shard[None], fsdp, seq, False)[0]
    parts = whole.reshape(4, 2, 4, -1, whole.shape[1])
    return parts[:, 0], parts[:, 1]


def whole_sum(keep, away, fsdp, seq):
    whole = jnp.stack([keep, away], axis=1).reshape(-1, keep.shape[3])
    return scatter_blocks(whole[None], fsdp, seq, False)[0]


def regroup(three, rows, to, wide):
    feat = three.shape[0]
    sub = wide // feat
    outer = three[:, wide:].reshape(-1, rows, sub, feat).transpose(0, 2, 1, 3)
    outer = outer.reshape(-1, sub, to, feat).transpose(0, 2, 1, 3)
    return jnp.concatenate([three[:, :wide], outer.reshape(feat, sub * feat)], axis=1)


def make(fsdp, seq):
    def on_device(
        source_copy,
        target_embed,
        glance_mask,
        segment_ids,
        pad_mask,
        encoder_out,
        out_grad,
        self_query,
        self_key,
        self_value,
        self_output,
        norm1_gain,
        norm1_shift,
        cross_query,
        cross_key,
        cross_value,
        cross_output,
        norm2_gain,
        norm2_shift,
        inner_weight,
        outer_weight,
        norm3_gain,
        norm3_shift,
    ):
        row_count, loc_count, feat = source_copy.shape
        count = row_count * loc_count
        chunk = self_query.shape[0]
        sub = outer_weight.shape[0] // chunk
        pos = jnp.stack([lax.axis_index("fsdp"), lax.axis_index("seq")]).astype(jnp.int32)
        ids = segment_ids.reshape(1, count)
        pad = pad_mask.reshape(1, count)
        encoder = encoder_out.reshape(count, feat)
        vectors = jnp.stack(
            [norm1_gain, norm1_shift, norm2_gain, norm2_shift, norm3_gain, norm3_shift]
        )
        vectors = jnp.pad(vectors, ((0, 0), (0, 128 - chunk)))
        wide = sub * feat
        three, early, mixed, encoder = kernel_call(
            functools.partial(pack_body, sub),
            (shape(chunk, 2 * wide), shape(chunk, 8 * feat + 128), shape(count + 16, feat), shape(count, feat)),
            [WHOLE] * 4,
            [WHOLE] * 17,
            [],
            "pack",
            10**9,
            2 * 10**6,
        )(
            source_copy,
            target_embed,
            glance_mask.reshape(1, count),
            ids,
            pad,
            encoder,
            self_query,
            self_key,
            self_value,
            self_output,
            cross_query,
            cross_key,
            cross_value,
            cross_output,
            vectors,
            inner_weight,
            outer_weight,
        )
        all_three = lax.all_gather(three, ("fsdp", "seq"), axis=0, tiled=True)
        home = pos
        near_rows = seq == 4 and fsdp == 8 and chunk % 16 == 0
        if near_rows:
            early_blocks = over_line(early, seq, spread)
            mixed_far = swap(mixed, "seq", seq, 2)
            mixed_near = swap(mixed, "seq", seq, 1)
            line_one, line_two = stack(
                early_blocks, ((0, 3 * feat), (3 * feat, 8 * feat + 128)), mixed_near
            )
            plane_one = spread(line_one, "fsdp", fsdp, 2, 2)
            near_one = join(plane_one, mixed_far)
            far_one = swap(near_one, "fsdp", fsdp, 1)
            mixed_far = hold(mixed_far, near_one, space=pltpu.VMEM)
            mixed_blocks = [mixed, mixed_near, mixed_far, swap(mixed_far, "seq", seq, 1)]
            plane_two = spread(line_two, "fsdp", fsdp, 2, 2)
            encoder_late = hold(encoder, far_one)
            encoder_far = swap(encoder_late, "seq", seq, 2)
            encoder_near = swap(encoder_late, "seq", seq, 1)
        else:
            home = jnp.zeros_like(pos)
            near_one, far_one = whole_parts(early[:, : 3 * feat], fsdp, seq)
            near_two, far_two = whole_parts(early[:, 3 * feat :], fsdp, seq)
            all_three = regroup(all_three, chunk, near_one.shape[2], wide)
            mixed_blocks = over_line(mixed, seq, spread)
            encoder_blocks = over_line(encoder, seq, spread)

        q_one, v_one, kt_one, mixed_one, inverse_one, key_rows, exps_one = self_attend(
            home, mixed_blocks, ids, [near_one], [far_one], count, feat, ()
        )
        if near_rows:
            encoder_far = hold(encoder_far, mixed_one, space=pltpu.VMEM)
            got_two = [hold(part, encoder_far, space=pltpu.VMEM) for part in plane_two[1:]]
            encoder_near = hold(encoder_near, mixed_one, space=pltpu.VMEM)
            near_two = join([line_two, *got_two], encoder_near)
            far_two = swap(near_two, "fsdp", fsdp, 1)
            near_two, far_two = [near_two], [far_two]
            encoder_blocks = [encoder, encoder_near, encoder_far]
            encoder_blocks.append(swap(encoder_far, "seq", seq, 1))
        else:
            near_two, far_two = [near_two], [far_two]
        (
            vec,
            unit_one,
            inv_one,
            q_two,
            v_two,
            kt_two,
            mixed_two,
            inverse_two,
            unit_two,
            inv_two,
            exps_two,
        ) = cross_attend(
            home,
            encoder_blocks,
            ids,
            key_rows,
            mixed,
            mixed_one,
            near_two,
            far_two,
            (),
        )
        layer_out, flow_two, vec_grad, keep_three, away_three = feed(
            home,
            unit_two,
            inv_two,
            vec,
            out_grad.reshape(count, feat),
            pad,
            all_three,
            near_one.shape[:3] + (2 * wide,),
        )
        after_feed = ()
        if near_rows:
            away_three = swap(away_three, "fsdp", fsdp, 1)
            far_three = far_step(keep_three, away_three, (), fsdp)
            after_feed = (far_three[0],)
        flow_one, one_t, keep_two, away_two, encoder_parts = cross_back(
            home,
            pos[1:],
            encoder_blocks,
            near_two,
            far_two,
            after_feed,
            flow_two,
            mixed_two,
            inverse_two,
            q_two,
            kt_two,
            v_two,
            exps_two,
            unit_one,
            inv_one,
            vec,
            vec_grad,
            mixed_one,
            inverse_one,
        )
        if near_rows:
            mid_three = mid_step(far_three, (flow_one,), fsdp)
            away_two = swap(hold(away_two, mid_three[0], space=pltpu.VMEM), "fsdp", fsdp, 1)
        encoder_grad = lax.psum_scatter(
            encoder_parts, "seq", scatter_dimension=0, tiled=True
        ).astype(F32)
        after_back, after_grads = (), ()
        if near_rows:
            far_two = far_step(keep_two, away_two, (), fsdp)
            after_back = (far_two[0],)
        input_own, query_t, kv, input_parts = self_back(
            home,
            pos[1:],
            seq,
            [near_one],
            [far_one],
            after_back,
            flow_one,
            one_t,
            mixed_one,
            q_one,
            kt_one,
            v_one,
            exps_one,
        )
        if near_rows:
            near_three = near_step(mid_three, (query_t,))
            mid_two = mid_step(far_two, (query_t,), fsdp)
            after_grads = (near_three[0], mid_two[0])
        keep_one, away_one = self_grads(
            home, mixed_blocks, query_t, kv, near_one.shape, after_grads
        )
        if near_rows:
            got_two = [hold(got, keep_one, space=pltpu.VMEM) for got in mid_two[1:3]]
            mid_two = (mid_two[0], *got_two, *mid_two[3:])
            away_one = swap(hold(away_one, *got_two, space=pltpu.VMEM), "fsdp", fsdp, 1)
            one_send = add_call(
                add_one_body,
                [shape(*keep_one.shape[1:])] * 4,
                (keep_one, away_one),
                (),
                "add_one",
            )
            near_two = near_step(mid_two, (one_send[0],))
            near_three = finish_line(near_three, seq, one_send[0])
            got_one = [swap(one_send[e], "fsdp", fsdp, 2 * e) for e in (1, 2, 3)]
            line_one = add_call(
                add_line_body,
                [shape(*keep_one.shape[2:])] * 4,
                (one_send[0], *got_one),
                (),
                "add_line",
            )
            got_line = [swap(line_one[d], "seq", seq, d) for d in (1, 2, 3)]
            grads_three = near_three[0] + hold(near_three[1], got_line[0]).astype(F32)
            near_two = finish_line(near_two, seq, line_one[0])
            grads_two = near_two[0] + near_two[1].astype(F32)
            grads_one = line_one[0].astype(F32)
            for block in got_line:
                grads_one = grads_one + block.astype(F32)
        else:
            grads_one = whole_sum(keep_one, away_one, fsdp, seq)
            grads_two = whole_sum(keep_two, away_two, fsdp, seq)
            grads_three = jnp.stack([keep_three, away_three], axis=1).reshape(feat, 2 * wide)
            grads_three = regroup(grads_three, near_one.shape[2], chunk, wide)
            grads_three = scatter_blocks(grads_three[None], fsdp, seq, False)[0]
        input_got = lax.psum_scatter(input_parts, "seq", scatter_dimension=0, tiled=True)
        input_grad = input_own + input_got.astype(F32)

        def stacked(flat_rows):
            return flat_rows.reshape(row_count, loc_count, feat)

        def cols(grads, place):
            return grads[:, place * feat : (place + 1) * feat]

        vec_out = grads_two[:, 5 * feat : 5 * feat + 6].T
        grad_outer = jnp.concatenate(
            [grads_three[:, wide + r * feat : wide + (r + 1) * feat] for r in range(sub)], axis=0
        )
        return (
            stacked(layer_out),
            stacked(input_grad),
            stacked(encoder_grad),
            cols(grads_one, 0),
            cols(grads_one, 1),
            cols(grads_one, 2),
            cols(grads_two, 0),
            vec_out[0],
            vec_out[1],
            cols(grads_two, 1),
            cols(grads_two, 2),
            cols(grads_two, 3),
            cols(grads_two, 4),
            vec_out[2],
            vec_out[3],
            grads_three[:, :wide],
            grad_outer,
            vec_out[4],
            vec_out[5],
        )

    return on_device


def solution(mesh):
    rows = P("fsdp", "seq", None)
    marks = P("fsdp", "seq")
    weight = P(("fsdp", "seq"), None)
    vector = P(("fsdp", "seq"))
    layer = (weight,) * 4 + (vector,) * 2
    return jax.shard_map(
        make(mesh.shape["fsdp"], mesh.shape["seq"]),
        mesh=mesh,
        in_specs=(rows, rows, marks, marks, marks, rows, rows)
        + layer
        + layer
        + (weight,) * 2
        + (vector,) * 2,
        out_specs=(rows,) * 3 + layer + layer + (weight,) * 2 + (vector,) * 2,
        check_vma=False,
    )
```

profile of v0, /device:TPU:0, one launch (start us, length us, event | category | flops | bytes accessed | tf_op | source)
XLA Modules:
  0.0 210.5 jit_solution(598495095717537279)
XLA Ops:
  7.2 0.8 stack.40
  8.6 2.2 %pack.1 = (bf16[16,4096]{1,0:T(8,128)(2,1)}, bf16[16,4224]{1,0:T(8,128)(2,1)}, bf16[272,512]{1,0:T(8,128)(2,1)}, bf16[256,512]{1,0:T(8,128)(2,1)}) custom-call(bf16[1,256,512]{2,1,0:T(8,128)(2,1)} %source.1, bf16[1,256,512]{2,1,0:T(8,128)(2,1)} %target.1, s32[1,256]{1,0:T(1,128)} %glance.1, s32[1,256]{1,0:T(1,128)} %refs_6_.5, s32[1,256]{1,0:T(1,128)} %pad.20, ...), custom_call_target="tpu_custom_call" | custom-call | flops 1000000000 | bytes 2000000 | tf_op jit(solution)/shard_map/pack/pallas_call | solution.py:298
  10.9 3.1 %collective-permute-start.3 = (bf16[272,512]{1,0:T(8,128)(2,1)}, bf16[272,512]{1,0:T(8,128)(2,1)S(1)}, u32[]{:S(2)}, u32[]{:S(2)}) collective-permute-start(bf16[272,512]{1,0:T(8,128)(2,1)} %get-tuple-element.91.refs_0_.refs_8_.refs_1_), channel_id=1, source_target_pairs={{0,1},{1,0},{2,3},{3,2},{4,5},{5,4},{6,7},{7,6},{8,9},{9,8},{10,11... | collective-permute-start | bytes 835592 | tf_op jit(solution)/shard_map/ppermute | solution.py:700
  14.0 2.5 %collective-permute-start.2 = (bf16[16,4224]{1,0:T(8,128)(2,1)}, bf16[16,4224]{1,0:T(8,128)(2,1)S(1)}, u32[]{:S(2)}, u32[]{:S(2)}) collective-permute-start(bf16[16,4224]{1,0:T(8,128)(2,1)} %get-tuple-element.90.refs_0_), channel_id=1, source_target_pairs={{0,3},{1,2},{2,1},{3,0},{4,7},{5,6},{6,5},{7,4},{8,11},{9,10},{10,... | collective-permute-start | bytes 405512 | tf_op jit(solution)/shard_map/ppermute | solution.py:700
  16.6 1.8 collective-permute-start
  18.4 1.7 collective-permute-start.7
  20.1 7.1 %collective-permute-done.2.refs_3_ = bf16[16,4224]{1,0:T(8,128)(2,1)S(1)} collective-permute-done((bf16[16,4224]{1,0:T(8,128)(2,1)}, bf16[16,4224]{1,0:T(8,128)(2,1)S(1)}, u32[]{:S(2)}, u32[]{:S(2)}) %collective-permute-start.2) | collective-permute-done | bytes 135200 | tf_op jit(solution)/shard_map/ppermute | solution.py:700
  27.2 4.0 %collective-permute-done.1.refs_2_ = bf16[16,4224]{1,0:T(8,128)(2,1)S(1)} collective-permute-done((bf16[16,4224]{1,0:T(8,128)(2,1)}, bf16[16,4224]{1,0:T(8,128)(2,1)S(1)}, u32[]{:S(2)}, u32[]{:S(2)}) %collective-permute-start.1) | collective-permute-done | bytes 135200 | tf_op jit(solution)/shard_map/ppermute | solution.py:700
  31.2 2.9 %collective-permute-done.refs_1_ = bf16[16,4224]{1,0:T(8,128)(2,1)S(1)} collective-permute-done((bf16[16,4224]{1,0:T(8,128)(2,1)}, bf16[16,4224]{1,0:T(8,128)(2,1)S(1)}, u32[]{:S(2)}, u32[]{:S(2)}) %collective-permute-start) | collective-permute-done | bytes 135200 | tf_op jit(solution)/shard_map/ppermute | solution.py:700
  34.2 0.9 copy-done.18
  35.1 0.7 copy-done.17
  35.8 2.9 %collective-permute-start.6 = (bf16[4,16,1536]{2,1,0:T(8,128)(2,1)S(1)}, bf16[4,16,1536]{2,1,0:T(8,128)(2,1)S(1)}, u32[]{:S(2)}, u32[]{:S(2)}) collective-permute-start(bf16[4,16,1536]{2,1,0:T(8,128)(2,1)S(1)} %get-tuple-element.92.refs_0_), channel_id=1, source_target_pairs={{0,24},{4,28},{8,16},{12,20},{16,8},{20,12},{24,0},{28,4},{1,25},{... | collective-permute-start | bytes 589832 | tf_op jit(solution)/shard_map/ppermute | solution.py:700
  39.4 4.1 %collective-permute-done.7.refs_4_.refs_0_ = bf16[272,512]{1,0:T(8,128)(2,1)S(1)} collective-permute-done((bf16[272,512]{1,0:T(8,128)(2,1)}, bf16[272,512]{1,0:T(8,128)(2,1)S(1)}, u32[]{:S(2)}, u32[]{:S(2)}) %collective-permute-start.7) | collective-permute-done | bytes 278560 | tf_op jit(solution)/shard_map/ppermute | solution.py:700
  43.5 1.2 collective-permute-done.5.refs_2_
  45.3 0.8 copy-done.4
  46.3 0.7 copy.56.refs_0_
  47.1 1.4 collective-permute-start.15
  48.5 1.3 collective-permute-start.14
  49.8 0.7 collective-permute-start.13
  50.5 0.9 copy-done.32
  51.5 4.5 %collective-permute-start.11 = (bf16[256,512]{1,0:T(8,128)(2,1)}, bf16[256,512]{1,0:T(8,128)(2,1)S(1)}, u32[]{:S(2)}, u32[]{:S(2)}) collective-permute-start(bf16[256,512]{1,0:T(8,128)(2,1)} %hold.14), channel_id=1, source_target_pairs={{0,2},{1,3},{2,0},{3,1},{4,6},{5,7},{6,4},{7,5},{8,10},{9,11},{10,... | collective-permute-start | bytes 786440 | tf_op jit(solution)/shard_map/ppermute | solution.py:700
  56.0 7.5 %collective-permute-done.10.refs_3_.refs_4_ = bf16[272,512]{1,0:T(8,128)(2,1)} collective-permute-done((bf16[272,512]{1,0:T(8,128)(2,1)S(1)}, bf16[272,512]{1,0:T(8,128)(2,1)}, u32[]{:S(2)}, u32[]{:S(2)}) %collective-permute-start.10) | collective-permute-done | bytes 278560 | tf_op jit(solution)/shard_map/ppermute | solution.py:700
  63.5 8.8 %self_attend.1 = (bf16[256,512]{1,0:T(8,128)(2,1)}, bf16[1024,512]{1,0:T(8,128)(2,1)}, bf16[512,1024]{1,0:T(8,128)(2,1)}, bf16[512,256]{1,0:T(8,128)(2,1)}, f32[...) custom-call(s32[2]{0:T(128)S(1)} %pad_add_fusion.pos.refs_0_, ...), custom_call_target="tpu_custom_call" | custom-call | flops 12000000000 | bytes 20000000 | tf_op jit(solution)/shard_map/self_attend/pallas_call | solution.py:298
  72.4 4.8 %collective-permute-done.9.refs_0_ = bf16[256,512]{1,0:T(8,128)(2,1)S(1)} collective-permute-done((bf16[256,512]{1,0:T(8,128)(2,1)}, bf16[256,512]{1,0:T(8,128)(2,1)S(1)}, u32[]{:S(2)}, u32[]{:S(2)}) %collective-permute-start.9) | collective-permute-done | bytes 262176 | tf_op jit(solution)/shard_map/ppermute | solution.py:700
  78.3 13.3 %collective-permute-done.12.refs_3_.refs_5_ = bf16[256,512]{1,0:T(8,128)(2,1)S(1)} collective-permute-done((bf16[256,512]{1,0:T(8,128)(2,1)S(1)}, bf16[256,512]{1,0:T(8,128)(2,1)S(1)}, u32[]{:S(2)}, u32[]{:S(2)}) %collective-permute-start.12) | collective-permute-done | bytes 262176 | tf_op jit(solution)/shard_map/ppermute | solution.py:700
  91.6 0.7 copy-done.38
  92.8 10.1 %cross_attend.1 = (f32[8,512]{1,0:T(8,128)}, f32[256,512]{1,0:T(8,128)}, f32[256,128]{1,0:T(8,128)}, bf16[256,512]{1,0:T(8,128)(2,1)}, bf16[1024,512]{1,0:T(8,12...) custom-call(s32[2]{0:T(128)S(1)} %pad_add_fusion.pos.refs_0_, ...), custom_call_target="tpu_custom_call" | custom-call | flops 14000000000 | bytes 20000000 | tf_op jit(solution)/shard_map/cross_attend/pallas_call | solution.py:298
  102.9 8.0 %feed.1 = (bf16[256,512]{1,0:T(8,128)(2,1)}, f32[256,512]{1,0:T(8,128)S(1)}, f32[8,512]{1,0:T(8,128)S(1)}, bf16[4,4,16,4096]{3,2,1,0:T(8,128)(2,1)S(1)}, bf16[4,4,16,4096]{3,2,1,0:T(8,128)(2,1)S(1)}) custom-call(s32[2]{0:T(128)S(1)} %pad_add_fusion.pos.refs_0_, f32[256,512]{1,0:T(8,128)S(1)} %get-tuple-element.96.unit_in, ...), custom_call_target="tpu_custom_call" | custom-call | flops 6000000000 | bytes 20000000 | tf_op jit(solution)/shard_map/feed/pallas_call | solution.py:298
  110.9 4.2 %collective-permute-done.17.away = bf16[4,4,16,4096]{3,2,1,0:T(8,128)(2,1)S(1)} collective-permute-done((bf16[4,4,16,4096]{3,2,1,0:T(8,128)(2,1)S(1)}, bf16[4,4,16,4096]{3,2,1,0:T(8,128)(2,1)S(1)}, u32[]{:S(2)}, u32[]{:S(2)}) %collective-permute-start.17) | collective-permute-done | bytes 2097184 | tf_op jit(solution)/shard_map/ppermute | solution.py:700
  115.5 1.5 collective-permute-start.19
  117.1 13.2 %cross_back.1 = (f32[256,512]{1,0:T(8,128)S(1)}, bf16[512,256]{1,0:T(8,128)(2,1)S(1)}, bf16[4,4,16,2688]{3,2,1,0:T(8,128)(2,1)S(1)}, bf16[4,4,16,2688]{3,2,1,0:T(8,128)(2,1)S(1)}, bf16[1024,512]{1,0:T(8,128)(2,1)}) custom-call(s32[2]{0:T(128)S(1)} %pad_add_fusion.pos.refs_0_, s32[1]{0:T(128)} %bitcast.1.refs_1_, ...), custom_call_target="tpu_custom_call" | custom-call | flops 15000000512 | bytes 20000000 | tf_op jit(solution)/shard_map/cross_back/pallas_call | solution.py:298
  131.0 0.7 copy-done.10
  131.7 0.8 copy-done.23
  132.5 0.8 copy-done.25
  133.4 0.8 copy-done.11
  134.2 1.7 collective-permute-start.21
  136.6 1.5 copy-done.20
  138.4 1.8 collective-permute-start.23
  140.6 10.6 %self_back.1 = (f32[256,512]{1,0:T(8,128)}, bf16[512,256]{1,0:T(8,128)(2,1)S(1)}, bf16[1024,1024]{1,0:T(8,128)(2,1)S(1)}, bf16[1024,512]{1,0:T(8,128)(2,1)}) custom-call(s32[2]{0:T(128)S(1)} %pad_add_fusion.pos.refs_0_, s32[1]{0:T(128)} %bitcast.1.refs_1_, f32[256,512]{1,0:T(8,128)S(1)} %copy-done.22, bf16[512,256]{1,0:T(8,128)(2,1)S(1)} %get-tuple-element.116.refs_3_, ...), custom_call_target="tpu_custom_call" | custom-call | flops 12000000000 | bytes 20000000 | tf_op jit(solution)/shard_map/self_back/pallas_call | solution.py:298
  151.5 0.7 copy-done.27
  152.2 0.7 copy-done.29
  153.0 1.6 collective-permute-start.25
  154.9 2.8 %self_grads.1 = (bf16[4,4,16,1536]{3,2,1,0:T(8,128)(2,1)S(1)}, bf16[4,4,16,1536]{3,2,1,0:T(8,128)(2,1)S(1)}) custom-call(s32[2]{0:T(128)S(1)} %pad_add_fusion.pos.refs_0_, bf16[272,512]{1,0:T(8,128)(2,1)} %get-tuple-element.91.refs_0_.refs_8_.refs_1_, bf16[272,512]{1,0:T(8,128)(2,1)} %copy-done.17, bf16[272,512]{1,0:T(8,128)(2,1)} %copy-done.9, ...), custom_call_target="tpu_custom_call" | custom-call | flops 5000000000 | bytes 8000000 | tf_op jit(solution)/shard_map/self_grads/pallas_call | solution.py:298
  157.7 0.9 copy-done.2
  158.7 1.7 collective-permute-done.26.refs_0_
  160.3 0.7 copy-done.5
  161.2 1.9 bitcast_convert_fusion
  163.4 1.4 add_one.1
  165.0 1.7 collective-permute-start.34
  167.1 1.6 collective-permute-start.29
  168.6 1.6 collective-permute-start.30
  170.2 3.5 %collective-permute-done.36.refs_0_ = bf16[2,16,4096]{2,1,0:T(8,128)(2,1)S(1)} collective-permute-done((bf16[2,16,4096]{2,1,0:T(8,128)(2,1)S(1)}, bf16[2,16,4096]{2,1,0:T(8,128)(2,1)S(1)}, u32[]{:S(2)}, u32[]{:S(2)}) %collective-permute-start.36) | collective-permute-done | bytes 262176 | tf_op jit(solution)/shard_map/ppermute | solution.py:700
  173.8 0.7 collective-permute-done.28.first
  174.5 3.2 %collective-permute-done.29.second = bf16[4,16,1536]{2,1,0:T(8,128)(2,1)S(1)} collective-permute-done((bf16[4,16,1536]{2,1,0:T(8,128)(2,1)S(1)}, bf16[4,16,1536]{2,1,0:T(8,128)(2,1)S(1)}, u32[]{:S(2)}, u32[]{:S(2)}) %collective-permute-start.29) | collective-permute-done | bytes 196640 | tf_op jit(solution)/shard_map/ppermute | solution.py:700
  177.7 0.9 copy-done.15
  179.7 1.9 collective-permute-start.32
  181.6 2.1 collective-permute-start.33
  183.7 3.9 %collective-permute-done.34.refs_0_ = bf16[2,16,2688]{2,1,0:T(8,128)(2,1)S(1)} collective-permute-done((bf16[2,16,2688]{2,1,0:T(8,128)(2,1)S(1)}, bf16[2,16,2688]{2,1,0:T(8,128)(2,1)S(1)}, u32[]{:S(2)}, u32[]{:S(2)}) %collective-permute-start.34) | collective-permute-done | bytes 172064 | tf_op jit(solution)/shard_map/ppermute | solution.py:700
  187.7 5.8 %collective-permute-done.37.refs_0_ = bf16[16,4096]{1,0:T(8,128)(2,1)S(1)} collective-permute-done((bf16[16,4096]{1,0:T(8,128)(2,1)S(1)}, bf16[16,4096]{1,0:T(8,128)(2,1)S(1)}, u32[]{:S(2)}, u32[]{:S(2)}) %collective-permute-start.37) | collective-permute-done | bytes 131104 | tf_op jit(solution)/shard_map/ppermute | solution.py:700
  194.8 1.0 fusion.1
  197.1 0.9 convert_add_fusion.4
  199.2 1.4 collective-permute-done.35
  200.7 0.8 slice_reduce_fusion
  202.1 1.8 add_bitcast_fusion
  (149 shorter events, 14.0 us)
Async XLA Ops:
  7.2 95.7 %all-gather.2.cloned.1.call-start = ((), (), s32[]{:S(2)}) async-start(), calls=%async_computation.2 | async-start | bytes 4325376 | tf_op jit(solution)/shard_map/all_gather | solution.py:966
  10.8 150.3 %reduce-scatter.5.cloned.1.call-start = ((), (), s32[]{:S(2)}) async-start(), calls=%async_computation.4 | async-start | bytes 1310720 | tf_op jit(solution)/shard_map/reduce_scatter | solution.py:1069
  10.9 23.3 %collective-permute-start.3 = (bf16[272,512]{1,0:T(8,128)(2,1)}, bf16[272,512]{1,0:T(8,128)(2,1)S(1)}, u32[]{:S(2)}, u32[]{:S(2)}) collective-permute-start(bf16[272,512]{1,0:T(8,128)(2,1)} %get-tuple-element.91.refs_0_.refs_8_.refs_1_), channel_id=1, source_target_pairs={{0,1},{1,0},{2,3},{3,2},{4,5},{5,4},{6,7},{7,6},{8,9},{9,8},{10,11... | collective-permute-start | bytes 835592 | tf_op jit(solution)/shard_map/ppermute | solution.py:700
  14.0 13.2 %collective-permute-start.2 = (bf16[16,4224]{1,0:T(8,128)(2,1)}, bf16[16,4224]{1,0:T(8,128)(2,1)S(1)}, u32[]{:S(2)}, u32[]{:S(2)}) collective-permute-start(bf16[16,4224]{1,0:T(8,128)(2,1)} %get-tuple-element.90.refs_0_), channel_id=1, source_target_pairs={{0,3},{1,2},{2,1},{3,0},{4,7},{5,6},{6,5},{7,4},{8,11},{9,10},{10,... | collective-permute-start | bytes 405512 | tf_op jit(solution)/shard_map/ppermute | solution.py:700
  16.5 14.8 %collective-permute-start.1 = (bf16[16,4224]{1,0:T(8,128)(2,1)}, bf16[16,4224]{1,0:T(8,128)(2,1)S(1)}, u32[]{:S(2)}, u32[]{:S(2)}) collective-permute-start(bf16[16,4224]{1,0:T(8,128)(2,1)} %get-tuple-element.90.refs_0_), channel_id=1, source_target_pairs={{0,2},{1,3},{2,0},{3,1},{4,6},{5,7},{6,4},{7,5},{8,10},{9,11},{10,... | collective-permute-start | bytes 405512 | tf_op jit(solution)/shard_map/ppermute | solution.py:700
  16.6 17.6 %collective-permute-start = (bf16[16,4224]{1,0:T(8,128)(2,1)}, bf16[16,4224]{1,0:T(8,128)(2,1)S(1)}, u32[]{:S(2)}, u32[]{:S(2)}) collective-permute-start(bf16[16,4224]{1,0:T(8,128)(2,1)} %get-tuple-element.90.refs_0_), channel_id=1, source_target_pairs={{0,1},{1,0},{2,3},{3,2},{4,5},{5,4},{6,7},{7,6},{8,9},{9,8},{10,11... | collective-permute-start | bytes 405512 | tf_op jit(solution)/shard_map/ppermute | solution.py:700
  18.4 25.2 %collective-permute-start.7 = (bf16[272,512]{1,0:T(8,128)(2,1)}, bf16[272,512]{1,0:T(8,128)(2,1)S(1)}, u32[]{:S(2)}, u32[]{:S(2)}) collective-permute-start(bf16[272,512]{1,0:T(8,128)(2,1)} %get-tuple-element.91.refs_0_.refs_8_.refs_1_), channel_id=1, source_target_pairs={{0,2},{1,3},{2,0},{3,1},{4,6},{5,7},{6,4},{7,5},{8,10},{9,11},{10,... | collective-permute-start | bytes 835592 | tf_op jit(solution)/shard_map/ppermute | solution.py:700
  35.8 10.5 %copy-start.35 = (bf16[256,512]{1,0:T(8,128)(2,1)S(1)}, bf16[256,512]{1,0:T(8,128)(2,1)}, u32[]{:S(2)}) copy-start(bf16[256,512]{1,0:T(8,128)(2,1)} %get-tuple-element.89.refs_0_.refs_2_) | copy-start | bytes 786436
  35.8 7.7 %collective-permute-start.6 = (bf16[4,16,1536]{2,1,0:T(8,128)(2,1)S(1)}, bf16[4,16,1536]{2,1,0:T(8,128)(2,1)S(1)}, u32[]{:S(2)}, u32[]{:S(2)}) collective-permute-start(bf16[4,16,1536]{2,1,0:T(8,128)(2,1)S(1)} %get-tuple-element.92.refs_0_), channel_id=1, source_target_pairs={{0,24},{4,28},{8,16},{12,20},{16,8},{20,12},{24,0},{28,4},{1,25},{... | collective-permute-start | bytes 589832 | tf_op jit(solution)/shard_map/ppermute | solution.py:700
  38.7 6.1 %collective-permute-start.5 = (bf16[4,16,1536]{2,1,0:T(8,128)(2,1)S(1)}, bf16[4,16,1536]{2,1,0:T(8,128)(2,1)S(1)}, u32[]{:S(2)}, u32[]{:S(2)}) collective-permute-start(bf16[4,16,1536]{2,1,0:T(8,128)(2,1)S(1)} %get-tuple-element.92.refs_0_), channel_id=1, source_target_pairs={{0,16},{4,20},{8,24},{12,28},{16,0},{20,4},{24,8},{28,12},{1,17},{... | collective-permute-start | bytes 589832 | tf_op jit(solution)/shard_map/ppermute | solution.py:700
  39.2 6.0 %collective-permute-start.4 = (bf16[4,16,1536]{2,1,0:T(8,128)(2,1)S(1)}, bf16[4,16,1536]{2,1,0:T(8,128)(2,1)S(1)}, u32[]{:S(2)}, u32[]{:S(2)}) collective-permute-start(bf16[4,16,1536]{2,1,0:T(8,128)(2,1)S(1)} %get-tuple-element.92.refs_0_), channel_id=1, source_target_pairs={{0,8},{4,12},{8,0},{12,4},{16,24},{20,28},{24,16},{28,20},{1,9},{5... | collective-permute-start | bytes 589832 | tf_op jit(solution)/shard_map/ppermute | solution.py:700
  45.2 5.3 %collective-permute-start.8 = (bf16[4,4,16,1536]{3,2,1,0:T(8,128)(2,1)S(1)}, bf16[4,4,16,1536]{3,2,1,0:T(8,128)(2,1)S(1)}, u32[]{:S(2)}, u32[]{:S(2)}) collective-permute-start(bf16[4,4,16,1536]{3,2,1,0:T(8,128)(2,1)S(1)} %join.2.refs_1_.refs_4_.refs_9_), channel_id=1, source_target_pairs={{0,4},{4,0},{8,12},{12,8},{16,20},{20,16},{24,28},{28,24},{1,5},{5... | collective-permute-start | bytes 2359304 | tf_op jit(solution)/shard_map/ppermute | solution.py:700
  46.1 17.4 %copy-start.9 = (bf16[272,512]{1,0:T(8,128)(2,1)}, bf16[272,512]{1,0:T(8,128)(2,1)S(1)}, u32[]{:S(2)}) copy-start(bf16[272,512]{1,0:T(8,128)(2,1)S(1)} %hold.15.refs_2_.refs_3_) | copy-start | bytes 835588
  46.1 17.4 %collective-permute-start.10 = (bf16[272,512]{1,0:T(8,128)(2,1)S(1)}, bf16[272,512]{1,0:T(8,128)(2,1)}, u32[]{:S(2)}, u32[]{:S(2)}) collective-permute-start(bf16[272,512]{1,0:T(8,128)(2,1)S(1)} %hold.15.refs_2_.refs_3_), channel_id=1, source_target_pairs={{0,1},{1,0},{2,3},{3,2},{4,5},{5,4},{6,7},{7,6},{8,9},{9,8},{10,11... | collective-permute-start | bytes 835592 | tf_op jit(solution)/shard_map/ppermute | solution.py:700
  47.1 30.2 %collective-permute-start.15 = (bf16[4,16,2688]{2,1,0:T(8,128)(2,1)S(1)}, bf16[4,16,2688]{2,1,0:T(8,128)(2,1)S(1)}, u32[]{:S(2)}, u32[]{:S(2)}) collective-permute-start(bf16[4,16,2688]{2,1,0:T(8,128)(2,1)S(1)} %get-tuple-element.94.refs_0_), channel_id=1, source_target_pairs={{0,24},{4,28},{8,16},{12,20},{16,8},{20,12},{24,0},{28,4},{1,25},{... | collective-permute-start | bytes 1032200 | tf_op jit(solution)/shard_map/ppermute | solution.py:700
  48.5 28.7 %collective-permute-start.14 = (bf16[4,16,2688]{2,1,0:T(8,128)(2,1)S(1)}, bf16[4,16,2688]{2,1,0:T(8,128)(2,1)S(1)}, u32[]{:S(2)}, u32[]{:S(2)}) collective-permute-start(bf16[4,16,2688]{2,1,0:T(8,128)(2,1)S(1)} %get-tuple-element.94.refs_0_), channel_id=1, source_target_pairs={{0,16},{4,20},{8,24},{12,28},{16,0},{20,4},{24,8},{28,12},{1,17},{... | collective-permute-start | bytes 1032200 | tf_op jit(solution)/shard_map/ppermute | solution.py:700
  49.8 27.5 %collective-permute-start.13 = (bf16[4,16,2688]{2,1,0:T(8,128)(2,1)S(1)}, bf16[4,16,2688]{2,1,0:T(8,128)(2,1)S(1)}, u32[]{:S(2)}, u32[]{:S(2)}) collective-permute-start(bf16[4,16,2688]{2,1,0:T(8,128)(2,1)S(1)} %get-tuple-element.94.refs_0_), channel_id=1, source_target_pairs={{0,8},{4,12},{8,0},{12,4},{16,24},{20,28},{24,16},{28,20},{1,9},{5... | collective-permute-start | bytes 1032200 | tf_op jit(solution)/shard_map/ppermute | solution.py:700
  51.5 20.9 %collective-permute-start.11 = (bf16[256,512]{1,0:T(8,128)(2,1)}, bf16[256,512]{1,0:T(8,128)(2,1)S(1)}, u32[]{:S(2)}, u32[]{:S(2)}) collective-permute-start(bf16[256,512]{1,0:T(8,128)(2,1)} %hold.14), channel_id=1, source_target_pairs={{0,2},{1,3},{2,0},{3,1},{4,6},{5,7},{6,4},{7,5},{8,10},{9,11},{10,... | collective-permute-start | bytes 786440 | tf_op jit(solution)/shard_map/ppermute | solution.py:700
  63.5 13.7 %collective-permute-start.9 = (bf16[256,512]{1,0:T(8,128)(2,1)}, bf16[256,512]{1,0:T(8,128)(2,1)S(1)}, u32[]{:S(2)}, u32[]{:S(2)}) collective-permute-start(bf16[256,512]{1,0:T(8,128)(2,1)} %hold.14), channel_id=1, source_target_pairs={{0,1},{1,0},{2,3},{3,2},{4,5},{5,4},{6,7},{7,6},{8,9},{9,8},{10,11... | collective-permute-start | bytes 786440 | tf_op jit(solution)/shard_map/ppermute | solution.py:700
  72.4 4.9 %copy-start = (bf16[256,512]{1,0:T(8,128)(2,1)}, bf16[256,512]{1,0:T(8,128)(2,1)S(1)}, u32[]{:S(2)}) copy-start(bf16[256,512]{1,0:T(8,128)(2,1)S(1)} %hold.17.refs_1_.refs_2_.refs_4_) | copy-start | bytes 786436
  77.3 1.0 copy-start.1
  77.9 13.6 %copy-start.16 = (bf16[4,4,16,2688]{3,2,1,0:T(8,128)(2,1)}, bf16[4,4,16,2688]{3,2,1,0:T(8,128)(2,1)S(1)}, u32[]{:S(2)}) copy-start(bf16[4,4,16,2688]{3,2,1,0:T(8,128)(2,1)S(1)} %join.3.refs_4_.refs_6_) | copy-start | bytes 4128772
  77.9 13.6 %collective-permute-start.16 = (bf16[4,4,16,2688]{3,2,1,0:T(8,128)(2,1)S(1)}, bf16[4,4,16,2688]{3,2,1,0:T(8,128)(2,1)S(1)}, u32[]{:S(2)}, u32[]{:S(2)}) collective-permute-start(bf16[4,4,16,2688]{3,2,1,0:T(8,128)(2,1)S(1)} %join.3.refs_4_.refs_6_), channel_id=1, source_target_pairs={{0,4},{4,0},{8,12},{12,8},{16,20},{20,16},{24,28},{28,24},{1,5},{5... | collective-permute-start | bytes 4128776 | tf_op jit(solution)/shard_map/ppermute | solution.py:700
  78.3 13.3 %collective-permute-start.12 = (bf16[256,512]{1,0:T(8,128)(2,1)S(1)}, bf16[256,512]{1,0:T(8,128)(2,1)S(1)}, u32[]{:S(2)}, u32[]{:S(2)}) collective-permute-start(bf16[256,512]{1,0:T(8,128)(2,1)S(1)} %copy-done.1), channel_id=1, source_target_pairs={{0,1},{1,0},{2,3},{3,2},{4,5},{5,4},{6,7},{7,6},{8,9},{9,8},{10,11... | collective-permute-start | bytes 786440 | tf_op jit(solution)/shard_map/ppermute | solution.py:700
  91.6 1.2 copy-start.37
  110.9 4.6 %copy-start.31 = (f32[8,512]{1,0:T(8,128)}, f32[8,512]{1,0:T(8,128)S(1)}, u32[]{:S(2)}) copy-start(f32[8,512]{1,0:T(8,128)S(1)} %get-tuple-element.110.refs_18_) | copy-start | bytes 49156
  110.9 4.2 %collective-permute-start.17 = (bf16[4,4,16,4096]{3,2,1,0:T(8,128)(2,1)S(1)}, bf16[4,4,16,4096]{3,2,1,0:T(8,128)(2,1)S(1)}, u32[]{:S(2)}, u32[]{:S(2)}) collective-permute-start(bf16[4,4,16,4096]{3,2,1,0:T(8,128)(2,1)S(1)} %get-tuple-element.113), channel_id=1, source_target_pairs={{0,4},{4,0},{8,12},{12,8},{16,20},{20,16},{24,28},{28,24},{1,5},{5... | collective-permute-start | bytes 6291464 | tf_op jit(solution)/shard_map/ppermute | solution.py:700
  115.5 14.7 %collective-permute-start.19 = (bf16[2,4,16,2048]{3,2,1,0:T(8,128)(2,1)S(1)}, bf16[2,4,16,2048]{3,2,1,0:T(8,128)(2,1)S(1)}, u32[]{:S(2)}, u32[]{:S(2)}) collective-permute-start(bf16[2,4,16,2048]{3,2,1,0:T(8,128)(2,1)S(1)} %get-tuple-element.125), channel_id=1, source_target_pairs={{0,16},{4,20},{8,24},{12,28},{16,0},{20,4},{24,8},{28,12},{1,17},{... | collective-permute-start | bytes 1572872 | tf_op jit(solution)/shard_map/ppermute | solution.py:700
  117.1 13.7 %collective-permute-start.18 = (bf16[2,4,16,2048]{3,2,1,0:T(8,128)(2,1)S(1)}, bf16[2,4,16,2048]{3,2,1,0:T(8,128)(2,1)S(1)}, u32[]{:S(2)}, u32[]{:S(2)}) collective-permute-start(bf16[2,4,16,2048]{3,2,1,0:T(8,128)(2,1)S(1)} %get-tuple-element.114.refs_21_), channel_id=1, source_target_pairs={{0,8},{4,12},{8,0},{12,4},{16,24},{20,28},{24,16},{28,20},{1,9},{5... | collective-permute-start | bytes 1572872 | tf_op jit(solution)/shard_map/ppermute | solution.py:700
  130.3 3.0 %copy-start.19 = (bf16[4,4,16,2688]{3,2,1,0:T(8,128)(2,1)}, bf16[4,4,16,2688]{3,2,1,0:T(8,128)(2,1)S(1)}, u32[]{:S(2)}) copy-start(bf16[4,4,16,2688]{3,2,1,0:T(8,128)(2,1)S(1)} %get-tuple-element.121.keep) | copy-start | bytes 4128772
  130.3 3.0 %copy-start.21 = (f32[256,512]{1,0:T(8,128)}, f32[256,512]{1,0:T(8,128)S(1)}, u32[]{:S(2)}) copy-start(f32[256,512]{1,0:T(8,128)S(1)} %get-tuple-element.115.refs_4_.refs_2_) | copy-start | bytes 1572868
  133.3 1.0 copy-start.11
  133.3 3.3 %collective-permute-start.20 = (bf16[4,4,16,2688]{3,2,1,0:T(8,128)(2,1)S(1)}, bf16[4,4,16,2688]{3,2,1,0:T(8,128)(2,1)S(1)}, u32[]{:S(2)}, u32[]{:S(2)}) collective-permute-start(bf16[4,4,16,2688]{3,2,1,0:T(8,128)(2,1)S(1)} %hold.21), channel_id=1, source_target_pairs={{0,4},{4,0},{8,12},{12,8},{16,20},{20,16},{24,28},{28,24},{1,5},{5... | collective-permute-start | bytes 4128776 | tf_op jit(solution)/shard_map/ppermute | solution.py:700
  133.4 68.7 %reduce-scatter.3.cloned.1.call-start = ((), (), s32[]{:S(2)}) async-start(), calls=%async_computation.3 | async-start | bytes 1310720 | tf_op jit(solution)/shard_map/reduce_scatter | solution.py:1132
  134.2 17.0 %collective-permute-start.21 = (bf16[4,16,2048]{2,1,0:T(8,128)(2,1)S(1)}, bf16[4,16,2048]{2,1,0:T(8,128)(2,1)S(1)}, u32[]{:S(2)}, u32[]{:S(2)}) collective-permute-start(bf16[4,16,2048]{2,1,0:T(8,128)(2,1)S(1)} %copy-done.11), channel_id=1, source_target_pairs={{0,16},{4,20},{8,24},{12,28},{16,0},{20,4},{24,8},{28,12},{1,17},{... | collective-permute-start | bytes 786440 | tf_op jit(solution)/shard_map/ppermute | solution.py:700
  136.0 15.2 %collective-permute-start.22 = (bf16[4,16,2048]{2,1,0:T(8,128)(2,1)S(1)}, bf16[4,16,2048]{2,1,0:T(8,128)(2,1)S(1)}, u32[]{:S(2)}, u32[]{:S(2)}) collective-permute-start(bf16[4,16,2048]{2,1,0:T(8,128)(2,1)S(1)} %get-tuple-element.135), channel_id=1, source_target_pairs={{0,8},{4,12},{8,0},{12,4},{16,24},{20,28},{24,16},{28,20},{1,9},{5... | collective-permute-start | bytes 786440 | tf_op jit(solution)/shard_map/ppermute | solution.py:700
  136.6 1.5 copy-start.20
  138.1 2.5 %copy-start.22 = (f32[256,512]{1,0:T(8,128)S(1)}, f32[256,512]{1,0:T(8,128)}, u32[]{:S(2)}) copy-start(f32[256,512]{1,0:T(8,128)} %copy-done.21) | copy-start | bytes 1572868
  138.4 12.9 %collective-permute-start.23 = (bf16[2,4,16,1280]{3,2,1,0:T(8,128)(2,1)S(1)}, bf16[2,4,16,1280]{3,2,1,0:T(8,128)(2,1)S(1)}, u32[]{:S(2)}, u32[]{:S(2)}) collective-permute-start(bf16[2,4,16,1280]{3,2,1,0:T(8,128)(2,1)S(1)} %get-tuple-element.127.refs_11_), channel_id=1, source_target_pairs={{0,8},{4,12},{8,0},{12,4},{16,24},{20,28},{24,16},{28,20},{1,9},{5... | collective-permute-start | bytes 983048 | tf_op jit(solution)/shard_map/ppermute | solution.py:700
  140.2 11.1 %collective-permute-start.24 = (bf16[2,4,16,1408]{3,2,1,0:T(8,128)(2,1)S(1)}, bf16[2,4,16,1408]{3,2,1,0:T(8,128)(2,1)S(1)}, u32[]{:S(2)}, u32[]{:S(2)}) collective-permute-start(bf16[2,4,16,1408]{3,2,1,0:T(8,128)(2,1)S(1)} %get-tuple-element.139), channel_id=1, source_target_pairs={{0,16},{4,20},{8,24},{12,28},{16,0},{20,4},{24,8},{28,12},{1,17},{... | collective-permute-start | bytes 1081352 | tf_op jit(solution)/shard_map/ppermute | solution.py:700
  140.6 10.6 %copy-start.24 = (f32[4,16,2048]{2,1,0:T(8,128)S(1)}, f32[4,16,2048]{2,1,0:T(8,128)}, u32[]{:S(2)}) copy-start(f32[4,16,2048]{2,1,0:T(8,128)} %copy-done.23) | copy-start | bytes 1572868
  140.6 10.6 %copy-start.26 = (f32[4,16,2048]{2,1,0:T(8,128)S(1)}, f32[4,16,2048]{2,1,0:T(8,128)}, u32[]{:S(2)}) copy-start(f32[4,16,2048]{2,1,0:T(8,128)} %copy-done.25) | copy-start | bytes 1572868
  153.0 5.7 %collective-permute-start.25 = (bf16[4,16,1280]{2,1,0:T(8,128)(2,1)S(1)}, bf16[4,16,1280]{2,1,0:T(8,128)(2,1)S(1)}, u32[]{:S(2)}, u32[]{:S(2)}) collective-permute-start(bf16[4,16,1280]{2,1,0:T(8,128)(2,1)S(1)} %get-tuple-element.140.refs_8_), channel_id=1, source_target_pairs={{0,16},{4,20},{8,24},{12,28},{16,0},{20,4},{24,8},{28,12},{1,17},{... | collective-permute-start | bytes 491528 | tf_op jit(solution)/shard_map/ppermute | solution.py:700
  154.6 5.8 %collective-permute-start.26 = (bf16[4,16,1408]{2,1,0:T(8,128)(2,1)S(1)}, bf16[4,16,1408]{2,1,0:T(8,128)(2,1)S(1)}, u32[]{:S(2)}, u32[]{:S(2)}) collective-permute-start(bf16[4,16,1408]{2,1,0:T(8,128)(2,1)S(1)} %get-tuple-element.143), channel_id=1, source_target_pairs={{0,8},{4,12},{8,0},{12,4},{16,24},{20,28},{24,16},{28,20},{1,9},{5... | collective-permute-start | bytes 540680 | tf_op jit(solution)/shard_map/ppermute | solution.py:700
  158.7 2.4 %copy-start.7 = (bf16[4,16,1280]{2,1,0:T(8,128)(2,1)}, bf16[4,16,1280]{2,1,0:T(8,128)(2,1)S(1)}, u32[]{:S(2)}) copy-start(bf16[4,16,1280]{2,1,0:T(8,128)(2,1)S(1)} %hold.22.refs_1_) | copy-start | bytes 491524
  161.0 2.4 %copy-start.3 = (bf16[4,4,16,1536]{3,2,1,0:T(8,128)(2,1)S(1)}, bf16[4,4,16,1536]{3,2,1,0:T(8,128)(2,1)}, u32[]{:S(2)}) copy-start(bf16[4,4,16,1536]{3,2,1,0:T(8,128)(2,1)} %copy-done.2) | copy-start | bytes 2359300
  161.0 2.4 %collective-permute-start.27 = (bf16[4,4,16,1536]{3,2,1,0:T(8,128)(2,1)S(1)}, bf16[4,4,16,1536]{3,2,1,0:T(8,128)(2,1)}, u32[]{:S(2)}, u32[]{:S(2)}) collective-permute-start(bf16[4,4,16,1536]{3,2,1,0:T(8,128)(2,1)S(1)} %hold.24), channel_id=1, source_target_pairs={{0,4},{4,0},{8,12},{12,8},{16,20},{20,16},{24,28},{28,24},{1,5},{5... | collective-permute-start | bytes 2359304 | tf_op jit(solution)/shard_map/ppermute | solution.py:700
  161.0 12.6 %collective-permute-start.36 = (bf16[2,16,4096]{2,1,0:T(8,128)(2,1)S(1)}, bf16[2,16,4096]{2,1,0:T(8,128)(2,1)S(1)}, u32[]{:S(2)}, u32[]{:S(2)}) collective-permute-start(bf16[2,16,4096]{2,1,0:T(8,128)(2,1)S(1)} %get-tuple-element.157), channel_id=1, source_target_pairs={{0,1},{1,0},{2,3},{3,2},{4,5},{5,4},{6,7},{7,6},{8,9},{9,8},{10,11... | collective-permute-start | bytes 786440 | tf_op jit(solution)/shard_map/ppermute | solution.py:700
  161.1 3.7 %copy-start.6 = (bf16[4,16,1408]{2,1,0:T(8,128)(2,1)S(1)}, bf16[4,16,1408]{2,1,0:T(8,128)(2,1)}, u32[]{:S(2)}) copy-start(bf16[4,16,1408]{2,1,0:T(8,128)(2,1)} %copy-done.5) | copy-start | bytes 540676
  161.1 3.7 %copy-start.8 = (bf16[4,16,1280]{2,1,0:T(8,128)(2,1)S(1)}, bf16[4,16,1280]{2,1,0:T(8,128)(2,1)}, u32[]{:S(2)}) copy-start(bf16[4,16,1280]{2,1,0:T(8,128)(2,1)} %copy-done.7) | copy-start | bytes 491524
  161.2 3.7 %copy-start.28 = (f32[4,16,1408]{2,1,0:T(8,128)S(1)}, f32[4,16,1408]{2,1,0:T(8,128)}, u32[]{:S(2)}) copy-start(f32[4,16,1408]{2,1,0:T(8,128)} %copy-done.27) | copy-start | bytes 1081348
  161.2 3.7 %copy-start.30 = (f32[4,16,1280]{2,1,0:T(8,128)S(1)}, f32[4,16,1280]{2,1,0:T(8,128)}, u32[]{:S(2)}) copy-start(f32[4,16,1280]{2,1,0:T(8,128)} %copy-done.29) | copy-start | bytes 983044
  164.8 8.8 %copy-start.14 = (bf16[4,16,1536]{2,1,0:T(8,128)(2,1)}, bf16[4,16,1536]{2,1,0:T(8,128)(2,1)S(1)}, u32[]{:S(2)}) copy-start(bf16[4,16,1536]{2,1,0:T(8,128)(2,1)S(1)} %get-tuple-element.144.own.refs_4_.refs_1_) | copy-start | bytes 589828
  165.0 22.6 %collective-permute-start.34 = (bf16[2,16,2688]{2,1,0:T(8,128)(2,1)S(1)}, bf16[2,16,2688]{2,1,0:T(8,128)(2,1)S(1)}, u32[]{:S(2)}, u32[]{:S(2)}) collective-permute-start(bf16[2,16,2688]{2,1,0:T(8,128)(2,1)S(1)} %get-tuple-element.155), channel_id=1, source_target_pairs={{0,1},{1,0},{2,3},{3,2},{4,5},{5,4},{6,7},{7,6},{8,9},{9,8},{10,11... | collective-permute-start | bytes 516104 | tf_op jit(solution)/shard_map/ppermute | solution.py:700
  166.7 7.8 %collective-permute-start.28 = (bf16[4,16,1536]{2,1,0:T(8,128)(2,1)S(1)}, bf16[4,16,1536]{2,1,0:T(8,128)(2,1)S(1)}, u32[]{:S(2)}, u32[]{:S(2)}) collective-permute-start(bf16[4,16,1536]{2,1,0:T(8,128)(2,1)S(1)} %get-tuple-element.145), channel_id=1, source_target_pairs={{0,8},{4,12},{8,0},{12,4},{16,24},{20,28},{24,16},{28,20},{1,9},{5... | collective-permute-start | bytes 589832 | tf_op jit(solution)/shard_map/ppermute | solution.py:700
  167.1 10.6 %collective-permute-start.29 = (bf16[4,16,1536]{2,1,0:T(8,128)(2,1)S(1)}, bf16[4,16,1536]{2,1,0:T(8,128)(2,1)S(1)}, u32[]{:S(2)}, u32[]{:S(2)}) collective-permute-start(bf16[4,16,1536]{2,1,0:T(8,128)(2,1)S(1)} %get-tuple-element.146), channel_id=1, source_target_pairs={{0,16},{4,20},{8,24},{12,28},{16,0},{20,4},{24,8},{28,12},{1,17},{... | collective-permute-start | bytes 589832 | tf_op jit(solution)/shard_map/ppermute | solution.py:700
  168.6 9.1 %collective-permute-start.30 = (bf16[4,16,1536]{2,1,0:T(8,128)(2,1)S(1)}, bf16[4,16,1536]{2,1,0:T(8,128)(2,1)S(1)}, u32[]{:S(2)}, u32[]{:S(2)}) collective-permute-start(bf16[4,16,1536]{2,1,0:T(8,128)(2,1)S(1)} %get-tuple-element.147), channel_id=1, source_target_pairs={{0,24},{4,28},{8,16},{12,20},{16,8},{20,12},{24,0},{28,4},{1,25},{... | collective-permute-start | bytes 589832 | tf_op jit(solution)/shard_map/ppermute | solution.py:700
  173.7 19.9 %collective-permute-start.37 = (bf16[16,4096]{1,0:T(8,128)(2,1)S(1)}, bf16[16,4096]{1,0:T(8,128)(2,1)S(1)}, u32[]{:S(2)}, u32[]{:S(2)}) collective-permute-start(bf16[16,4096]{1,0:T(8,128)(2,1)S(1)} %fusion), channel_id=1, source_target_pairs={{0,2},{1,3},{2,0},{3,1},{4,6},{5,7},{6,4},{7,5},{8,10},{9,11},{10,... | collective-permute-start | bytes 393224 | tf_op jit(solution)/shard_map/ppermute | solution.py:700
  177.7 0.9 copy-start.15
  179.3 22.8 %copy-start.33 = (f32[256,512]{1,0:T(8,128)S(1)}, f32[256,512]{1,0:T(8,128)}, u32[]{:S(2)}) copy-start(f32[256,512]{1,0:T(8,128)} %get-tuple-element.128) | copy-start | bytes 1572868
  179.3 14.2 %collective-permute-start.31 = (bf16[16,1536]{1,0:T(8,128)(2,1)S(1)}, bf16[16,1536]{1,0:T(8,128)(2,1)S(1)}, u32[]{:S(2)}, u32[]{:S(2)}) collective-permute-start(bf16[16,1536]{1,0:T(8,128)(2,1)S(1)} %get-tuple-element.149), channel_id=1, source_target_pairs={{0,1},{1,0},{2,3},{3,2},{4,5},{5,4},{6,7},{7,6},{8,9},{9,8},{10,11... | collective-permute-start | bytes 147464 | tf_op jit(solution)/shard_map/ppermute | solution.py:700
  179.7 17.4 %collective-permute-start.32 = (bf16[16,1536]{1,0:T(8,128)(2,1)S(1)}, bf16[16,1536]{1,0:T(8,128)(2,1)S(1)}, u32[]{:S(2)}, u32[]{:S(2)}) collective-permute-start(bf16[16,1536]{1,0:T(8,128)(2,1)S(1)} %get-tuple-element.150), channel_id=1, source_target_pairs={{0,2},{1,3},{2,0},{3,1},{4,6},{5,7},{6,4},{7,5},{8,10},{9,11},{10,... | collective-permute-start | bytes 147464 | tf_op jit(solution)/shard_map/ppermute | solution.py:700
  181.6 15.4 %collective-permute-start.33 = (bf16[16,1536]{1,0:T(8,128)(2,1)S(1)}, bf16[16,1536]{1,0:T(8,128)(2,1)S(1)}, u32[]{:S(2)}, u32[]{:S(2)}) collective-permute-start(bf16[16,1536]{1,0:T(8,128)(2,1)S(1)} %get-tuple-element.151), channel_id=1, source_target_pairs={{0,3},{1,2},{2,1},{3,0},{4,7},{5,6},{6,5},{7,4},{8,11},{9,10},{10,... | collective-permute-start | bytes 147464 | tf_op jit(solution)/shard_map/ppermute | solution.py:700
  187.6 13.0 %collective-permute-start.35 = (bf16[16,2688]{1,0:T(8,128)(2,1)S(1)}, bf16[16,2688]{1,0:T(8,128)(2,1)S(1)}, u32[]{:S(2)}, u32[]{:S(2)}) collective-permute-start(bf16[16,2688]{1,0:T(8,128)(2,1)S(1)} %fusion.2), channel_id=1, source_target_pairs={{0,2},{1,3},{2,0},{3,1},{4,6},{5,7},{6,4},{7,5},{8,10},{9,11},{10,... | collective-permute-start | bytes 258056 | tf_op jit(solution)/shard_map/ppermute | solution.py:700
  (16 other events, 12.1 us)
Sparse Core Ops, SparseCore 0:
  11.6 79.0 all-gather.1
  133.5 25.0 reduce-scatter.4
  161.2 35.9 reduce-scatter.2
where the time goes:
time: 211 us; the launch traced here: 210 us
  waiting for transfers between devices  71.4 us (34%)
  Pallas kernels  58.7 us (28%)
  starting transfers between devices  39.1 us (19%)
  local copies, waits for them, and re-layouts  20.7 us (10%)
  between operations  14.3 us (7%)
  other arithmetic  6.36 us (3%)
    ppermute x38, waiting for transfers between devices, swap(): return lax.ppermute(block, axis_name, [(i, i ^ bits) for i in range(size)])  71.3 us
    pallas_call x18, Pallas kernels, go(): return call(*operands, *after)  58.7 us
    ppermute x38, starting transfers between devices, swap(): return lax.ppermute(block, axis_name, [(i, i ^ bits) for i in range(size)])  39 us
    unnamed x79, local copies, waits for them, and re-layouts  16.6 us
  transfers between devices with their start and end apart: 41, of which 20 were waited for; matrix products, arithmetic and copies ran while one was open for 4% of the time, Pallas kernels for 23%

commit v1 on v0

--- a/solution.py
+++ b/solution.py
@@ -70,6 +70,16 @@
                     target[pl.ds(start, rows), :] = part[
                         d, :, col + r * width : col + (r + 1) * width
                     ]
+
+
+def fetch_parts(near, far, held, sem):
+    copies = [
+        pltpu.make_async_copy(ref, held.at[side], sem.at[side])
+        for side, ref in enumerate((near, far))
+    ]
+    for copy in copies:
+        copy.start()
+    return copies
 
 
 def by_distance(pos, source, parts, col, sub=1):
@@ -260,20 +270,20 @@
 
 
 def kernel_call(
-    body, outs, out_specs, in_specs, scratch, name, flops, size, after=(), held_in=(), held_out=()
+    body, outs, out_specs, in_specs, scratch, name, flops, size, after=(), held_in=(), held_out=(), far_in=(), far_out=()
 ):
     n_in = len(in_specs)
     small = name in SMALL
 
-    def space(place, held):
-        return pltpu.VMEM if small or place in held else pltpu.HBM
+    def space(place, held, far):
+        return pltpu.VMEM if small and place not in far or place in held else pltpu.HBM
 
     def run(*refs):
         body(*refs[:n_in], *refs[n_in + len(after) :])
 
     single = not isinstance(outs, (tuple, list))
     outs = tuple(
-        space(place, held_out)(out.shape, out.dtype)
+        space(place, held_out, far_out)(out.shape, out.dtype)
         for place, out in enumerate([outs] if single else outs)
     )
     outs = outs[0] if single else outs
@@ -283,7 +293,7 @@
         in_specs=in_specs + [APART] * len(after),
         out_specs=out_specs,
         scratch_shapes=scratch,
-        compiler_params=pltpu.CompilerParams(vmem_limit_bytes=(4 if small else ROOM.get(name, 12)) * 2**20),
+        compiler_params=pltpu.CompilerParams(vmem_limit_bytes=(8 if small else ROOM.get(name, 12)) * 2**20),
         cost_estimate=pl.CostEstimate(flops=flops, bytes_accessed=size, transcendentals=0),
         name=name,
     )
@@ -292,7 +302,7 @@
         operands = [
             x
             if spec is SCALARS
-            else pltpu.with_memory_space_constraint(x, space(place, held_in))
+            else pltpu.with_memory_space_constraint(x, space(place, held_in, far_in))
             for place, (x, spec) in enumerate(zip(operands, in_specs, strict=True))
         ]
         return call(*operands, *after)
@@ -536,13 +546,13 @@
 def self_back_body(
     n_blocks, n_parts, pos, line, flow_in, one_t, mixed_one, query, keys_t, values, exps_in, *refs
 ):
-    near, far, refs = refs[:n_parts], refs[n_parts : 2 * n_parts], refs[2 * n_parts :]
+    near, far, refs = refs[0], refs[1], refs[2:]
     (own_out, query_t_out, kv_out, parts_out) = refs[:4]
-    weight, exps, sem = refs[4:]
+    weight, exps, sem, held, part_sem = refs[4:]
     count, feat = query.shape
     for pair in range(HEADS // 2):
         fetch(exps_in, exps, sem, pair).start()
-    in_order(pos, (near, far), weight, 0)
+    copies = fetch_parts(near, far, held, part_sem)
     grad_t = one_t[...]
     attend_back(
         query,
@@ -557,6 +567,9 @@
         query_t_out,
         kv_out,
     )
+    for copy in copies:
+        copy.wait()
+    in_order(pos, ([held.at[0]], [held.at[1]]), weight, 0)
     for d in range(n_blocks):
         part = dot_t(kv_out[d * count : (d + 1) * count, :], weight[:, feat:])
         place = pl.multiple_of((line[0] ^ d) * count, count)
@@ -576,8 +589,10 @@
             shape(keys, feat),
         ),
         [WHOLE] * 4,
-        [SCALARS] * 2 + [WHOLE] * 6 + [APART] + [WHOLE] * (2 * len(near)),
-        [VM((feat, 3 * feat), BF)] + back_scratch(keys, feat, count)[2:],
+        [SCALARS] * 2 + [WHOLE] * 6 + [APART] * 3,
+        [VM((feat, 3 * feat), BF)]
+        + back_scratch(keys, feat, count)[2:]
+        + [VM((2,) + near[0].shape, BF), pltpu.SemaphoreType.DMA((2,))],
         "self_back",
         12 * 10**9,
         20 * 10**6,
@@ -615,9 +630,10 @@
 
 
 def pack_body(sub, source, target, glance, ids, pad, encoder, *refs):
-    refs, encoder_out = refs[:-1], refs[-1]
+    refs, encoder_out = (*refs[:-2], refs[-1]), refs[-2]
     encoder_out[...] = encoder[...]
-    weights, (vectors, inner, outer, three, early, mixed) = refs[:8], refs[8:]
+    weights, vectors, refs = refs[:8], refs[8:14], refs[14:]
+    inner, outer, three, early, mixed, lines = refs
     rows, feat = weights[0].shape
     count = glance.shape[1]
     wide = inner.shape[1]
@@ -626,9 +642,10 @@
         three[:, wide + r * feat : wide + (r + 1) * feat] = outer[r * rows : (r + 1) * rows, :]
     for place, weight in enumerate(weights):
         early[:, place * feat : (place + 1) * feat] = weight[...]
-    lines = vectors[...].astype(F32)
-    lines = jnp.concatenate([lines, jnp.zeros((128 - lines.shape[0], lines.shape[1]), F32)], axis=0)
-    early[:, 8 * feat :] = low(lines.T)[:rows, :]
+    lines[...] = jnp.zeros_like(lines)
+    for place, vector in enumerate(vectors):
+        lines[place : place + 1, :rows] = vector[...].astype(F32)
+    early[:, 8 * feat :] = low(lines[...].T)[:rows, :]
     taken = jnp.broadcast_to(glance[...].astype(F32), (128, count)).T[:, :1]
     mixed[:count, :] = jnp.where(taken > 0.5, target[0], source[0])
     key_ids = jnp.where(pad[...] == 1, ids[...], -1).astype(F32)
@@ -766,7 +783,7 @@
             odd[d // 2, :, cut:] = low(right)
 
 
-def add_call(body, outs, operands, after, name):
+def add_call(body, outs, operands, after, name, far_in=(), far_out=()):
     return kernel_call(
         body,
         outs,
@@ -777,6 +794,8 @@
         10**9,
         4 * 10**6,
         after,
+        far_in=far_in,
+        far_out=far_out,
     )(*operands)
 
 
@@ -796,7 +815,7 @@
     x_dims, y_dims = x_rest.shape[1:], y_rest.shape[1:]
     outs = [shape(*x_dims), shape(*y_dims), shape(*x_dims, dtype=F32), shape(*y_dims, dtype=F32)]
     y_send, x_send, x_own, y_own = add_call(
-        add_mid_body, outs, (x_rest, x_got, y_rest, y_got), after, "add_mid"
+        add_mid_body, outs, (x_rest, x_got, y_rest, y_got), after, "add_mid", (), (2, 3)
     )
     return (y_send, swap(y_send, "fsdp", fsdp, 4), swap(x_send, "fsdp", fsdp, 2), x_own, y_own)
 
@@ -807,7 +826,7 @@
     rows, cols = x_own.shape[1], cut + y_own.shape[2]
     outs = [shape(rows, cols, dtype=F32), shape(2, rows, cols), shape(rows, cols)]
     return add_call(
-        functools.partial(add_near_body, cut), outs, (x_own, x_got, y_own, y_got), after, "add_near"
+        functools.partial(add_near_body, cut), outs, (x_own, x_got, y_own, y_got), after, "add_near", (0, 2)
     )
 
 
@@ -930,17 +949,15 @@
         ids = segment_ids.reshape(1, count)
         pad = pad_mask.reshape(1, count)
         encoder = encoder_out.reshape(count, feat)
-        vectors = jnp.stack(
-            [norm1_gain, norm1_shift, norm2_gain, norm2_shift, norm3_gain, norm3_shift]
-        )
-        vectors = jnp.pad(vectors, ((0, 0), (0, 128 - chunk)))
+        vectors = (norm1_gain, norm1_shift, norm2_gain, norm2_shift, norm3_gain, norm3_shift)
+        vectors = [vector.reshape(1, chunk) for vector in vectors]
         wide = sub * feat
         three, early, mixed, encoder = kernel_call(
             functools.partial(pack_body, sub),
             (shape(chunk, 2 * wide), shape(chunk, 8 * feat + 128), shape(count + 16, feat), shape(count, feat)),
             [WHOLE] * 4,
-            [WHOLE] * 17,
-            [],
+            [WHOLE] * 22,
+            [VM((128, 128), F32)],
             "pack",
             10**9,
             2 * 10**6,
@@ -959,7 +976,7 @@
             cross_key,
             cross_value,
             cross_output,
-            vectors,
+            *vectors,
             inner_weight,
             outer_weight,
         )
@@ -1096,9 +1113,7 @@
             home, mixed_blocks, query_t, kv, near_one.shape, after_grads
         )
         if near_rows:
-            got_two = [hold(got, keep_one, space=pltpu.VMEM) for got in mid_two[1:3]]
-            mid_two = (mid_two[0], *got_two, *mid_two[3:])
-            away_one = swap(hold(away_one, *got_two, space=pltpu.VMEM), "fsdp", fsdp, 1)
+            away_one = swap(away_one, "fsdp", fsdp, 1)
             one_send = add_call(
                 add_one_body,
                 [shape(*keep_one.shape[1:])] * 4,
@@ -1106,7 +1121,9 @@
                 (),
                 "add_one",
             )
-            near_two = near_step(mid_two, (one_send[0],))
+            got_two = [hold(got, one_send[0], space=pltpu.VMEM) for got in mid_two[1:3]]
+            mid_two = (mid_two[0], *got_two, *mid_two[3:])
+            near_two = near_step(mid_two, ())
             near_three = finish_line(near_three, seq, one_send[0])
             got_one = [swap(one_send[e], "fsdp", fsdp, 2 * e) for e in (1, 2, 3)]
             line_one = add_call(

time: 211 us -> 208 us (0.986)
  local copies, waits for them, and re-layouts: 20.7 us -> 17.3 us
    unnamed x79 -> x59, local copies, waits for them, and re-layouts: 16.6 us -> 14.6 us
  transfers between devices with their start and end apart: 41 -> 41, of which waited for: 20 -> 17; matrix products, arithmetic and copies ran while one was open for 4% -> 4% of each run, Pallas kernels for 23% -> 23%
where the time goes in v1:
time: 208 us
  waiting for transfers between devices  69.7 us (34%)
  Pallas kernels  60.7 us (29%)
  starting transfers between devices  39.3 us (19%)
  local copies, waits for them, and re-layouts  17.3 us (8%)
  between operations  14.2 us (7%)
  other arithmetic  6.25 us (3%)
    ppermute x38, waiting for transfers between devices, swap(): return lax.ppermute(block, axis_name, [(i, i ^ bits) for i in range(size)])  69.6 us
    pallas_call x18, Pallas kernels, go(): return call(*operands, *after)  60.7 us
    ppermute x38, starting transfers between devices, swap(): return lax.ppermute(block, axis_name, [(i, i ^ bits) for i in range(size)])  39.2 us
    unnamed x59, local copies, waits for them, and re-layouts  14.6 us
  transfers between devices with their start and end apart: 41, of which 17 were waited for; matrix products, arithmetic and copies ran while one was open for 4% of the time, Pallas kernels for 23%

profile of v1, /device:TPU:0, one launch (start us, length us, event | category | flops | bytes accessed | tf_op | source)
XLA Modules:
  0.0 207.5 jit_solution(1721256483747910704)
XLA Ops:
  7.2 2.3 %pack.1 = (bf16[16,4096]{1,0:T(8,128)(2,1)}, bf16[16,4224]{1,0:T(8,128)(2,1)}, bf16[272,512]{1,0:T(8,128)(2,1)}, bf16[256,512]{1,0:T(8,128)(2,1)}) custom-call(bf16[1,256,512]{2,1,0:T(8,128)(2,1)} %source.1, bf16[1,256,512]{2,1,0:T(8,128)(2,1)} %target.1, s32[1,256]{1,0:T(1,128)} %glance.1, s32[1,256]{1,0:T(1,128)} %refs_6_.5, s32[1,256]{1,0:T(1,128)} %pad.15, ...), custom_call_target="tpu_custom_call" | custom-call | flops 1000000000 | bytes 2000000 | tf_op jit(solution)/shard_map/pack/pallas_call | solution.py:308
  9.6 3.1 %collective-permute-start.3 = (bf16[272,512]{1,0:T(8,128)(2,1)}, bf16[272,512]{1,0:T(8,128)(2,1)S(1)}, u32[]{:S(2)}, u32[]{:S(2)}) collective-permute-start(bf16[272,512]{1,0:T(8,128)(2,1)} %get-tuple-element.91.refs_0_.refs_8_.refs_1_), channel_id=1, source_target_pairs={{0,1},{1,0},{2,3},{3,2},{4,5},{5,4},{6,7},{7,6},{8,9},{9,8},{10,11... | collective-permute-start | bytes 835592 | tf_op jit(solution)/shard_map/ppermute | solution.py:717
  12.7 2.5 %collective-permute-start.2 = (bf16[16,4224]{1,0:T(8,128)(2,1)}, bf16[16,4224]{1,0:T(8,128)(2,1)S(1)}, u32[]{:S(2)}, u32[]{:S(2)}) collective-permute-start(bf16[16,4224]{1,0:T(8,128)(2,1)} %get-tuple-element.90.refs_0_), channel_id=1, source_target_pairs={{0,3},{1,2},{2,1},{3,0},{4,7},{5,6},{6,5},{7,4},{8,11},{9,10},{10,... | collective-permute-start | bytes 405512 | tf_op jit(solution)/shard_map/ppermute | solution.py:717
  15.3 1.8 collective-permute-start
  17.1 1.7 collective-permute-start.7
  18.8 7.1 %collective-permute-done.2.refs_3_ = bf16[16,4224]{1,0:T(8,128)(2,1)S(1)} collective-permute-done((bf16[16,4224]{1,0:T(8,128)(2,1)}, bf16[16,4224]{1,0:T(8,128)(2,1)S(1)}, u32[]{:S(2)}, u32[]{:S(2)}) %collective-permute-start.2) | collective-permute-done | bytes 135200 | tf_op jit(solution)/shard_map/ppermute | solution.py:717
  25.9 3.6 %collective-permute-done.1.refs_2_ = bf16[16,4224]{1,0:T(8,128)(2,1)S(1)} collective-permute-done((bf16[16,4224]{1,0:T(8,128)(2,1)}, bf16[16,4224]{1,0:T(8,128)(2,1)S(1)}, u32[]{:S(2)}, u32[]{:S(2)}) %collective-permute-start.1) | collective-permute-done | bytes 135200 | tf_op jit(solution)/shard_map/ppermute | solution.py:717
  29.5 3.4 %collective-permute-done.refs_1_ = bf16[16,4224]{1,0:T(8,128)(2,1)S(1)} collective-permute-done((bf16[16,4224]{1,0:T(8,128)(2,1)}, bf16[16,4224]{1,0:T(8,128)(2,1)S(1)}, u32[]{:S(2)}, u32[]{:S(2)}) %collective-permute-start) | collective-permute-done | bytes 135200 | tf_op jit(solution)/shard_map/ppermute | solution.py:717
  32.9 0.9 copy-done.12
  33.8 0.7 copy-done.11
  34.5 2.9 %collective-permute-start.6 = (bf16[4,16,1536]{2,1,0:T(8,128)(2,1)S(1)}, bf16[4,16,1536]{2,1,0:T(8,128)(2,1)S(1)}, u32[]{:S(2)}, u32[]{:S(2)}) collective-permute-start(bf16[4,16,1536]{2,1,0:T(8,128)(2,1)S(1)} %get-tuple-element.92.refs_0_), channel_id=1, source_target_pairs={{0,24},{4,28},{8,16},{12,20},{16,8},{20,12},{24,0},{28,4},{1,25},{... | collective-permute-start | bytes 589832 | tf_op jit(solution)/shard_map/ppermute | solution.py:717
  38.0 4.3 %collective-permute-done.7.refs_4_.refs_0_ = bf16[272,512]{1,0:T(8,128)(2,1)S(1)} collective-permute-done((bf16[272,512]{1,0:T(8,128)(2,1)}, bf16[272,512]{1,0:T(8,128)(2,1)S(1)}, u32[]{:S(2)}, u32[]{:S(2)}) %collective-permute-start.7) | collective-permute-done | bytes 278560 | tf_op jit(solution)/shard_map/ppermute | solution.py:717
  42.3 0.9 collective-permute-done.5.refs_2_
  43.7 0.8 copy-done.4
  44.9 0.7 copy.55.refs_0_
  45.6 1.5 collective-permute-start.15
  47.1 1.3 collective-permute-start.14
  48.5 0.7 collective-permute-start.13
  49.1 0.9 copy-done.22
  50.0 4.6 %collective-permute-start.11 = (bf16[256,512]{1,0:T(8,128)(2,1)}, bf16[256,512]{1,0:T(8,128)(2,1)S(1)}, u32[]{:S(2)}, u32[]{:S(2)}) collective-permute-start(bf16[256,512]{1,0:T(8,128)(2,1)} %hold.13), channel_id=1, source_target_pairs={{0,2},{1,3},{2,0},{3,1},{4,6},{5,7},{6,4},{7,5},{8,10},{9,11},{10,... | collective-permute-start | bytes 786440 | tf_op jit(solution)/shard_map/ppermute | solution.py:717
  54.7 7.4 %collective-permute-done.10.refs_3_.refs_4_ = bf16[272,512]{1,0:T(8,128)(2,1)} collective-permute-done((bf16[272,512]{1,0:T(8,128)(2,1)S(1)}, bf16[272,512]{1,0:T(8,128)(2,1)}, u32[]{:S(2)}, u32[]{:S(2)}) %collective-permute-start.10) | collective-permute-done | bytes 278560 | tf_op jit(solution)/shard_map/ppermute | solution.py:717
  62.1 8.8 %self_attend.1 = (bf16[256,512]{1,0:T(8,128)(2,1)}, bf16[1024,512]{1,0:T(8,128)(2,1)}, bf16[512,1024]{1,0:T(8,128)(2,1)}, bf16[512,256]{1,0:T(8,128)(2,1)}, f32[...) custom-call(s32[2]{0:T(128)S(1)} %pad_add_fusion.pos.refs_0_, ...), custom_call_target="tpu_custom_call" | custom-call | flops 12000000000 | bytes 20000000 | tf_op jit(solution)/shard_map/self_attend/pallas_call | solution.py:308
  71.0 4.9 %collective-permute-done.9.refs_0_ = bf16[256,512]{1,0:T(8,128)(2,1)S(1)} collective-permute-done((bf16[256,512]{1,0:T(8,128)(2,1)}, bf16[256,512]{1,0:T(8,128)(2,1)S(1)}, u32[]{:S(2)}, u32[]{:S(2)}) %collective-permute-start.9) | collective-permute-done | bytes 262176 | tf_op jit(solution)/shard_map/ppermute | solution.py:717
  76.9 13.3 %collective-permute-done.12.refs_3_.refs_5_ = bf16[256,512]{1,0:T(8,128)(2,1)S(1)} collective-permute-done((bf16[256,512]{1,0:T(8,128)(2,1)S(1)}, bf16[256,512]{1,0:T(8,128)(2,1)S(1)}, u32[]{:S(2)}, u32[]{:S(2)}) %collective-permute-start.12) | collective-permute-done | bytes 262176 | tf_op jit(solution)/shard_map/ppermute | solution.py:717
  90.2 0.7 copy-done.28
  91.4 10.1 %cross_attend.1 = (f32[8,512]{1,0:T(8,128)}, f32[256,512]{1,0:T(8,128)}, f32[256,128]{1,0:T(8,128)}, bf16[256,512]{1,0:T(8,128)(2,1)}, bf16[1024,512]{1,0:T(8,12...) custom-call(s32[2]{0:T(128)S(1)} %pad_add_fusion.pos.refs_0_, ...), custom_call_target="tpu_custom_call" | custom-call | flops 14000000000 | bytes 20000000 | tf_op jit(solution)/shard_map/cross_attend/pallas_call | solution.py:308
  101.5 8.0 %feed.1 = (bf16[256,512]{1,0:T(8,128)(2,1)}, f32[256,512]{1,0:T(8,128)S(1)}, f32[8,512]{1,0:T(8,128)S(1)}, bf16[4,4,16,4096]{3,2,1,0:T(8,128)(2,1)S(1)}, bf16[4,4,16,4096]{3,2,1,0:T(8,128)(2,1)S(1)}) custom-call(s32[2]{0:T(128)S(1)} %pad_add_fusion.pos.refs_0_, f32[256,512]{1,0:T(8,128)S(1)} %get-tuple-element.96.unit_in, ...), custom_call_target="tpu_custom_call" | custom-call | flops 6000000000 | bytes 20000000 | tf_op jit(solution)/shard_map/feed/pallas_call | solution.py:308
  109.5 4.2 %collective-permute-done.17.away = bf16[4,4,16,4096]{3,2,1,0:T(8,128)(2,1)S(1)} collective-permute-done((bf16[4,4,16,4096]{3,2,1,0:T(8,128)(2,1)S(1)}, bf16[4,4,16,4096]{3,2,1,0:T(8,128)(2,1)S(1)}, u32[]{:S(2)}, u32[]{:S(2)}) %collective-permute-start.17) | collective-permute-done | bytes 2097184 | tf_op jit(solution)/shard_map/ppermute | solution.py:717
  114.1 1.5 collective-permute-start.19
  115.6 13.2 %cross_back.1 = (f32[256,512]{1,0:T(8,128)S(1)}, bf16[512,256]{1,0:T(8,128)(2,1)S(1)}, bf16[4,4,16,2688]{3,2,1,0:T(8,128)(2,1)S(1)}, bf16[4,4,16,2688]{3,2,1,0:T(8,128)(2,1)S(1)}, bf16[1024,512]{1,0:T(8,128)(2,1)}) custom-call(s32[2]{0:T(128)S(1)} %pad_add_fusion.pos.refs_0_, s32[1]{0:T(128)} %bitcast.1.refs_1_, ...), custom_call_target="tpu_custom_call" | custom-call | flops 15000000512 | bytes 20000000 | tf_op jit(solution)/shard_map/cross_back/pallas_call | solution.py:308
  129.3 1.2 add_mid.2
  130.5 0.7 copy-done.6
  131.5 0.8 copy-done.7
  132.2 1.5 collective-permute-start.21
  133.7 0.8 collective-permute-start.22
  134.5 1.4 copy-done.14
  136.3 1.7 collective-permute-start.23
  138.5 0.9 copy-done.20
  139.5 9.6 %self_back.1 = (f32[256,512]{1,0:T(8,128)}, bf16[512,256]{1,0:T(8,128)(2,1)S(1)}, bf16[1024,1024]{1,0:T(8,128)(2,1)S(1)}, bf16[1024,512]{1,0:T(8,128)(2,1)}) custom-call(s32[2]{0:T(128)S(1)} %pad_add_fusion.pos.refs_0_, s32[1]{0:T(128)} %bitcast.1.refs_1_, f32[256,512]{1,0:T(8,128)S(1)} %copy-done.16, bf16[512,256]{1,0:T(8,128)(2,1)S(1)} %copy-done.20, ...), custom_call_target="tpu_custom_call" | custom-call | flops 12000000000 | bytes 20000000 | tf_op jit(solution)/shard_map/self_back/pallas_call | solution.py:308
  149.1 1.3 add_near.2
  150.4 0.9 add_mid.3
  151.3 2.7 %self_grads.1 = (bf16[4,4,16,1536]{3,2,1,0:T(8,128)(2,1)S(1)}, bf16[4,4,16,1536]{3,2,1,0:T(8,128)(2,1)S(1)}) custom-call(s32[2]{0:T(128)S(1)} %pad_add_fusion.pos.refs_0_, bf16[272,512]{1,0:T(8,128)(2,1)} %get-tuple-element.91.refs_0_.refs_8_.refs_1_, bf16[272,512]{1,0:T(8,128)(2,1)} %copy-done.11, bf16[272,512]{1,0:T(8,128)(2,1)} %copy-done.5, ...), custom_call_target="tpu_custom_call" | custom-call | flops 5000000000 | bytes 8000000 | tf_op jit(solution)/shard_map/self_grads/pallas_call | solution.py:308
  154.1 0.9 copy-done.17
  155.0 1.5 collective-permute-start.32
  157.0 1.8 bitcast_convert_fusion
  158.8 1.1 copy-done.18
  160.1 0.7 copy-done.2
  160.8 2.4 %collective-permute-done.33.refs_0_ = bf16[4,16,1408]{2,1,0:T(8,128)(2,1)S(1)} collective-permute-done((bf16[4,16,1408]{2,1,0:T(8,128)(2,1)S(1)}, bf16[4,16,1408]{2,1,0:T(8,128)(2,1)S(1)}, u32[]{:S(2)}, u32[]{:S(2)}) %collective-permute-start.33) | collective-permute-done | bytes 180256 | tf_op jit(solution)/shard_map/ppermute | solution.py:717
  163.2 1.3 add_near.3
  164.5 1.8 collective-permute-start.34
  166.6 1.4 collective-permute-start.27
  168.0 1.8 collective-permute-start.28
  170.0 3.9 %collective-permute-done.26.first = bf16[4,16,1536]{2,1,0:T(8,128)(2,1)S(1)} collective-permute-done((bf16[4,16,1536]{2,1,0:T(8,128)(2,1)S(1)}, bf16[4,16,1536]{2,1,0:T(8,128)(2,1)S(1)}, u32[]{:S(2)}, u32[]{:S(2)}) %collective-permute-start.26) | collective-permute-done | bytes 196640 | tf_op jit(solution)/shard_map/ppermute | solution.py:717
  173.9 2.4 %collective-permute-done.27.second = bf16[4,16,1536]{2,1,0:T(8,128)(2,1)S(1)} collective-permute-done((bf16[4,16,1536]{2,1,0:T(8,128)(2,1)S(1)}, bf16[4,16,1536]{2,1,0:T(8,128)(2,1)S(1)}, u32[]{:S(2)}, u32[]{:S(2)}) %collective-permute-start.27) | collective-permute-done | bytes 196640 | tf_op jit(solution)/shard_map/ppermute | solution.py:717
  177.5 1.5 collective-permute-start.30
  179.0 2.3 %collective-permute-start.31 = (bf16[16,1536]{1,0:T(8,128)(2,1)S(1)}, bf16[16,1536]{1,0:T(8,128)(2,1)S(1)}, u32[]{:S(2)}, u32[]{:S(2)}) collective-permute-start(bf16[16,1536]{1,0:T(8,128)(2,1)S(1)} %get-tuple-element.150), channel_id=1, source_target_pairs={{0,3},{1,2},{2,1},{3,0},{4,7},{5,6},{6,5},{7,4},{8,11},{9,10},{10,... | collective-permute-start | bytes 147464 | tf_op jit(solution)/shard_map/ppermute | solution.py:717
  181.5 7.5 %collective-permute-done.37.refs_0_ = bf16[16,4096]{1,0:T(8,128)(2,1)S(1)} collective-permute-done((bf16[16,4096]{1,0:T(8,128)(2,1)S(1)}, bf16[16,4096]{1,0:T(8,128)(2,1)S(1)}, u32[]{:S(2)}, u32[]{:S(2)}) %collective-permute-start.37) | collective-permute-done | bytes 131104 | tf_op jit(solution)/shard_map/ppermute | solution.py:717
  190.3 0.9 fusion.1
  191.9 1.7 collective-permute-done.30
  193.6 0.9 convert_add_fusion.4
  195.1 0.7 pad_maximum_fusion
  195.8 1.9 collective-permute-done.35
  197.7 0.8 slice_reduce_fusion
  199.2 1.8 add_bitcast_fusion
  (126 shorter events, 11.2 us)
Async XLA Ops:
  7.2 94.3 %all-gather.2.cloned.1.call-start = ((), (), s32[]{:S(2)}) async-start(), calls=%async_computation.2 | async-start | bytes 4325376 | tf_op jit(solution)/shard_map/all_gather | solution.py:983
  9.6 147.4 %reduce-scatter.5.cloned.1.call-start = ((), (), s32[]{:S(2)}) async-start(), calls=%async_computation.4 | async-start | bytes 1310720 | tf_op jit(solution)/shard_map/reduce_scatter | solution.py:1086
  9.6 23.2 %collective-permute-start.3 = (bf16[272,512]{1,0:T(8,128)(2,1)}, bf16[272,512]{1,0:T(8,128)(2,1)S(1)}, u32[]{:S(2)}, u32[]{:S(2)}) collective-permute-start(bf16[272,512]{1,0:T(8,128)(2,1)} %get-tuple-element.91.refs_0_.refs_8_.refs_1_), channel_id=1, source_target_pairs={{0,1},{1,0},{2,3},{3,2},{4,5},{5,4},{6,7},{7,6},{8,9},{9,8},{10,11... | collective-permute-start | bytes 835592 | tf_op jit(solution)/shard_map/ppermute | solution.py:717
  12.7 13.2 %collective-permute-start.2 = (bf16[16,4224]{1,0:T(8,128)(2,1)}, bf16[16,4224]{1,0:T(8,128)(2,1)S(1)}, u32[]{:S(2)}, u32[]{:S(2)}) collective-permute-start(bf16[16,4224]{1,0:T(8,128)(2,1)} %get-tuple-element.90.refs_0_), channel_id=1, source_target_pairs={{0,3},{1,2},{2,1},{3,0},{4,7},{5,6},{6,5},{7,4},{8,11},{9,10},{10,... | collective-permute-start | bytes 405512 | tf_op jit(solution)/shard_map/ppermute | solution.py:717
  15.2 14.3 %collective-permute-start.1 = (bf16[16,4224]{1,0:T(8,128)(2,1)}, bf16[16,4224]{1,0:T(8,128)(2,1)S(1)}, u32[]{:S(2)}, u32[]{:S(2)}) collective-permute-start(bf16[16,4224]{1,0:T(8,128)(2,1)} %get-tuple-element.90.refs_0_), channel_id=1, source_target_pairs={{0,2},{1,3},{2,0},{3,1},{4,6},{5,7},{6,4},{7,5},{8,10},{9,11},{10,... | collective-permute-start | bytes 405512 | tf_op jit(solution)/shard_map/ppermute | solution.py:717
  15.3 17.6 %collective-permute-start = (bf16[16,4224]{1,0:T(8,128)(2,1)}, bf16[16,4224]{1,0:T(8,128)(2,1)S(1)}, u32[]{:S(2)}, u32[]{:S(2)}) collective-permute-start(bf16[16,4224]{1,0:T(8,128)(2,1)} %get-tuple-element.90.refs_0_), channel_id=1, source_target_pairs={{0,1},{1,0},{2,3},{3,2},{4,5},{5,4},{6,7},{7,6},{8,9},{9,8},{10,11... | collective-permute-start | bytes 405512 | tf_op jit(solution)/shard_map/ppermute | solution.py:717
  17.1 25.2 %collective-permute-start.7 = (bf16[272,512]{1,0:T(8,128)(2,1)}, bf16[272,512]{1,0:T(8,128)(2,1)S(1)}, u32[]{:S(2)}, u32[]{:S(2)}) collective-permute-start(bf16[272,512]{1,0:T(8,128)(2,1)} %get-tuple-element.91.refs_0_.refs_8_.refs_1_), channel_id=1, source_target_pairs={{0,2},{1,3},{2,0},{3,1},{4,6},{5,7},{6,4},{7,5},{8,10},{9,11},{10,... | collective-permute-start | bytes 835592 | tf_op jit(solution)/shard_map/ppermute | solution.py:717
  32.9 0.9 copy-start.12
  33.8 0.7 copy-start.11
  34.5 10.4 %copy-start.25 = (bf16[256,512]{1,0:T(8,128)(2,1)S(1)}, bf16[256,512]{1,0:T(8,128)(2,1)}, u32[]{:S(2)}) copy-start(bf16[256,512]{1,0:T(8,128)(2,1)} %get-tuple-element.89.refs_0_.refs_2_) | copy-start | bytes 786436
  34.5 7.8 %collective-permute-start.6 = (bf16[4,16,1536]{2,1,0:T(8,128)(2,1)S(1)}, bf16[4,16,1536]{2,1,0:T(8,128)(2,1)S(1)}, u32[]{:S(2)}, u32[]{:S(2)}) collective-permute-start(bf16[4,16,1536]{2,1,0:T(8,128)(2,1)S(1)} %get-tuple-element.92.refs_0_), channel_id=1, source_target_pairs={{0,24},{4,28},{8,16},{12,20},{16,8},{20,12},{24,0},{28,4},{1,25},{... | collective-permute-start | bytes 589832 | tf_op jit(solution)/shard_map/ppermute | solution.py:717
  37.4 5.8 %collective-permute-start.5 = (bf16[4,16,1536]{2,1,0:T(8,128)(2,1)S(1)}, bf16[4,16,1536]{2,1,0:T(8,128)(2,1)S(1)}, u32[]{:S(2)}, u32[]{:S(2)}) collective-permute-start(bf16[4,16,1536]{2,1,0:T(8,128)(2,1)S(1)} %get-tuple-element.92.refs_0_), channel_id=1, source_target_pairs={{0,16},{4,20},{8,24},{12,28},{16,0},{20,4},{24,8},{28,12},{1,17},{... | collective-permute-start | bytes 589832 | tf_op jit(solution)/shard_map/ppermute | solution.py:717
  37.8 5.8 %collective-permute-start.4 = (bf16[4,16,1536]{2,1,0:T(8,128)(2,1)S(1)}, bf16[4,16,1536]{2,1,0:T(8,128)(2,1)S(1)}, u32[]{:S(2)}, u32[]{:S(2)}) collective-permute-start(bf16[4,16,1536]{2,1,0:T(8,128)(2,1)S(1)} %get-tuple-element.92.refs_0_), channel_id=1, source_target_pairs={{0,8},{4,12},{8,0},{12,4},{16,24},{20,28},{24,16},{28,20},{1,9},{5... | collective-permute-start | bytes 589832 | tf_op jit(solution)/shard_map/ppermute | solution.py:717
  43.7 0.9 copy-start.4
  43.7 5.5 %collective-permute-start.8 = (bf16[4,4,16,1536]{3,2,1,0:T(8,128)(2,1)S(1)}, bf16[4,4,16,1536]{3,2,1,0:T(8,128)(2,1)S(1)}, u32[]{:S(2)}, u32[]{:S(2)}) collective-permute-start(bf16[4,4,16,1536]{3,2,1,0:T(8,128)(2,1)S(1)} %join.2.refs_1_.refs_4_.refs_9_), channel_id=1, source_target_pairs={{0,4},{4,0},{8,12},{12,8},{16,20},{20,16},{24,28},{28,24},{1,5},{5... | collective-permute-start | bytes 2359304 | tf_op jit(solution)/shard_map/ppermute | solution.py:717
  44.5 17.5 %copy-start.5 = (bf16[272,512]{1,0:T(8,128)(2,1)}, bf16[272,512]{1,0:T(8,128)(2,1)S(1)}, u32[]{:S(2)}) copy-start(bf16[272,512]{1,0:T(8,128)(2,1)S(1)} %hold.14.refs_2_.refs_3_) | copy-start | bytes 835588
  44.5 17.5 %collective-permute-start.10 = (bf16[272,512]{1,0:T(8,128)(2,1)S(1)}, bf16[272,512]{1,0:T(8,128)(2,1)}, u32[]{:S(2)}, u32[]{:S(2)}) collective-permute-start(bf16[272,512]{1,0:T(8,128)(2,1)S(1)} %hold.14.refs_2_.refs_3_), channel_id=1, source_target_pairs={{0,1},{1,0},{2,3},{3,2},{4,5},{5,4},{6,7},{7,6},{8,9},{9,8},{10,11... | collective-permute-start | bytes 835592 | tf_op jit(solution)/shard_map/ppermute | solution.py:717
  45.6 30.2 %collective-permute-start.15 = (bf16[4,16,2688]{2,1,0:T(8,128)(2,1)S(1)}, bf16[4,16,2688]{2,1,0:T(8,128)(2,1)S(1)}, u32[]{:S(2)}, u32[]{:S(2)}) collective-permute-start(bf16[4,16,2688]{2,1,0:T(8,128)(2,1)S(1)} %get-tuple-element.94.refs_0_), channel_id=1, source_target_pairs={{0,24},{4,28},{8,16},{12,20},{16,8},{20,12},{24,0},{28,4},{1,25},{... | collective-permute-start | bytes 1032200 | tf_op jit(solution)/shard_map/ppermute | solution.py:717
  47.1 28.8 %collective-permute-start.14 = (bf16[4,16,2688]{2,1,0:T(8,128)(2,1)S(1)}, bf16[4,16,2688]{2,1,0:T(8,128)(2,1)S(1)}, u32[]{:S(2)}, u32[]{:S(2)}) collective-permute-start(bf16[4,16,2688]{2,1,0:T(8,128)(2,1)S(1)} %get-tuple-element.94.refs_0_), channel_id=1, source_target_pairs={{0,16},{4,20},{8,24},{12,28},{16,0},{20,4},{24,8},{28,12},{1,17},{... | collective-permute-start | bytes 1032200 | tf_op jit(solution)/shard_map/ppermute | solution.py:717
  48.5 27.5 %collective-permute-start.13 = (bf16[4,16,2688]{2,1,0:T(8,128)(2,1)S(1)}, bf16[4,16,2688]{2,1,0:T(8,128)(2,1)S(1)}, u32[]{:S(2)}, u32[]{:S(2)}) collective-permute-start(bf16[4,16,2688]{2,1,0:T(8,128)(2,1)S(1)} %get-tuple-element.94.refs_0_), channel_id=1, source_target_pairs={{0,8},{4,12},{8,0},{12,4},{16,24},{20,28},{24,16},{28,20},{1,9},{5... | collective-permute-start | bytes 1032200 | tf_op jit(solution)/shard_map/ppermute | solution.py:717
  49.1 0.9 copy-start.22
  50.0 20.9 %collective-permute-start.11 = (bf16[256,512]{1,0:T(8,128)(2,1)}, bf16[256,512]{1,0:T(8,128)(2,1)S(1)}, u32[]{:S(2)}, u32[]{:S(2)}) collective-permute-start(bf16[256,512]{1,0:T(8,128)(2,1)} %hold.13), channel_id=1, source_target_pairs={{0,2},{1,3},{2,0},{3,1},{4,6},{5,7},{6,4},{7,5},{8,10},{9,11},{10,... | collective-permute-start | bytes 786440 | tf_op jit(solution)/shard_map/ppermute | solution.py:717
  62.1 13.8 %collective-permute-start.9 = (bf16[256,512]{1,0:T(8,128)(2,1)}, bf16[256,512]{1,0:T(8,128)(2,1)S(1)}, u32[]{:S(2)}, u32[]{:S(2)}) collective-permute-start(bf16[256,512]{1,0:T(8,128)(2,1)} %hold.13), channel_id=1, source_target_pairs={{0,1},{1,0},{2,3},{3,2},{4,5},{5,4},{6,7},{7,6},{8,9},{9,8},{10,11... | collective-permute-start | bytes 786440 | tf_op jit(solution)/shard_map/ppermute | solution.py:717
  70.9 4.9 %copy-start = (bf16[256,512]{1,0:T(8,128)(2,1)}, bf16[256,512]{1,0:T(8,128)(2,1)S(1)}, u32[]{:S(2)}) copy-start(bf16[256,512]{1,0:T(8,128)(2,1)S(1)} %hold.16.refs_1_.refs_2_.refs_4_) | copy-start | bytes 786436
  75.9 1.0 copy-start.1
  76.6 13.6 %copy-start.10 = (bf16[4,4,16,2688]{3,2,1,0:T(8,128)(2,1)}, bf16[4,4,16,2688]{3,2,1,0:T(8,128)(2,1)S(1)}, u32[]{:S(2)}) copy-start(bf16[4,4,16,2688]{3,2,1,0:T(8,128)(2,1)S(1)} %join.3.refs_4_.refs_6_) | copy-start | bytes 4128772
  76.6 13.6 %collective-permute-start.16 = (bf16[4,4,16,2688]{3,2,1,0:T(8,128)(2,1)S(1)}, bf16[4,4,16,2688]{3,2,1,0:T(8,128)(2,1)S(1)}, u32[]{:S(2)}, u32[]{:S(2)}) collective-permute-start(bf16[4,4,16,2688]{3,2,1,0:T(8,128)(2,1)S(1)} %join.3.refs_4_.refs_6_), channel_id=1, source_target_pairs={{0,4},{4,0},{8,12},{12,8},{16,20},{20,16},{24,28},{28,24},{1,5},{5... | collective-permute-start | bytes 4128776 | tf_op jit(solution)/shard_map/ppermute | solution.py:717
  76.9 13.3 %collective-permute-start.12 = (bf16[256,512]{1,0:T(8,128)(2,1)S(1)}, bf16[256,512]{1,0:T(8,128)(2,1)S(1)}, u32[]{:S(2)}, u32[]{:S(2)}) collective-permute-start(bf16[256,512]{1,0:T(8,128)(2,1)S(1)} %copy-done.1), channel_id=1, source_target_pairs={{0,1},{1,0},{2,3},{3,2},{4,5},{5,4},{6,7},{7,6},{8,9},{9,8},{10,11... | collective-permute-start | bytes 786440 | tf_op jit(solution)/shard_map/ppermute | solution.py:717
  90.2 1.2 copy-start.27
  109.5 4.6 %copy-start.21 = (f32[8,512]{1,0:T(8,128)}, f32[8,512]{1,0:T(8,128)S(1)}, u32[]{:S(2)}) copy-start(f32[8,512]{1,0:T(8,128)S(1)} %get-tuple-element.110.refs_18_) | copy-start | bytes 49156
  109.5 4.2 %collective-permute-start.17 = (bf16[4,4,16,4096]{3,2,1,0:T(8,128)(2,1)S(1)}, bf16[4,4,16,4096]{3,2,1,0:T(8,128)(2,1)S(1)}, u32[]{:S(2)}, u32[]{:S(2)}) collective-permute-start(bf16[4,4,16,4096]{3,2,1,0:T(8,128)(2,1)S(1)} %get-tuple-element.113), channel_id=1, source_target_pairs={{0,4},{4,0},{8,12},{12,8},{16,20},{20,16},{24,28},{28,24},{1,5},{5... | collective-permute-start | bytes 6291464 | tf_op jit(solution)/shard_map/ppermute | solution.py:717
  114.1 14.7 %collective-permute-start.19 = (bf16[2,4,16,2048]{3,2,1,0:T(8,128)(2,1)S(1)}, bf16[2,4,16,2048]{3,2,1,0:T(8,128)(2,1)S(1)}, u32[]{:S(2)}, u32[]{:S(2)}) collective-permute-start(bf16[2,4,16,2048]{3,2,1,0:T(8,128)(2,1)S(1)} %get-tuple-element.125), channel_id=1, source_target_pairs={{0,16},{4,20},{8,24},{12,28},{16,0},{20,4},{24,8},{28,12},{1,17},{... | collective-permute-start | bytes 1572872 | tf_op jit(solution)/shard_map/ppermute | solution.py:717
  115.6 13.7 %collective-permute-start.18 = (bf16[2,4,16,2048]{3,2,1,0:T(8,128)(2,1)S(1)}, bf16[2,4,16,2048]{3,2,1,0:T(8,128)(2,1)S(1)}, u32[]{:S(2)}, u32[]{:S(2)}) collective-permute-start(bf16[2,4,16,2048]{3,2,1,0:T(8,128)(2,1)S(1)} %get-tuple-element.114.refs_21_), channel_id=1, source_target_pairs={{0,8},{4,12},{8,0},{12,4},{16,24},{20,28},{24,16},{28,20},{1,9},{5... | collective-permute-start | bytes 1572872 | tf_op jit(solution)/shard_map/ppermute | solution.py:717
  128.8 2.4 %copy-start.13 = (bf16[4,4,16,2688]{3,2,1,0:T(8,128)(2,1)}, bf16[4,4,16,2688]{3,2,1,0:T(8,128)(2,1)S(1)}, u32[]{:S(2)}) copy-start(bf16[4,4,16,2688]{3,2,1,0:T(8,128)(2,1)S(1)} %get-tuple-element.121.keep) | copy-start | bytes 4128772
  128.9 2.4 %copy-start.15 = (f32[256,512]{1,0:T(8,128)}, f32[256,512]{1,0:T(8,128)S(1)}, u32[]{:S(2)}) copy-start(f32[256,512]{1,0:T(8,128)S(1)} %get-tuple-element.115.refs_4_.refs_2_) | copy-start | bytes 1572868
  128.9 2.4 %copy-start.19 = (bf16[512,256]{1,0:T(8,128)(2,1)}, bf16[512,256]{1,0:T(8,128)(2,1)S(1)}, u32[]{:S(2)}) copy-start(bf16[512,256]{1,0:T(8,128)(2,1)S(1)} %get-tuple-element.116.refs_3_) | copy-start | bytes 786436
  130.5 0.7 copy-start.6
  131.3 1.0 copy-start.7
  131.3 3.2 %collective-permute-start.20 = (bf16[4,4,16,2688]{3,2,1,0:T(8,128)(2,1)S(1)}, bf16[4,4,16,2688]{3,2,1,0:T(8,128)(2,1)S(1)}, u32[]{:S(2)}, u32[]{:S(2)}) collective-permute-start(bf16[4,4,16,2688]{3,2,1,0:T(8,128)(2,1)S(1)} %hold.20), channel_id=1, source_target_pairs={{0,4},{4,0},{8,12},{12,8},{16,20},{20,16},{24,28},{28,24},{1,5},{5... | collective-permute-start | bytes 4128776 | tf_op jit(solution)/shard_map/ppermute | solution.py:717
  131.4 67.8 %reduce-scatter.3.cloned.1.call-start = ((), (), s32[]{:S(2)}) async-start(), calls=%async_computation.3 | async-start | bytes 1310720 | tf_op jit(solution)/shard_map/reduce_scatter | solution.py:1149
  132.2 16.8 %collective-permute-start.21 = (bf16[4,16,2048]{2,1,0:T(8,128)(2,1)S(1)}, bf16[4,16,2048]{2,1,0:T(8,128)(2,1)S(1)}, u32[]{:S(2)}, u32[]{:S(2)}) collective-permute-start(bf16[4,16,2048]{2,1,0:T(8,128)(2,1)S(1)} %copy-done.7), channel_id=1, source_target_pairs={{0,16},{4,20},{8,24},{12,28},{16,0},{20,4},{24,8},{28,12},{1,17},{... | collective-permute-start | bytes 786440 | tf_op jit(solution)/shard_map/ppermute | solution.py:717
  133.7 15.3 %collective-permute-start.22 = (bf16[4,16,2048]{2,1,0:T(8,128)(2,1)S(1)}, bf16[4,16,2048]{2,1,0:T(8,128)(2,1)S(1)}, u32[]{:S(2)}, u32[]{:S(2)}) collective-permute-start(bf16[4,16,2048]{2,1,0:T(8,128)(2,1)S(1)} %get-tuple-element.135), channel_id=1, source_target_pairs={{0,8},{4,12},{8,0},{12,4},{16,24},{20,28},{24,16},{28,20},{1,9},{5... | collective-permute-start | bytes 786440 | tf_op jit(solution)/shard_map/ppermute | solution.py:717
  134.5 1.4 copy-start.14
  135.9 2.6 %copy-start.16 = (f32[256,512]{1,0:T(8,128)S(1)}, f32[256,512]{1,0:T(8,128)}, u32[]{:S(2)}) copy-start(f32[256,512]{1,0:T(8,128)} %copy-done.15) | copy-start | bytes 1572868
  136.3 14.1 %collective-permute-start.23 = (bf16[2,4,16,1280]{3,2,1,0:T(8,128)(2,1)S(1)}, bf16[2,4,16,1280]{3,2,1,0:T(8,128)(2,1)S(1)}, u32[]{:S(2)}, u32[]{:S(2)}) collective-permute-start(bf16[2,4,16,1280]{3,2,1,0:T(8,128)(2,1)S(1)} %get-tuple-element.127.refs_11_), channel_id=1, source_target_pairs={{0,8},{4,12},{8,0},{12,4},{16,24},{20,28},{24,16},{28,20},{1,9},{5... | collective-permute-start | bytes 983048 | tf_op jit(solution)/shard_map/ppermute | solution.py:717
  137.9 12.4 %collective-permute-start.24 = (bf16[2,4,16,1408]{3,2,1,0:T(8,128)(2,1)S(1)}, bf16[2,4,16,1408]{3,2,1,0:T(8,128)(2,1)S(1)}, u32[]{:S(2)}, u32[]{:S(2)}) collective-permute-start(bf16[2,4,16,1408]{3,2,1,0:T(8,128)(2,1)S(1)} %get-tuple-element.139), channel_id=1, source_target_pairs={{0,16},{4,20},{8,24},{12,28},{16,0},{20,4},{24,8},{28,12},{1,17},{... | collective-permute-start | bytes 1081352 | tf_op jit(solution)/shard_map/ppermute | solution.py:717
  138.5 1.0 copy-start.20
  154.0 0.9 copy-start.17
  155.0 3.9 %collective-permute-start.25 = (bf16[4,4,16,1536]{3,2,1,0:T(8,128)(2,1)S(1)}, bf16[4,4,16,1536]{3,2,1,0:T(8,128)(2,1)S(1)}, u32[]{:S(2)}, u32[]{:S(2)}) collective-permute-start(bf16[4,4,16,1536]{3,2,1,0:T(8,128)(2,1)S(1)} %get-tuple-element.142), channel_id=1, source_target_pairs={{0,4},{4,0},{8,12},{12,8},{16,20},{20,16},{24,28},{28,24},{1,5},{5... | collective-permute-start | bytes 2359304 | tf_op jit(solution)/shard_map/ppermute | solution.py:717
  155.0 14.8 %collective-permute-start.36 = (bf16[2,16,4096]{2,1,0:T(8,128)(2,1)S(1)}, bf16[2,16,4096]{2,1,0:T(8,128)(2,1)S(1)}, u32[]{:S(2)}, u32[]{:S(2)}) collective-permute-start(bf16[2,16,4096]{2,1,0:T(8,128)(2,1)S(1)} %get-tuple-element.157), channel_id=1, source_target_pairs={{0,1},{1,0},{2,3},{3,2},{4,5},{5,4},{6,7},{7,6},{8,9},{9,8},{10,11... | collective-permute-start | bytes 786440 | tf_op jit(solution)/shard_map/ppermute | solution.py:717
  155.0 8.2 %collective-permute-start.32 = (bf16[4,16,1280]{2,1,0:T(8,128)(2,1)S(1)}, bf16[4,16,1280]{2,1,0:T(8,128)(2,1)S(1)}, u32[]{:S(2)}, u32[]{:S(2)}) collective-permute-start(bf16[4,16,1280]{2,1,0:T(8,128)(2,1)S(1)} %get-tuple-element.140.refs_8_), channel_id=1, source_target_pairs={{0,16},{4,20},{8,24},{12,28},{16,0},{20,4},{24,8},{28,12},{1,17},{... | collective-permute-start | bytes 491528 | tf_op jit(solution)/shard_map/ppermute | solution.py:717
  156.5 6.7 %collective-permute-start.33 = (bf16[4,16,1408]{2,1,0:T(8,128)(2,1)S(1)}, bf16[4,16,1408]{2,1,0:T(8,128)(2,1)S(1)}, u32[]{:S(2)}, u32[]{:S(2)}) collective-permute-start(bf16[4,16,1408]{2,1,0:T(8,128)(2,1)S(1)} %get-tuple-element.153), channel_id=1, source_target_pairs={{0,8},{4,12},{8,0},{12,4},{16,24},{20,28},{24,16},{28,20},{1,9},{5... | collective-permute-start | bytes 540680 | tf_op jit(solution)/shard_map/ppermute | solution.py:717
  158.8 1.1 copy-start.18
  163.2 13.1 %copy-start.3 = (bf16[4,16,1536]{2,1,0:T(8,128)(2,1)S(1)}, bf16[4,16,1536]{2,1,0:T(8,128)(2,1)}, u32[]{:S(2)}) copy-start(bf16[4,16,1536]{2,1,0:T(8,128)(2,1)} %copy-done.2) | copy-start | bytes 589828
  164.5 16.9 %collective-permute-start.34 = (bf16[2,16,2688]{2,1,0:T(8,128)(2,1)S(1)}, bf16[2,16,2688]{2,1,0:T(8,128)(2,1)S(1)}, u32[]{:S(2)}, u32[]{:S(2)}) collective-permute-start(bf16[2,16,2688]{2,1,0:T(8,128)(2,1)S(1)} %get-tuple-element.155), channel_id=1, source_target_pairs={{0,1},{1,0},{2,3},{3,2},{4,5},{5,4},{6,7},{7,6},{8,9},{9,8},{10,11... | collective-permute-start | bytes 516104 | tf_op jit(solution)/shard_map/ppermute | solution.py:717
  166.3 7.6 %collective-permute-start.26 = (bf16[4,16,1536]{2,1,0:T(8,128)(2,1)S(1)}, bf16[4,16,1536]{2,1,0:T(8,128)(2,1)S(1)}, u32[]{:S(2)}, u32[]{:S(2)}) collective-permute-start(bf16[4,16,1536]{2,1,0:T(8,128)(2,1)S(1)} %get-tuple-element.144), channel_id=1, source_target_pairs={{0,8},{4,12},{8,0},{12,4},{16,24},{20,28},{24,16},{28,20},{1,9},{5... | collective-permute-start | bytes 589832 | tf_op jit(solution)/shard_map/ppermute | solution.py:717
  166.6 9.7 %collective-permute-start.27 = (bf16[4,16,1536]{2,1,0:T(8,128)(2,1)S(1)}, bf16[4,16,1536]{2,1,0:T(8,128)(2,1)S(1)}, u32[]{:S(2)}, u32[]{:S(2)}) collective-permute-start(bf16[4,16,1536]{2,1,0:T(8,128)(2,1)S(1)} %get-tuple-element.145), channel_id=1, source_target_pairs={{0,16},{4,20},{8,24},{12,28},{16,0},{20,4},{24,8},{28,12},{1,17},{... | collective-permute-start | bytes 589832 | tf_op jit(solution)/shard_map/ppermute | solution.py:717
  168.0 8.3 %collective-permute-start.28 = (bf16[4,16,1536]{2,1,0:T(8,128)(2,1)S(1)}, bf16[4,16,1536]{2,1,0:T(8,128)(2,1)S(1)}, u32[]{:S(2)}, u32[]{:S(2)}) collective-permute-start(bf16[4,16,1536]{2,1,0:T(8,128)(2,1)S(1)} %get-tuple-element.146), channel_id=1, source_target_pairs={{0,24},{4,28},{8,16},{12,20},{16,8},{20,12},{24,0},{28,4},{1,25},{... | collective-permute-start | bytes 589832 | tf_op jit(solution)/shard_map/ppermute | solution.py:717
  169.8 19.2 %collective-permute-start.37 = (bf16[16,4096]{1,0:T(8,128)(2,1)S(1)}, bf16[16,4096]{1,0:T(8,128)(2,1)S(1)}, u32[]{:S(2)}, u32[]{:S(2)}) collective-permute-start(bf16[16,4096]{1,0:T(8,128)(2,1)S(1)} %fusion), channel_id=1, source_target_pairs={{0,2},{1,3},{2,0},{3,1},{4,6},{5,7},{6,4},{7,5},{8,10},{9,11},{10,... | collective-permute-start | bytes 393224 | tf_op jit(solution)/shard_map/ppermute | solution.py:717
  177.0 22.2 %copy-start.23 = (f32[256,512]{1,0:T(8,128)S(1)}, f32[256,512]{1,0:T(8,128)}, u32[]{:S(2)}) copy-start(f32[256,512]{1,0:T(8,128)} %get-tuple-element.128) | copy-start | bytes 1572868
  177.0 12.0 %collective-permute-start.29 = (bf16[16,1536]{1,0:T(8,128)(2,1)S(1)}, bf16[16,1536]{1,0:T(8,128)(2,1)S(1)}, u32[]{:S(2)}, u32[]{:S(2)}) collective-permute-start(bf16[16,1536]{1,0:T(8,128)(2,1)S(1)} %get-tuple-element.148), channel_id=1, source_target_pairs={{0,1},{1,0},{2,3},{3,2},{4,5},{5,4},{6,7},{7,6},{8,9},{9,8},{10,11... | collective-permute-start | bytes 147464 | tf_op jit(solution)/shard_map/ppermute | solution.py:717
  177.5 16.1 %collective-permute-start.30 = (bf16[16,1536]{1,0:T(8,128)(2,1)S(1)}, bf16[16,1536]{1,0:T(8,128)(2,1)S(1)}, u32[]{:S(2)}, u32[]{:S(2)}) collective-permute-start(bf16[16,1536]{1,0:T(8,128)(2,1)S(1)} %get-tuple-element.149), channel_id=1, source_target_pairs={{0,2},{1,3},{2,0},{3,1},{4,6},{5,7},{6,4},{7,5},{8,10},{9,11},{10,... | collective-permute-start | bytes 147464 | tf_op jit(solution)/shard_map/ppermute | solution.py:717
  179.0 14.6 %collective-permute-start.31 = (bf16[16,1536]{1,0:T(8,128)(2,1)S(1)}, bf16[16,1536]{1,0:T(8,128)(2,1)S(1)}, u32[]{:S(2)}, u32[]{:S(2)}) collective-permute-start(bf16[16,1536]{1,0:T(8,128)(2,1)S(1)} %get-tuple-element.150), channel_id=1, source_target_pairs={{0,3},{1,2},{2,1},{3,0},{4,7},{5,6},{6,5},{7,4},{8,11},{9,10},{10,... | collective-permute-start | bytes 147464 | tf_op jit(solution)/shard_map/ppermute | solution.py:717
  181.4 16.3 %collective-permute-start.35 = (bf16[16,2688]{1,0:T(8,128)(2,1)S(1)}, bf16[16,2688]{1,0:T(8,128)(2,1)S(1)}, u32[]{:S(2)}, u32[]{:S(2)}) collective-permute-start(bf16[16,2688]{1,0:T(8,128)(2,1)S(1)} %fusion.2), channel_id=1, source_target_pairs={{0,2},{1,3},{2,0},{3,1},{4,6},{5,7},{6,4},{7,5},{8,10},{9,11},{10,... | collective-permute-start | bytes 258056 | tf_op jit(solution)/shard_map/ppermute | solution.py:717
  (6 other events, 4.0 us)
Sparse Core Ops, SparseCore 0:
  11.6 77.5 all-gather.1
  131.5 25.3 reduce-scatter.4
  159.3 36.1 reduce-scatter.2

commit v2 on v1

--- a/solution.py
+++ b/solution.py
@@ -261,7 +261,7 @@
         pltpu.SemaphoreType.DMA((HEADS // 2,)),
         VM((keys, feat), BF),
         VM((feat, keys), BF),
-        pltpu.SemaphoreType.DMA((2,)),
+        pltpu.SemaphoreType.DMA((3,)),
     ]
 
 
@@ -336,10 +336,12 @@
 def cross_attend_body(n_blocks, n_parts, pos, *refs):
     blocks, refs = refs[:n_blocks], refs[n_blocks:]
     near, far, refs = refs[:n_parts], refs[n_parts : 2 * n_parts], refs[2 * n_parts :]
-    (ids, kid, mixed, mixed_one) = refs[:4]
-    (vec_out, unit_out, inv_out, q_out, v_out, kt_out, mixed_out, inverse_out) = refs[4:12]
-    (unit_two_out, inv_two_out, exps_out) = refs[12:15]
-    weight, keys, slots, bias, exps, sem, values, keys_t, out_sem = refs[15:]
+    (ids, kid, mixed, mixed_one, three) = refs[:5]
+    (vec_out, unit_out, inv_out, q_out, v_out, kt_out, mixed_out, inverse_out) = refs[5:13]
+    (unit_two_out, inv_two_out, exps_out, three_out) = refs[13:17]
+    weight, keys, slots, bias, exps, sem, values, keys_t, out_sem = refs[17:]
+    ahead = pltpu.make_async_copy(three, three_out, out_sem.at[2])
+    ahead.start()
     count, feat = q_out.shape
     in_order(pos, (near, far), weight, 0)
     vec_out[...] = weight[:, 5 * feat :].astype(F32).T[:8, :]
@@ -368,9 +370,10 @@
     inv_two_out[...] = jnp.broadcast_to(inverse, inv_two_out.shape)
     for copy in copies:
         copy.wait()
-
-
-def cross_attend(pos, blocks, ids, kid, mixed, mixed_one, near, far, after):
+    ahead.wait()
+
+
+def cross_attend(pos, blocks, ids, kid, mixed, mixed_one, three, near, far, after):
     count, feat = blocks[0].shape
     keys = count * len(blocks)
     return kernel_call(
@@ -387,16 +390,17 @@
             shape(count, feat, dtype=F32),
             shape(count, 128, dtype=F32),
             shape(HEADS // 2, keys, 2 * count),
+            shape(*three.shape),
         ),
-        [WHOLE] * 4 + [APART] * 2 + [WHOLE] * 4 + [APART],
-        [SCALARS] + [WHOLE] * (len(blocks) + 2 * len(near) + 4),
+        [WHOLE] * 4 + [APART] * 2 + [WHOLE] * 4 + [APART, WHOLE],
+        [SCALARS] + [WHOLE] * (len(blocks) + 2 * len(near) + 4) + [APART],
         [VM((feat, 5 * feat + 128), BF)] + attend_scratch(keys, feat, count),
         "cross_attend",
         14 * 10**9,
         20 * 10**6,
         after,
-        held_out=(8, 9),
-    )(pos, *blocks, *near, *far, ids, kid, mixed, mixed_one)
+        held_out=(8, 9, 11),
+    )(pos, *blocks, *near, *far, ids, kid, mixed, mixed_one, three)
 
 
 def feed_body(pos, unit_in, inv_in, vec, grad_in, pad, three, *refs):
@@ -463,7 +467,7 @@
         "feed",
         6 * 10**9,
         20 * 10**6,
-        held_in=(1, 2),
+        held_in=(1, 2, 6),
         held_out=(1, 2, 3, 4),
     )(pos, unit, inverse, vec, out_grad, pad, three)
 
@@ -475,10 +479,12 @@
     (unit_in, inv_in, vec, vec_grad, mixed_one, inverse_one) = refs[7:13]
     refs = refs[13:]
     flow_out, one_t_out, keep_out, away_out, parts_out = refs[:5]
-    weight, grads, kv, query_t, exps, sem = refs[5:]
+    weight, grads, kv, query_t, exps, sem, rows_held, unit_held, late_sem = refs[5:]
     count, feat = query.shape
     for pair in range(HEADS // 2):
         fetch(exps_in, exps, sem, pair).start()
+    late = [(block, rows_held.at[d]) for d, block in enumerate(blocks)] + [(unit_in, unit_held)]
+    late = send_out(late, late_sem)
     in_order(pos, (near, far), weight, 0)
     grad_y = low(flow_in[...])
     grad_t = over_sums(dot_t(weight[:, 4 * feat : 5 * feat], grad_y), inverse_two)
@@ -488,7 +494,9 @@
     )
     grad_query = query_t[...].T
     grad_normed = flow_in[...] + dot_t(grad_query, weight[:, feat : 2 * feat])
-    unit = unit_in[...]
+    for copy in late:
+        copy.wait()
+    unit = unit_held[...]
     grad_flow, grad_gain, grad_shift = normalise_back(grad_normed, unit, inv_in[:, :1], vec[0:1, :])
     flow_out[...] = grad_flow
     grad_y = low(grad_flow)
@@ -496,7 +504,7 @@
     grads[:, :feat] = low(dot(mixed_one[...], grad_y))
     normed = low(unit * vec[0:1, :] + vec[1:2, :])
     grads[:, feat : 2 * feat] = low(dot(normed.T, grad_query))
-    turned = jnp.concatenate([block[...].T for block in blocks], axis=1)
+    turned = jnp.concatenate([rows_held[d].T for d in range(n_blocks)], axis=1)
     grads[:, 2 * feat : 4 * feat] = low(dot(turned, kv[...]))
     rows = jnp.concatenate(
         [grad_gain, grad_shift, vec_grad[2:8, :], jnp.zeros((120, feat), F32)], axis=0
@@ -532,8 +540,18 @@
         )
         + (shape(keys, feat),),
         [WHOLE] * 5,
-        [SCALARS] * 2 + [WHOLE] * (len(blocks) + 2 * len(near) + 6) + [APART] + [WHOLE] * 6,
-        [VM((feat, 5 * feat + 128), BF)] * 2 + back_scratch(keys, feat, count),
+        [SCALARS] * 2
+        + [APART] * len(blocks)
+        + [WHOLE] * (2 * len(near) + 6)
+        + [APART] * 2
+        + [WHOLE] * 5,
+        [VM((feat, 5 * feat + 128), BF)] * 2
+        + back_scratch(keys, feat, count)
+        + [
+            VM((len(blocks), count, feat), BF),
+            VM((count, feat), F32),
+            pltpu.SemaphoreType.DMA((len(blocks) + 1,)),
+        ],
         "cross_back",
         15 * 10**9,
         20 * 10**6,
@@ -1033,6 +1051,7 @@
             unit_two,
             inv_two,
             exps_two,
+            three_near,
         ) = cross_attend(
             home,
             encoder_blocks,
@@ -1040,6 +1059,7 @@
             key_rows,
             mixed,
             mixed_one,
+            all_three,
             near_two,
             far_two,
             (),
@@ -1051,7 +1071,7 @@
             vec,
             out_grad.reshape(count, feat),
             pad,
-            all_three,
+            three_near,
             near_one.shape[:3] + (2 * wide,),
         )
         after_feed = ()

time: 208 us -> 207 us (level)
  transfers between devices with their start and end apart: 41 -> 41, of which waited for: 17 -> 19; matrix products, arithmetic and copies ran while one was open for 4% -> 4% of each run, Pallas kernels for 23% -> 19%
where the time goes in v2:
time: 207 us; the launch traced here: 206 us
  waiting for transfers between devices  68.5 us (33%)
  Pallas kernels  58.8 us (28%)
  starting transfers between devices  40.9 us (20%)
  local copies, waits for them, and re-layouts  17.2 us (8%)
  between operations  14.2 us (7%)
  other arithmetic  6.25 us (3%)
    ppermute x38, waiting for transfers between devices, swap(): return lax.ppermute(block, axis_name, [(i, i ^ bits) for i in range(size)])  68.5 us
    pallas_call x18, Pallas kernels, go(): return call(*operands, *after)  58.8 us
    ppermute x38, starting transfers between devices, swap(): return lax.ppermute(block, axis_name, [(i, i ^ bits) for i in range(size)])  40.8 us
    unnamed x59, local copies, waits for them, and re-layouts  14.5 us
  transfers between devices with their start and end apart: 41, of which 19 were waited for; matrix products, arithmetic and copies ran while one was open for 4% of the time, Pallas kernels for 19%

profile of v2, /device:TPU:0, one launch (start us, length us, event | category | flops | bytes accessed | tf_op | source)
XLA Modules:
  0.0 205.9 jit_solution(17519546248206943656)
XLA Ops:
  7.2 2.3 %pack.1 = (bf16[16,4096]{1,0:T(8,128)(2,1)}, bf16[16,4224]{1,0:T(8,128)(2,1)}, bf16[272,512]{1,0:T(8,128)(2,1)}, bf16[256,512]{1,0:T(8,128)(2,1)}) custom-call(bf16[1,256,512]{2,1,0:T(8,128)(2,1)} %source.1, bf16[1,256,512]{2,1,0:T(8,128)(2,1)} %target.1, s32[1,256]{1,0:T(1,128)} %glance.1, s32[1,256]{1,0:T(1,128)} %refs_6_.5, s32[1,256]{1,0:T(1,128)} %pad.15, ...), custom_call_target="tpu_custom_call" | custom-call | flops 1000000000 | bytes 2000000 | tf_op jit(solution)/shard_map/pack/pallas_call | solution.py:308
  9.6 3.1 %collective-permute-start.3 = (bf16[272,512]{1,0:T(8,128)(2,1)}, bf16[272,512]{1,0:T(8,128)(2,1)S(1)}, u32[]{:S(2)}, u32[]{:S(2)}) collective-permute-start(bf16[272,512]{1,0:T(8,128)(2,1)} %get-tuple-element.92.refs_0_.refs_8_.refs_1_), channel_id=1, source_target_pairs={{0,1},{1,0},{2,3},{3,2},{4,5},{5,4},{6,7},{7,6},{8,9},{9,8},{10,11... | collective-permute-start | bytes 835592 | tf_op jit(solution)/shard_map/ppermute | solution.py:735
  12.7 2.5 %collective-permute-start.2 = (bf16[16,4224]{1,0:T(8,128)(2,1)}, bf16[16,4224]{1,0:T(8,128)(2,1)S(1)}, u32[]{:S(2)}, u32[]{:S(2)}) collective-permute-start(bf16[16,4224]{1,0:T(8,128)(2,1)} %get-tuple-element.91.refs_0_), channel_id=1, source_target_pairs={{0,3},{1,2},{2,1},{3,0},{4,7},{5,6},{6,5},{7,4},{8,11},{9,10},{10,... | collective-permute-start | bytes 405512 | tf_op jit(solution)/shard_map/ppermute | solution.py:735
  15.3 1.8 collective-permute-start
  17.1 1.7 collective-permute-start.7
  18.8 7.1 %collective-permute-done.2.refs_3_ = bf16[16,4224]{1,0:T(8,128)(2,1)S(1)} collective-permute-done((bf16[16,4224]{1,0:T(8,128)(2,1)}, bf16[16,4224]{1,0:T(8,128)(2,1)S(1)}, u32[]{:S(2)}, u32[]{:S(2)}) %collective-permute-start.2) | collective-permute-done | bytes 135200 | tf_op jit(solution)/shard_map/ppermute | solution.py:735
  25.9 3.6 %collective-permute-done.1.refs_2_ = bf16[16,4224]{1,0:T(8,128)(2,1)S(1)} collective-permute-done((bf16[16,4224]{1,0:T(8,128)(2,1)}, bf16[16,4224]{1,0:T(8,128)(2,1)S(1)}, u32[]{:S(2)}, u32[]{:S(2)}) %collective-permute-start.1) | collective-permute-done | bytes 135200 | tf_op jit(solution)/shard_map/ppermute | solution.py:735
  29.5 3.4 %collective-permute-done.refs_1_ = bf16[16,4224]{1,0:T(8,128)(2,1)S(1)} collective-permute-done((bf16[16,4224]{1,0:T(8,128)(2,1)}, bf16[16,4224]{1,0:T(8,128)(2,1)S(1)}, u32[]{:S(2)}, u32[]{:S(2)}) %collective-permute-start) | collective-permute-done | bytes 135200 | tf_op jit(solution)/shard_map/ppermute | solution.py:735
  32.9 0.9 copy-done.12
  34.5 2.9 %collective-permute-start.6 = (bf16[4,16,1536]{2,1,0:T(8,128)(2,1)S(1)}, bf16[4,16,1536]{2,1,0:T(8,128)(2,1)S(1)}, u32[]{:S(2)}, u32[]{:S(2)}) collective-permute-start(bf16[4,16,1536]{2,1,0:T(8,128)(2,1)S(1)} %get-tuple-element.93.refs_0_), channel_id=1, source_target_pairs={{0,24},{4,28},{8,16},{12,20},{16,8},{20,12},{24,0},{28,4},{1,25},{... | collective-permute-start | bytes 589832 | tf_op jit(solution)/shard_map/ppermute | solution.py:735
  38.0 4.3 %collective-permute-done.7.refs_4_.refs_0_ = bf16[272,512]{1,0:T(8,128)(2,1)S(1)} collective-permute-done((bf16[272,512]{1,0:T(8,128)(2,1)}, bf16[272,512]{1,0:T(8,128)(2,1)S(1)}, u32[]{:S(2)}, u32[]{:S(2)}) %collective-permute-start.7) | collective-permute-done | bytes 278560 | tf_op jit(solution)/shard_map/ppermute | solution.py:735
  42.3 0.9 collective-permute-done.5.refs_2_
  43.7 0.8 copy-done.4
  45.6 1.5 collective-permute-start.15
  47.1 1.3 collective-permute-start.14
  49.1 0.9 copy-done.22
  50.0 4.6 %collective-permute-start.11 = (bf16[256,512]{1,0:T(8,128)(2,1)}, bf16[256,512]{1,0:T(8,128)(2,1)S(1)}, u32[]{:S(2)}, u32[]{:S(2)}) collective-permute-start(bf16[256,512]{1,0:T(8,128)(2,1)} %hold.13), channel_id=1, source_target_pairs={{0,2},{1,3},{2,0},{3,1},{4,6},{5,7},{6,4},{7,5},{8,10},{9,11},{10,... | collective-permute-start | bytes 786440 | tf_op jit(solution)/shard_map/ppermute | solution.py:735
  54.7 7.4 %collective-permute-done.10.refs_3_.refs_4_ = bf16[272,512]{1,0:T(8,128)(2,1)} collective-permute-done((bf16[272,512]{1,0:T(8,128)(2,1)S(1)}, bf16[272,512]{1,0:T(8,128)(2,1)}, u32[]{:S(2)}, u32[]{:S(2)}) %collective-permute-start.10) | collective-permute-done | bytes 278560 | tf_op jit(solution)/shard_map/ppermute | solution.py:735
  62.1 8.8 %self_attend.1 = (bf16[256,512]{1,0:T(8,128)(2,1)}, bf16[1024,512]{1,0:T(8,128)(2,1)}, bf16[512,1024]{1,0:T(8,128)(2,1)}, bf16[512,256]{1,0:T(8,128)(2,1)}, f32[...) custom-call(s32[2]{0:T(128)S(1)} %pad_add_fusion.pos.refs_0_, ...), custom_call_target="tpu_custom_call" | custom-call | flops 12000000000 | bytes 20000000 | tf_op jit(solution)/shard_map/self_attend/pallas_call | solution.py:308
  71.0 4.9 %collective-permute-done.9.refs_0_ = bf16[256,512]{1,0:T(8,128)(2,1)S(1)} collective-permute-done((bf16[256,512]{1,0:T(8,128)(2,1)}, bf16[256,512]{1,0:T(8,128)(2,1)S(1)}, u32[]{:S(2)}, u32[]{:S(2)}) %collective-permute-start.9) | collective-permute-done | bytes 262176 | tf_op jit(solution)/shard_map/ppermute | solution.py:735
  76.9 13.3 %collective-permute-done.12.refs_3_.refs_5_ = bf16[256,512]{1,0:T(8,128)(2,1)S(1)} collective-permute-done((bf16[256,512]{1,0:T(8,128)(2,1)S(1)}, bf16[256,512]{1,0:T(8,128)(2,1)S(1)}, u32[]{:S(2)}, u32[]{:S(2)}) %collective-permute-start.12) | collective-permute-done | bytes 262176 | tf_op jit(solution)/shard_map/ppermute | solution.py:735
  91.4 10.1 %cross_attend.1 = (f32[8,512]{1,0:T(8,128)}, f32[256,512]{1,0:T(8,128)}, f32[256,128]{1,0:T(8,128)}, bf16[256,512]{1,0:T(8,128)(2,1)}, bf16[1024,512]{1,0:T(8,12...) custom-call(s32[2]{0:T(128)S(1)} %pad_add_fusion.pos.refs_0_, ...), custom_call_target="tpu_custom_call" | custom-call | flops 14000000000 | bytes 20000000 | tf_op jit(solution)/shard_map/cross_attend/pallas_call | solution.py:308
  101.5 6.6 %feed.1 = (bf16[256,512]{1,0:T(8,128)(2,1)}, f32[256,512]{1,0:T(8,128)S(1)}, f32[8,512]{1,0:T(8,128)S(1)}, bf16[4,4,16,4096]{3,2,1,0:T(8,128)(2,1)S(1)}, bf16[4,4,16,4096]{3,2,1,0:T(8,128)(2,1)S(1)}) custom-call(s32[2]{0:T(128)S(1)} %pad_add_fusion.pos.refs_0_, f32[256,512]{1,0:T(8,128)S(1)} %get-tuple-element.98.unit_in, ...), custom_call_target="tpu_custom_call" | custom-call | flops 6000000000 | bytes 20000000 | tf_op jit(solution)/shard_map/feed/pallas_call | solution.py:308
  108.1 4.2 %collective-permute-done.17.away = bf16[4,4,16,4096]{3,2,1,0:T(8,128)(2,1)S(1)} collective-permute-done((bf16[4,4,16,4096]{3,2,1,0:T(8,128)(2,1)S(1)}, bf16[4,4,16,4096]{3,2,1,0:T(8,128)(2,1)S(1)}, u32[]{:S(2)}, u32[]{:S(2)}) %collective-permute-start.17) | collective-permute-done | bytes 2097184 | tf_op jit(solution)/shard_map/ppermute | solution.py:735
  112.7 1.5 collective-permute-start.19
  114.2 12.8 %cross_back.1 = (f32[256,512]{1,0:T(8,128)S(1)}, bf16[512,256]{1,0:T(8,128)(2,1)S(1)}, bf16[4,4,16,2688]{3,2,1,0:T(8,128)(2,1)S(1)}, bf16[4,4,16,2688]{3,2,1,0:T(8,128)(2,1)S(1)}, bf16[1024,512]{1,0:T(8,128)(2,1)}) custom-call(s32[2]{0:T(128)S(1)} %pad_add_fusion.pos.refs_0_, s32[1]{0:T(128)} %bitcast.1.refs_1_, ...), custom_call_target="tpu_custom_call" | custom-call | flops 15000000512 | bytes 20000000 | tf_op jit(solution)/shard_map/cross_back/pallas_call | solution.py:308
  127.1 0.8 collective-permute-done.18.refs_1_
  127.9 1.1 add_mid.2
  129.1 0.7 copy-done.6
  130.0 0.8 copy-done.7
  130.8 1.2 collective-permute-start.21
  131.9 0.9 collective-permute-start.22
  133.0 1.4 copy-done.14
  134.7 1.4 collective-permute-start.23
  136.8 0.9 copy-done.20
  137.8 9.5 %self_back.1 = (f32[256,512]{1,0:T(8,128)}, bf16[512,256]{1,0:T(8,128)(2,1)S(1)}, bf16[1024,1024]{1,0:T(8,128)(2,1)S(1)}, bf16[1024,512]{1,0:T(8,128)(2,1)}) custom-call(s32[2]{0:T(128)S(1)} %pad_add_fusion.pos.refs_0_, s32[1]{0:T(128)} %bitcast.1.refs_1_, f32[256,512]{1,0:T(8,128)S(1)} %copy-done.16, bf16[512,256]{1,0:T(8,128)(2,1)S(1)} %copy-done.20, ...), custom_call_target="tpu_custom_call" | custom-call | flops 12000000000 | bytes 20000000 | tf_op jit(solution)/shard_map/self_back/pallas_call | solution.py:308
  147.4 1.3 add_near.2
  148.7 0.9 add_mid.3
  149.6 2.7 %self_grads.1 = (bf16[4,4,16,1536]{3,2,1,0:T(8,128)(2,1)S(1)}, bf16[4,4,16,1536]{3,2,1,0:T(8,128)(2,1)S(1)}) custom-call(s32[2]{0:T(128)S(1)} %pad_add_fusion.pos.refs_0_, bf16[272,512]{1,0:T(8,128)(2,1)} %get-tuple-element.92.refs_0_.refs_8_.refs_1_, bf16[272,512]{1,0:T(8,128)(2,1)} %copy-done.11, bf16[272,512]{1,0:T(8,128)(2,1)} %copy-done.5, ...), custom_call_target="tpu_custom_call" | custom-call | flops 5000000000 | bytes 8000000 | tf_op jit(solution)/shard_map/self_grads/pallas_call | solution.py:308
  152.3 0.9 copy-done.17
  153.2 1.4 collective-permute-start.36
  154.6 1.2 collective-permute-start.32
  155.8 1.1 collective-permute-start.33
  157.0 1.8 bitcast_convert_fusion
  158.8 1.1 copy-done.18
  160.8 1.5 collective-permute-done.33.refs_0_
  162.3 1.2 add_near.3
  163.5 0.9 collective-permute-start.34
  164.3 0.7 collective-permute-start.26
  165.1 1.1 collective-permute-start.27
  166.2 1.6 collective-permute-start.28
  167.9 1.4 collective-permute-start.37
  169.3 2.8 %collective-permute-done.26.first = bf16[4,16,1536]{2,1,0:T(8,128)(2,1)S(1)} collective-permute-done((bf16[4,16,1536]{2,1,0:T(8,128)(2,1)S(1)}, bf16[4,16,1536]{2,1,0:T(8,128)(2,1)S(1)}, u32[]{:S(2)}, u32[]{:S(2)}) %collective-permute-start.26) | collective-permute-done | bytes 196640 | tf_op jit(solution)/shard_map/ppermute | solution.py:735
  172.1 2.6 %collective-permute-done.27.second = bf16[4,16,1536]{2,1,0:T(8,128)(2,1)S(1)} collective-permute-done((bf16[4,16,1536]{2,1,0:T(8,128)(2,1)S(1)}, bf16[4,16,1536]{2,1,0:T(8,128)(2,1)S(1)}, u32[]{:S(2)}, u32[]{:S(2)}) %collective-permute-start.27) | collective-permute-done | bytes 196640 | tf_op jit(solution)/shard_map/ppermute | solution.py:735
  175.3 1.6 collective-permute-start.29
  177.5 2.3 %collective-permute-start.31 = (bf16[16,1536]{1,0:T(8,128)(2,1)S(1)}, bf16[16,1536]{1,0:T(8,128)(2,1)S(1)}, u32[]{:S(2)}, u32[]{:S(2)}) collective-permute-start(bf16[16,1536]{1,0:T(8,128)(2,1)S(1)} %get-tuple-element.152), channel_id=1, source_target_pairs={{0,3},{1,2},{2,1},{3,0},{4,7},{5,6},{6,5},{7,4},{8,11},{9,10},{10,... | collective-permute-start | bytes 147464 | tf_op jit(solution)/shard_map/ppermute | solution.py:735
  179.7 1.3 collective-permute-done.34.refs_0_
  181.1 5.8 %collective-permute-done.37.refs_0_ = bf16[16,4096]{1,0:T(8,128)(2,1)S(1)} collective-permute-done((bf16[16,4096]{1,0:T(8,128)(2,1)S(1)}, bf16[16,4096]{1,0:T(8,128)(2,1)S(1)}, u32[]{:S(2)}, u32[]{:S(2)}) %collective-permute-start.37) | collective-permute-done | bytes 131104 | tf_op jit(solution)/shard_map/ppermute | solution.py:735
  188.2 0.9 fusion.1
  189.8 2.1 %collective-permute-done.30 = bf16[16,1536]{1,0:T(8,128)(2,1)S(1)} collective-permute-done((bf16[16,1536]{1,0:T(8,128)(2,1)S(1)}, bf16[16,1536]{1,0:T(8,128)(2,1)S(1)}, u32[]{:S(2)}, u32[]{:S(2)}) %collective-permute-start.30) | collective-permute-done | bytes 49184 | tf_op jit(solution)/shard_map/ppermute | solution.py:735
  191.9 0.9 convert_add_fusion.4
  194.0 2.0 collective-permute-done.35
  196.1 0.8 slice_reduce_fusion
  197.6 1.8 add_bitcast_fusion
  (126 shorter events, 14.2 us)
Async XLA Ops:
  7.2 83.0 %all-gather.2.cloned.1.call-start = ((), (), s32[]{:S(2)}) async-start(), calls=%async_computation.2 | async-start | bytes 4325376 | tf_op jit(solution)/shard_map/all_gather | solution.py:1001
  9.6 147.4 %reduce-scatter.5.cloned.1.call-start = ((), (), s32[]{:S(2)}) async-start(), calls=%async_computation.4 | async-start | bytes 1310720 | tf_op jit(solution)/shard_map/reduce_scatter | solution.py:1106
  9.6 23.2 %collective-permute-start.3 = (bf16[272,512]{1,0:T(8,128)(2,1)}, bf16[272,512]{1,0:T(8,128)(2,1)S(1)}, u32[]{:S(2)}, u32[]{:S(2)}) collective-permute-start(bf16[272,512]{1,0:T(8,128)(2,1)} %get-tuple-element.92.refs_0_.refs_8_.refs_1_), channel_id=1, source_target_pairs={{0,1},{1,0},{2,3},{3,2},{4,5},{5,4},{6,7},{7,6},{8,9},{9,8},{10,11... | collective-permute-start | bytes 835592 | tf_op jit(solution)/shard_map/ppermute | solution.py:735
  12.7 13.2 %collective-permute-start.2 = (bf16[16,4224]{1,0:T(8,128)(2,1)}, bf16[16,4224]{1,0:T(8,128)(2,1)S(1)}, u32[]{:S(2)}, u32[]{:S(2)}) collective-permute-start(bf16[16,4224]{1,0:T(8,128)(2,1)} %get-tuple-element.91.refs_0_), channel_id=1, source_target_pairs={{0,3},{1,2},{2,1},{3,0},{4,7},{5,6},{6,5},{7,4},{8,11},{9,10},{10,... | collective-permute-start | bytes 405512 | tf_op jit(solution)/shard_map/ppermute | solution.py:735
  15.2 14.3 %collective-permute-start.1 = (bf16[16,4224]{1,0:T(8,128)(2,1)}, bf16[16,4224]{1,0:T(8,128)(2,1)S(1)}, u32[]{:S(2)}, u32[]{:S(2)}) collective-permute-start(bf16[16,4224]{1,0:T(8,128)(2,1)} %get-tuple-element.91.refs_0_), channel_id=1, source_target_pairs={{0,2},{1,3},{2,0},{3,1},{4,6},{5,7},{6,4},{7,5},{8,10},{9,11},{10,... | collective-permute-start | bytes 405512 | tf_op jit(solution)/shard_map/ppermute | solution.py:735
  15.3 17.6 %collective-permute-start = (bf16[16,4224]{1,0:T(8,128)(2,1)}, bf16[16,4224]{1,0:T(8,128)(2,1)S(1)}, u32[]{:S(2)}, u32[]{:S(2)}) collective-permute-start(bf16[16,4224]{1,0:T(8,128)(2,1)} %get-tuple-element.91.refs_0_), channel_id=1, source_target_pairs={{0,1},{1,0},{2,3},{3,2},{4,5},{5,4},{6,7},{7,6},{8,9},{9,8},{10,11... | collective-permute-start | bytes 405512 | tf_op jit(solution)/shard_map/ppermute | solution.py:735
  17.1 25.2 %collective-permute-start.7 = (bf16[272,512]{1,0:T(8,128)(2,1)}, bf16[272,512]{1,0:T(8,128)(2,1)S(1)}, u32[]{:S(2)}, u32[]{:S(2)}) collective-permute-start(bf16[272,512]{1,0:T(8,128)(2,1)} %get-tuple-element.92.refs_0_.refs_8_.refs_1_), channel_id=1, source_target_pairs={{0,2},{1,3},{2,0},{3,1},{4,6},{5,7},{6,4},{7,5},{8,10},{9,11},{10,... | collective-permute-start | bytes 835592 | tf_op jit(solution)/shard_map/ppermute | solution.py:735
  32.9 0.9 copy-start.12
  33.8 0.7 copy-start.11
  34.5 10.4 %copy-start.25 = (bf16[256,512]{1,0:T(8,128)(2,1)S(1)}, bf16[256,512]{1,0:T(8,128)(2,1)}, u32[]{:S(2)}) copy-start(bf16[256,512]{1,0:T(8,128)(2,1)} %get-tuple-element.90.refs_0_.refs_2_) | copy-start | bytes 786436
  34.5 7.8 %collective-permute-start.6 = (bf16[4,16,1536]{2,1,0:T(8,128)(2,1)S(1)}, bf16[4,16,1536]{2,1,0:T(8,128)(2,1)S(1)}, u32[]{:S(2)}, u32[]{:S(2)}) collective-permute-start(bf16[4,16,1536]{2,1,0:T(8,128)(2,1)S(1)} %get-tuple-element.93.refs_0_), channel_id=1, source_target_pairs={{0,24},{4,28},{8,16},{12,20},{16,8},{20,12},{24,0},{28,4},{1,25},{... | collective-permute-start | bytes 589832 | tf_op jit(solution)/shard_map/ppermute | solution.py:735
  37.4 5.8 %collective-permute-start.5 = (bf16[4,16,1536]{2,1,0:T(8,128)(2,1)S(1)}, bf16[4,16,1536]{2,1,0:T(8,128)(2,1)S(1)}, u32[]{:S(2)}, u32[]{:S(2)}) collective-permute-start(bf16[4,16,1536]{2,1,0:T(8,128)(2,1)S(1)} %get-tuple-element.93.refs_0_), channel_id=1, source_target_pairs={{0,16},{4,20},{8,24},{12,28},{16,0},{20,4},{24,8},{28,12},{1,17},{... | collective-permute-start | bytes 589832 | tf_op jit(solution)/shard_map/ppermute | solution.py:735
  37.8 5.8 %collective-permute-start.4 = (bf16[4,16,1536]{2,1,0:T(8,128)(2,1)S(1)}, bf16[4,16,1536]{2,1,0:T(8,128)(2,1)S(1)}, u32[]{:S(2)}, u32[]{:S(2)}) collective-permute-start(bf16[4,16,1536]{2,1,0:T(8,128)(2,1)S(1)} %get-tuple-element.93.refs_0_), channel_id=1, source_target_pairs={{0,8},{4,12},{8,0},{12,4},{16,24},{20,28},{24,16},{28,20},{1,9},{5... | collective-permute-start | bytes 589832 | tf_op jit(solution)/shard_map/ppermute | solution.py:735
  43.7 0.9 copy-start.4
  43.7 5.5 %collective-permute-start.8 = (bf16[4,4,16,1536]{3,2,1,0:T(8,128)(2,1)S(1)}, bf16[4,4,16,1536]{3,2,1,0:T(8,128)(2,1)S(1)}, u32[]{:S(2)}, u32[]{:S(2)}) collective-permute-start(bf16[4,4,16,1536]{3,2,1,0:T(8,128)(2,1)S(1)} %join.2.refs_1_.refs_4_.refs_9_), channel_id=1, source_target_pairs={{0,4},{4,0},{8,12},{12,8},{16,20},{20,16},{24,28},{28,24},{1,5},{5... | collective-permute-start | bytes 2359304 | tf_op jit(solution)/shard_map/ppermute | solution.py:735
  44.5 17.5 %copy-start.5 = (bf16[272,512]{1,0:T(8,128)(2,1)}, bf16[272,512]{1,0:T(8,128)(2,1)S(1)}, u32[]{:S(2)}) copy-start(bf16[272,512]{1,0:T(8,128)(2,1)S(1)} %hold.14.refs_2_.refs_3_) | copy-start | bytes 835588
  44.5 17.5 %collective-permute-start.10 = (bf16[272,512]{1,0:T(8,128)(2,1)S(1)}, bf16[272,512]{1,0:T(8,128)(2,1)}, u32[]{:S(2)}, u32[]{:S(2)}) collective-permute-start(bf16[272,512]{1,0:T(8,128)(2,1)S(1)} %hold.14.refs_2_.refs_3_), channel_id=1, source_target_pairs={{0,1},{1,0},{2,3},{3,2},{4,5},{5,4},{6,7},{7,6},{8,9},{9,8},{10,11... | collective-permute-start | bytes 835592 | tf_op jit(solution)/shard_map/ppermute | solution.py:735
  45.6 30.2 %collective-permute-start.15 = (bf16[4,16,2688]{2,1,0:T(8,128)(2,1)S(1)}, bf16[4,16,2688]{2,1,0:T(8,128)(2,1)S(1)}, u32[]{:S(2)}, u32[]{:S(2)}) collective-permute-start(bf16[4,16,2688]{2,1,0:T(8,128)(2,1)S(1)} %get-tuple-element.95.refs_0_), channel_id=1, source_target_pairs={{0,24},{4,28},{8,16},{12,20},{16,8},{20,12},{24,0},{28,4},{1,25},{... | collective-permute-start | bytes 1032200 | tf_op jit(solution)/shard_map/ppermute | solution.py:735
  47.1 28.8 %collective-permute-start.14 = (bf16[4,16,2688]{2,1,0:T(8,128)(2,1)S(1)}, bf16[4,16,2688]{2,1,0:T(8,128)(2,1)S(1)}, u32[]{:S(2)}, u32[]{:S(2)}) collective-permute-start(bf16[4,16,2688]{2,1,0:T(8,128)(2,1)S(1)} %get-tuple-element.95.refs_0_), channel_id=1, source_target_pairs={{0,16},{4,20},{8,24},{12,28},{16,0},{20,4},{24,8},{28,12},{1,17},{... | collective-permute-start | bytes 1032200 | tf_op jit(solution)/shard_map/ppermute | solution.py:735
  48.5 27.5 %collective-permute-start.13 = (bf16[4,16,2688]{2,1,0:T(8,128)(2,1)S(1)}, bf16[4,16,2688]{2,1,0:T(8,128)(2,1)S(1)}, u32[]{:S(2)}, u32[]{:S(2)}) collective-permute-start(bf16[4,16,2688]{2,1,0:T(8,128)(2,1)S(1)} %get-tuple-element.95.refs_0_), channel_id=1, source_target_pairs={{0,8},{4,12},{8,0},{12,4},{16,24},{20,28},{24,16},{28,20},{1,9},{5... | collective-permute-start | bytes 1032200 | tf_op jit(solution)/shard_map/ppermute | solution.py:735
  49.1 0.9 copy-start.22
  50.0 20.9 %collective-permute-start.11 = (bf16[256,512]{1,0:T(8,128)(2,1)}, bf16[256,512]{1,0:T(8,128)(2,1)S(1)}, u32[]{:S(2)}, u32[]{:S(2)}) collective-permute-start(bf16[256,512]{1,0:T(8,128)(2,1)} %hold.13), channel_id=1, source_target_pairs={{0,2},{1,3},{2,0},{3,1},{4,6},{5,7},{6,4},{7,5},{8,10},{9,11},{10,... | collective-permute-start | bytes 786440 | tf_op jit(solution)/shard_map/ppermute | solution.py:735
  62.1 13.8 %collective-permute-start.9 = (bf16[256,512]{1,0:T(8,128)(2,1)}, bf16[256,512]{1,0:T(8,128)(2,1)S(1)}, u32[]{:S(2)}, u32[]{:S(2)}) collective-permute-start(bf16[256,512]{1,0:T(8,128)(2,1)} %hold.13), channel_id=1, source_target_pairs={{0,1},{1,0},{2,3},{3,2},{4,5},{5,4},{6,7},{7,6},{8,9},{9,8},{10,11... | collective-permute-start | bytes 786440 | tf_op jit(solution)/shard_map/ppermute | solution.py:735
  71.0 4.9 %copy-start = (bf16[256,512]{1,0:T(8,128)(2,1)}, bf16[256,512]{1,0:T(8,128)(2,1)S(1)}, u32[]{:S(2)}) copy-start(bf16[256,512]{1,0:T(8,128)(2,1)S(1)} %hold.16.refs_1_.refs_2_.refs_4_) | copy-start | bytes 786436
  75.9 1.0 copy-start.1
  76.6 13.6 %copy-start.10 = (bf16[4,4,16,2688]{3,2,1,0:T(8,128)(2,1)}, bf16[4,4,16,2688]{3,2,1,0:T(8,128)(2,1)S(1)}, u32[]{:S(2)}) copy-start(bf16[4,4,16,2688]{3,2,1,0:T(8,128)(2,1)S(1)} %join.3.refs_4_.refs_6_) | copy-start | bytes 4128772
  76.6 13.6 %collective-permute-start.16 = (bf16[4,4,16,2688]{3,2,1,0:T(8,128)(2,1)S(1)}, bf16[4,4,16,2688]{3,2,1,0:T(8,128)(2,1)S(1)}, u32[]{:S(2)}, u32[]{:S(2)}) collective-permute-start(bf16[4,4,16,2688]{3,2,1,0:T(8,128)(2,1)S(1)} %join.3.refs_4_.refs_6_), channel_id=1, source_target_pairs={{0,4},{4,0},{8,12},{12,8},{16,20},{20,16},{24,28},{28,24},{1,5},{5... | collective-permute-start | bytes 4128776 | tf_op jit(solution)/shard_map/ppermute | solution.py:735
  76.9 13.3 %collective-permute-start.12 = (bf16[256,512]{1,0:T(8,128)(2,1)S(1)}, bf16[256,512]{1,0:T(8,128)(2,1)S(1)}, u32[]{:S(2)}, u32[]{:S(2)}) collective-permute-start(bf16[256,512]{1,0:T(8,128)(2,1)S(1)} %copy-done.1), channel_id=1, source_target_pairs={{0,1},{1,0},{2,3},{3,2},{4,5},{5,4},{6,7},{7,6},{8,9},{9,8},{10,11... | collective-permute-start | bytes 786440 | tf_op jit(solution)/shard_map/ppermute | solution.py:735
  90.2 1.2 copy-start.27
  108.1 4.6 %copy-start.21 = (f32[8,512]{1,0:T(8,128)}, f32[8,512]{1,0:T(8,128)S(1)}, u32[]{:S(2)}) copy-start(f32[8,512]{1,0:T(8,128)S(1)} %get-tuple-element.112.refs_18_) | copy-start | bytes 49156
  108.1 4.2 %collective-permute-start.17 = (bf16[4,4,16,4096]{3,2,1,0:T(8,128)(2,1)S(1)}, bf16[4,4,16,4096]{3,2,1,0:T(8,128)(2,1)S(1)}, u32[]{:S(2)}, u32[]{:S(2)}) collective-permute-start(bf16[4,4,16,4096]{3,2,1,0:T(8,128)(2,1)S(1)} %get-tuple-element.115), channel_id=1, source_target_pairs={{0,4},{4,0},{8,12},{12,8},{16,20},{20,16},{24,28},{28,24},{1,5},{5... | collective-permute-start | bytes 6291464 | tf_op jit(solution)/shard_map/ppermute | solution.py:735
  112.7 14.3 %collective-permute-start.19 = (bf16[2,4,16,2048]{3,2,1,0:T(8,128)(2,1)S(1)}, bf16[2,4,16,2048]{3,2,1,0:T(8,128)(2,1)S(1)}, u32[]{:S(2)}, u32[]{:S(2)}) collective-permute-start(bf16[2,4,16,2048]{3,2,1,0:T(8,128)(2,1)S(1)} %get-tuple-element.127), channel_id=1, source_target_pairs={{0,16},{4,20},{8,24},{12,28},{16,0},{20,4},{24,8},{28,12},{1,17},{... | collective-permute-start | bytes 1572872 | tf_op jit(solution)/shard_map/ppermute | solution.py:735
  114.2 13.7 %collective-permute-start.18 = (bf16[2,4,16,2048]{3,2,1,0:T(8,128)(2,1)S(1)}, bf16[2,4,16,2048]{3,2,1,0:T(8,128)(2,1)S(1)}, u32[]{:S(2)}, u32[]{:S(2)}) collective-permute-start(bf16[2,4,16,2048]{3,2,1,0:T(8,128)(2,1)S(1)} %get-tuple-element.116.refs_21_), channel_id=1, source_target_pairs={{0,8},{4,12},{8,0},{12,4},{16,24},{20,28},{24,16},{28,20},{1,9},{5... | collective-permute-start | bytes 1572872 | tf_op jit(solution)/shard_map/ppermute | solution.py:735
  127.0 2.8 %copy-start.13 = (bf16[4,4,16,2688]{3,2,1,0:T(8,128)(2,1)}, bf16[4,4,16,2688]{3,2,1,0:T(8,128)(2,1)S(1)}, u32[]{:S(2)}) copy-start(bf16[4,4,16,2688]{3,2,1,0:T(8,128)(2,1)S(1)} %get-tuple-element.123.keep) | copy-start | bytes 4128772
  127.0 2.8 %copy-start.15 = (f32[256,512]{1,0:T(8,128)}, f32[256,512]{1,0:T(8,128)S(1)}, u32[]{:S(2)}) copy-start(f32[256,512]{1,0:T(8,128)S(1)} %get-tuple-element.117.refs_4_.refs_2_) | copy-start | bytes 1572868
  127.1 2.7 %copy-start.19 = (bf16[512,256]{1,0:T(8,128)(2,1)}, bf16[512,256]{1,0:T(8,128)(2,1)S(1)}, u32[]{:S(2)}) copy-start(bf16[512,256]{1,0:T(8,128)(2,1)S(1)} %get-tuple-element.118.refs_3_) | copy-start | bytes 786436
  129.1 0.7 copy-start.6
  129.8 1.0 copy-start.7
  129.8 3.2 %collective-permute-start.20 = (bf16[4,4,16,2688]{3,2,1,0:T(8,128)(2,1)S(1)}, bf16[4,4,16,2688]{3,2,1,0:T(8,128)(2,1)S(1)}, u32[]{:S(2)}, u32[]{:S(2)}) collective-permute-start(bf16[4,4,16,2688]{3,2,1,0:T(8,128)(2,1)S(1)} %hold.20), channel_id=1, source_target_pairs={{0,4},{4,0},{8,12},{12,8},{16,20},{20,16},{24,28},{28,24},{1,5},{5... | collective-permute-start | bytes 4128776 | tf_op jit(solution)/shard_map/ppermute | solution.py:735
  129.9 67.6 %reduce-scatter.3.cloned.1.call-start = ((), (), s32[]{:S(2)}) async-start(), calls=%async_computation.3 | async-start | bytes 1310720 | tf_op jit(solution)/shard_map/reduce_scatter | solution.py:1169
  130.8 16.6 %collective-permute-start.21 = (bf16[4,16,2048]{2,1,0:T(8,128)(2,1)S(1)}, bf16[4,16,2048]{2,1,0:T(8,128)(2,1)S(1)}, u32[]{:S(2)}, u32[]{:S(2)}) collective-permute-start(bf16[4,16,2048]{2,1,0:T(8,128)(2,1)S(1)} %copy-done.7), channel_id=1, source_target_pairs={{0,16},{4,20},{8,24},{12,28},{16,0},{20,4},{24,8},{28,12},{1,17},{... | collective-permute-start | bytes 786440 | tf_op jit(solution)/shard_map/ppermute | solution.py:735
  131.9 15.4 %collective-permute-start.22 = (bf16[4,16,2048]{2,1,0:T(8,128)(2,1)S(1)}, bf16[4,16,2048]{2,1,0:T(8,128)(2,1)S(1)}, u32[]{:S(2)}, u32[]{:S(2)}) collective-permute-start(bf16[4,16,2048]{2,1,0:T(8,128)(2,1)S(1)} %get-tuple-element.137), channel_id=1, source_target_pairs={{0,8},{4,12},{8,0},{12,4},{16,24},{20,28},{24,16},{28,20},{1,9},{5... | collective-permute-start | bytes 786440 | tf_op jit(solution)/shard_map/ppermute | solution.py:735
  133.0 1.4 copy-start.14
  134.4 2.4 %copy-start.16 = (f32[256,512]{1,0:T(8,128)S(1)}, f32[256,512]{1,0:T(8,128)}, u32[]{:S(2)}) copy-start(f32[256,512]{1,0:T(8,128)} %copy-done.15) | copy-start | bytes 1572868
  134.7 13.9 %collective-permute-start.23 = (bf16[2,4,16,1280]{3,2,1,0:T(8,128)(2,1)S(1)}, bf16[2,4,16,1280]{3,2,1,0:T(8,128)(2,1)S(1)}, u32[]{:S(2)}, u32[]{:S(2)}) collective-permute-start(bf16[2,4,16,1280]{3,2,1,0:T(8,128)(2,1)S(1)} %get-tuple-element.129.refs_11_), channel_id=1, source_target_pairs={{0,8},{4,12},{8,0},{12,4},{16,24},{20,28},{24,16},{28,20},{1,9},{5... | collective-permute-start | bytes 983048 | tf_op jit(solution)/shard_map/ppermute | solution.py:735
  136.1 12.5 %collective-permute-start.24 = (bf16[2,4,16,1408]{3,2,1,0:T(8,128)(2,1)S(1)}, bf16[2,4,16,1408]{3,2,1,0:T(8,128)(2,1)S(1)}, u32[]{:S(2)}, u32[]{:S(2)}) collective-permute-start(bf16[2,4,16,1408]{3,2,1,0:T(8,128)(2,1)S(1)} %get-tuple-element.141), channel_id=1, source_target_pairs={{0,16},{4,20},{8,24},{12,28},{16,0},{20,4},{24,8},{28,12},{1,17},{... | collective-permute-start | bytes 1081352 | tf_op jit(solution)/shard_map/ppermute | solution.py:735
  136.8 1.0 copy-start.20
  152.3 0.9 copy-start.17
  153.2 5.5 %collective-permute-start.25 = (bf16[4,4,16,1536]{3,2,1,0:T(8,128)(2,1)S(1)}, bf16[4,4,16,1536]{3,2,1,0:T(8,128)(2,1)S(1)}, u32[]{:S(2)}, u32[]{:S(2)}) collective-permute-start(bf16[4,4,16,1536]{3,2,1,0:T(8,128)(2,1)S(1)} %get-tuple-element.144), channel_id=1, source_target_pairs={{0,4},{4,0},{8,12},{12,8},{16,20},{20,16},{24,28},{28,24},{1,5},{5... | collective-permute-start | bytes 2359304 | tf_op jit(solution)/shard_map/ppermute | solution.py:735
  153.2 14.6 %collective-permute-start.36 = (bf16[2,16,4096]{2,1,0:T(8,128)(2,1)S(1)}, bf16[2,16,4096]{2,1,0:T(8,128)(2,1)S(1)}, u32[]{:S(2)}, u32[]{:S(2)}) collective-permute-start(bf16[2,16,4096]{2,1,0:T(8,128)(2,1)S(1)} %get-tuple-element.159), channel_id=1, source_target_pairs={{0,1},{1,0},{2,3},{3,2},{4,5},{5,4},{6,7},{7,6},{8,9},{9,8},{10,11... | collective-permute-start | bytes 786440 | tf_op jit(solution)/shard_map/ppermute | solution.py:735
  154.6 7.6 %collective-permute-start.32 = (bf16[4,16,1280]{2,1,0:T(8,128)(2,1)S(1)}, bf16[4,16,1280]{2,1,0:T(8,128)(2,1)S(1)}, u32[]{:S(2)}, u32[]{:S(2)}) collective-permute-start(bf16[4,16,1280]{2,1,0:T(8,128)(2,1)S(1)} %get-tuple-element.142.refs_8_), channel_id=1, source_target_pairs={{0,16},{4,20},{8,24},{12,28},{16,0},{20,4},{24,8},{28,12},{1,17},{... | collective-permute-start | bytes 491528 | tf_op jit(solution)/shard_map/ppermute | solution.py:735
  155.8 6.4 %collective-permute-start.33 = (bf16[4,16,1408]{2,1,0:T(8,128)(2,1)S(1)}, bf16[4,16,1408]{2,1,0:T(8,128)(2,1)S(1)}, u32[]{:S(2)}, u32[]{:S(2)}) collective-permute-start(bf16[4,16,1408]{2,1,0:T(8,128)(2,1)S(1)} %get-tuple-element.155), channel_id=1, source_target_pairs={{0,8},{4,12},{8,0},{12,4},{16,24},{20,28},{24,16},{28,20},{1,9},{5... | collective-permute-start | bytes 540680 | tf_op jit(solution)/shard_map/ppermute | solution.py:735
  158.8 1.1 copy-start.18
  162.3 12.4 %copy-start.3 = (bf16[4,16,1536]{2,1,0:T(8,128)(2,1)S(1)}, bf16[4,16,1536]{2,1,0:T(8,128)(2,1)}, u32[]{:S(2)}) copy-start(bf16[4,16,1536]{2,1,0:T(8,128)(2,1)} %copy-done.2) | copy-start | bytes 589828
  163.5 17.5 %collective-permute-start.34 = (bf16[2,16,2688]{2,1,0:T(8,128)(2,1)S(1)}, bf16[2,16,2688]{2,1,0:T(8,128)(2,1)S(1)}, u32[]{:S(2)}, u32[]{:S(2)}) collective-permute-start(bf16[2,16,2688]{2,1,0:T(8,128)(2,1)S(1)} %get-tuple-element.157), channel_id=1, source_target_pairs={{0,1},{1,0},{2,3},{3,2},{4,5},{5,4},{6,7},{7,6},{8,9},{9,8},{10,11... | collective-permute-start | bytes 516104 | tf_op jit(solution)/shard_map/ppermute | solution.py:735
  164.3 7.7 %collective-permute-start.26 = (bf16[4,16,1536]{2,1,0:T(8,128)(2,1)S(1)}, bf16[4,16,1536]{2,1,0:T(8,128)(2,1)S(1)}, u32[]{:S(2)}, u32[]{:S(2)}) collective-permute-start(bf16[4,16,1536]{2,1,0:T(8,128)(2,1)S(1)} %get-tuple-element.146), channel_id=1, source_target_pairs={{0,8},{4,12},{8,0},{12,4},{16,24},{20,28},{24,16},{28,20},{1,9},{5... | collective-permute-start | bytes 589832 | tf_op jit(solution)/shard_map/ppermute | solution.py:735
  165.1 9.5 %collective-permute-start.27 = (bf16[4,16,1536]{2,1,0:T(8,128)(2,1)S(1)}, bf16[4,16,1536]{2,1,0:T(8,128)(2,1)S(1)}, u32[]{:S(2)}, u32[]{:S(2)}) collective-permute-start(bf16[4,16,1536]{2,1,0:T(8,128)(2,1)S(1)} %get-tuple-element.147), channel_id=1, source_target_pairs={{0,16},{4,20},{8,24},{12,28},{16,0},{20,4},{24,8},{28,12},{1,17},{... | collective-permute-start | bytes 589832 | tf_op jit(solution)/shard_map/ppermute | solution.py:735
  166.2 8.4 %collective-permute-start.28 = (bf16[4,16,1536]{2,1,0:T(8,128)(2,1)S(1)}, bf16[4,16,1536]{2,1,0:T(8,128)(2,1)S(1)}, u32[]{:S(2)}, u32[]{:S(2)}) collective-permute-start(bf16[4,16,1536]{2,1,0:T(8,128)(2,1)S(1)} %get-tuple-element.148), channel_id=1, source_target_pairs={{0,24},{4,28},{8,16},{12,20},{16,8},{20,12},{24,0},{28,4},{1,25},{... | collective-permute-start | bytes 589832 | tf_op jit(solution)/shard_map/ppermute | solution.py:735
  167.9 19.0 %collective-permute-start.37 = (bf16[16,4096]{1,0:T(8,128)(2,1)S(1)}, bf16[16,4096]{1,0:T(8,128)(2,1)S(1)}, u32[]{:S(2)}, u32[]{:S(2)}) collective-permute-start(bf16[16,4096]{1,0:T(8,128)(2,1)S(1)} %fusion), channel_id=1, source_target_pairs={{0,2},{1,3},{2,0},{3,1},{4,6},{5,7},{6,4},{7,5},{8,10},{9,11},{10,... | collective-permute-start | bytes 393224 | tf_op jit(solution)/shard_map/ppermute | solution.py:735
  175.3 22.2 %copy-start.23 = (f32[256,512]{1,0:T(8,128)S(1)}, f32[256,512]{1,0:T(8,128)}, u32[]{:S(2)}) copy-start(f32[256,512]{1,0:T(8,128)} %get-tuple-element.130) | copy-start | bytes 1572868
  175.3 11.5 %collective-permute-start.29 = (bf16[16,1536]{1,0:T(8,128)(2,1)S(1)}, bf16[16,1536]{1,0:T(8,128)(2,1)S(1)}, u32[]{:S(2)}, u32[]{:S(2)}) collective-permute-start(bf16[16,1536]{1,0:T(8,128)(2,1)S(1)} %get-tuple-element.150), channel_id=1, source_target_pairs={{0,1},{1,0},{2,3},{3,2},{4,5},{5,4},{6,7},{7,6},{8,9},{9,8},{10,11... | collective-permute-start | bytes 147464 | tf_op jit(solution)/shard_map/ppermute | solution.py:735
  176.9 14.9 %collective-permute-start.30 = (bf16[16,1536]{1,0:T(8,128)(2,1)S(1)}, bf16[16,1536]{1,0:T(8,128)(2,1)S(1)}, u32[]{:S(2)}, u32[]{:S(2)}) collective-permute-start(bf16[16,1536]{1,0:T(8,128)(2,1)S(1)} %get-tuple-element.151), channel_id=1, source_target_pairs={{0,2},{1,3},{2,0},{3,1},{4,6},{5,7},{6,4},{7,5},{8,10},{9,11},{10,... | collective-permute-start | bytes 147464 | tf_op jit(solution)/shard_map/ppermute | solution.py:735
  177.5 14.4 %collective-permute-start.31 = (bf16[16,1536]{1,0:T(8,128)(2,1)S(1)}, bf16[16,1536]{1,0:T(8,128)(2,1)S(1)}, u32[]{:S(2)}, u32[]{:S(2)}) collective-permute-start(bf16[16,1536]{1,0:T(8,128)(2,1)S(1)} %get-tuple-element.152), channel_id=1, source_target_pairs={{0,3},{1,2},{2,1},{3,0},{4,7},{5,6},{6,5},{7,4},{8,11},{9,10},{10,... | collective-permute-start | bytes 147464 | tf_op jit(solution)/shard_map/ppermute | solution.py:735
  181.0 15.0 %collective-permute-start.35 = (bf16[16,2688]{1,0:T(8,128)(2,1)S(1)}, bf16[16,2688]{1,0:T(8,128)(2,1)S(1)}, u32[]{:S(2)}, u32[]{:S(2)}) collective-permute-start(bf16[16,2688]{1,0:T(8,128)(2,1)S(1)} %fusion.2), channel_id=1, source_target_pairs={{0,2},{1,3},{2,0},{3,1},{4,6},{5,7},{6,4},{7,5},{8,10},{9,11},{10,... | collective-permute-start | bytes 258056 | tf_op jit(solution)/shard_map/ppermute | solution.py:735
  (6 other events, 4.0 us)
Sparse Core Ops, SparseCore 0:
  11.6 77.5 all-gather.1
  130.0 25.4 reduce-scatter.4
  157.9 35.9 reduce-scatter.2

commit v3 on v2

--- a/solution.py
+++ b/solution.py
@@ -479,18 +479,22 @@
     (unit_in, inv_in, vec, vec_grad, mixed_one, inverse_one) = refs[7:13]
     refs = refs[13:]
     flow_out, one_t_out, keep_out, away_out, parts_out = refs[:5]
-    weight, grads, kv, query_t, exps, sem, rows_held, unit_held, late_sem = refs[5:]
+    weight, grads, kv, query_t, exps, sem, rows_held, unit_held, late_sem, one_held, turned_held = refs[5:]
+    soon = pltpu.make_async_copy(keys_t, turned_held, late_sem.at[n_blocks + 2])
+    soon.start()
     count, feat = query.shape
     for pair in range(HEADS // 2):
         fetch(exps_in, exps, sem, pair).start()
     late = [(block, rows_held.at[d]) for d, block in enumerate(blocks)] + [(unit_in, unit_held)]
+    late.append((mixed_one, one_held))
     late = send_out(late, late_sem)
     in_order(pos, (near, far), weight, 0)
     grad_y = low(flow_in[...])
     grad_t = over_sums(dot_t(weight[:, 4 * feat : 5 * feat], grad_y), inverse_two)
     grads[:, 4 * feat : 5 * feat] = low(dot(mixed_two[...], grad_y))
+    soon.wait()
     attend_back(
-        query, keys_t, values, mixed_two, grad_t, grad_t.T, exps_in, exps, sem, query_t, kv
+        query, turned_held, values, mixed_two, grad_t, grad_t.T, exps_in, exps, sem, query_t, kv
     )
     grad_query = query_t[...].T
     grad_normed = flow_in[...] + dot_t(grad_query, weight[:, feat : 2 * feat])
@@ -501,7 +505,7 @@
     flow_out[...] = grad_flow
     grad_y = low(grad_flow)
     one_t_out[...] = over_sums(dot_t(weight[:, :feat], grad_y), inverse_one)
-    grads[:, :feat] = low(dot(mixed_one[...], grad_y))
+    grads[:, :feat] = low(dot(one_held[...], grad_y))
     normed = low(unit * vec[0:1, :] + vec[1:2, :])
     grads[:, feat : 2 * feat] = low(dot(normed.T, grad_query))
     turned = jnp.concatenate([rows_held[d].T for d in range(n_blocks)], axis=1)
@@ -542,15 +546,19 @@
         [WHOLE] * 5,
         [SCALARS] * 2
         + [APART] * len(blocks)
-        + [WHOLE] * (2 * len(near) + 6)
+        + [WHOLE] * (2 * len(near) + 4)
+        + [APART, WHOLE]
         + [APART] * 2
-        + [WHOLE] * 5,
+        + [WHOLE] * 3
+        + [APART, WHOLE],
         [VM((feat, 5 * feat + 128), BF)] * 2
         + back_scratch(keys, feat, count)
         + [
             VM((len(blocks), count, feat), BF),
             VM((count, feat), F32),
-            pltpu.SemaphoreType.DMA((len(blocks) + 1,)),
+            pltpu.SemaphoreType.DMA((len(blocks) + 3,)),
+            VM((feat, count), BF),
+            VM((feat, keys), BF),
         ],
         "cross_back",
         15 * 10**9,

time: 207 us -> 207 us (level)
  transfers between devices with their start and end apart: 41 -> 41, of which waited for: 19 -> 18; matrix products, arithmetic and copies ran while one was open for 4% -> 4% of each run, Pallas kernels for 19% -> 19%
where the time goes in v3:
time: 207 us; the launch traced here: 206 us
  waiting for transfers between devices  67.7 us (33%)
  Pallas kernels  59.2 us (29%)
  starting transfers between devices  41.5 us (20%)
  local copies, waits for them, and re-layouts  17.2 us (8%)
  between operations  14.2 us (7%)
  other arithmetic  6.26 us (3%)
    ppermute x38, waiting for transfers between devices, swap(): return lax.ppermute(block, axis_name, [(i, i ^ bits) for i in range(size)])  67.7 us
    pallas_call x18, Pallas kernels, go(): return call(*operands, *after)  59.2 us
    ppermute x38, starting transfers between devices, swap(): return lax.ppermute(block, axis_name, [(i, i ^ bits) for i in range(size)])  41.4 us
    unnamed x59, local copies, waits for them, and re-layouts  14.5 us
  transfers between devices with their start and end apart: 41, of which 18 were waited for; matrix products, arithmetic and copies ran while one was open for 4% of the time, Pallas kernels for 19%

profile of v3, /device:TPU:0, one launch (start us, length us, event | category | flops | bytes accessed | tf_op | source)
XLA Modules:
  0.0 206.2 jit_solution(16303973290650596897)
XLA Ops:
  7.2 2.3 %pack.1 = (bf16[16,4096]{1,0:T(8,128)(2,1)}, bf16[16,4224]{1,0:T(8,128)(2,1)}, bf16[272,512]{1,0:T(8,128)(2,1)}, bf16[256,512]{1,0:T(8,128)(2,1)}) custom-call(bf16[1,256,512]{2,1,0:T(8,128)(2,1)} %source.1, bf16[1,256,512]{2,1,0:T(8,128)(2,1)} %target.1, s32[1,256]{1,0:T(1,128)} %glance.1, s32[1,256]{1,0:T(1,128)} %refs_6_.5, s32[1,256]{1,0:T(1,128)} %pad.15, ...), custom_call_target="tpu_custom_call" | custom-call | flops 1000000000 | bytes 2000000 | tf_op jit(solution)/shard_map/pack/pallas_call | solution.py:308
  9.6 3.1 %collective-permute-start.3 = (bf16[272,512]{1,0:T(8,128)(2,1)}, bf16[272,512]{1,0:T(8,128)(2,1)S(1)}, u32[]{:S(2)}, u32[]{:S(2)}) collective-permute-start(bf16[272,512]{1,0:T(8,128)(2,1)} %get-tuple-element.92.refs_0_.refs_8_.refs_1_), channel_id=1, source_target_pairs={{0,1},{1,0},{2,3},{3,2},{4,5},{5,4},{6,7},{7,6},{8,9},{9,8},{10,11... | collective-permute-start | bytes 835592 | tf_op jit(solution)/shard_map/ppermute | solution.py:743
  12.7 2.5 %collective-permute-start.2 = (bf16[16,4224]{1,0:T(8,128)(2,1)}, bf16[16,4224]{1,0:T(8,128)(2,1)S(1)}, u32[]{:S(2)}, u32[]{:S(2)}) collective-permute-start(bf16[16,4224]{1,0:T(8,128)(2,1)} %get-tuple-element.91.refs_0_), channel_id=1, source_target_pairs={{0,3},{1,2},{2,1},{3,0},{4,7},{5,6},{6,5},{7,4},{8,11},{9,10},{10,... | collective-permute-start | bytes 405512 | tf_op jit(solution)/shard_map/ppermute | solution.py:743
  15.3 1.8 collective-permute-start
  17.1 1.7 collective-permute-start.7
  18.8 7.1 %collective-permute-done.2.refs_3_ = bf16[16,4224]{1,0:T(8,128)(2,1)S(1)} collective-permute-done((bf16[16,4224]{1,0:T(8,128)(2,1)}, bf16[16,4224]{1,0:T(8,128)(2,1)S(1)}, u32[]{:S(2)}, u32[]{:S(2)}) %collective-permute-start.2) | collective-permute-done | bytes 135200 | tf_op jit(solution)/shard_map/ppermute | solution.py:743
  25.9 3.6 %collective-permute-done.1.refs_2_ = bf16[16,4224]{1,0:T(8,128)(2,1)S(1)} collective-permute-done((bf16[16,4224]{1,0:T(8,128)(2,1)}, bf16[16,4224]{1,0:T(8,128)(2,1)S(1)}, u32[]{:S(2)}, u32[]{:S(2)}) %collective-permute-start.1) | collective-permute-done | bytes 135200 | tf_op jit(solution)/shard_map/ppermute | solution.py:743
  29.5 3.4 %collective-permute-done.refs_1_ = bf16[16,4224]{1,0:T(8,128)(2,1)S(1)} collective-permute-done((bf16[16,4224]{1,0:T(8,128)(2,1)}, bf16[16,4224]{1,0:T(8,128)(2,1)S(1)}, u32[]{:S(2)}, u32[]{:S(2)}) %collective-permute-start) | collective-permute-done | bytes 135200 | tf_op jit(solution)/shard_map/ppermute | solution.py:743
  32.9 0.9 copy-done.12
  33.8 0.7 copy-done.11
  34.5 2.9 %collective-permute-start.6 = (bf16[4,16,1536]{2,1,0:T(8,128)(2,1)S(1)}, bf16[4,16,1536]{2,1,0:T(8,128)(2,1)S(1)}, u32[]{:S(2)}, u32[]{:S(2)}) collective-permute-start(bf16[4,16,1536]{2,1,0:T(8,128)(2,1)S(1)} %get-tuple-element.93.refs_0_), channel_id=1, source_target_pairs={{0,24},{4,28},{8,16},{12,20},{16,8},{20,12},{24,0},{28,4},{1,25},{... | collective-permute-start | bytes 589832 | tf_op jit(solution)/shard_map/ppermute | solution.py:743
  38.0 4.3 %collective-permute-done.7.refs_4_.refs_0_ = bf16[272,512]{1,0:T(8,128)(2,1)S(1)} collective-permute-done((bf16[272,512]{1,0:T(8,128)(2,1)}, bf16[272,512]{1,0:T(8,128)(2,1)S(1)}, u32[]{:S(2)}, u32[]{:S(2)}) %collective-permute-start.7) | collective-permute-done | bytes 278560 | tf_op jit(solution)/shard_map/ppermute | solution.py:743
  42.3 0.9 collective-permute-done.5.refs_2_
  43.7 0.8 copy-done.4
  44.9 0.7 copy.55.refs_0_
  45.6 1.5 collective-permute-start.15
  47.1 1.3 collective-permute-start.14
  49.1 0.9 copy-done.22
  50.0 4.6 %collective-permute-start.11 = (bf16[256,512]{1,0:T(8,128)(2,1)}, bf16[256,512]{1,0:T(8,128)(2,1)S(1)}, u32[]{:S(2)}, u32[]{:S(2)}) collective-permute-start(bf16[256,512]{1,0:T(8,128)(2,1)} %hold.13), channel_id=1, source_target_pairs={{0,2},{1,3},{2,0},{3,1},{4,6},{5,7},{6,4},{7,5},{8,10},{9,11},{10,... | collective-permute-start | bytes 786440 | tf_op jit(solution)/shard_map/ppermute | solution.py:743
  54.7 7.4 %collective-permute-done.10.refs_3_.refs_4_ = bf16[272,512]{1,0:T(8,128)(2,1)} collective-permute-done((bf16[272,512]{1,0:T(8,128)(2,1)S(1)}, bf16[272,512]{1,0:T(8,128)(2,1)}, u32[]{:S(2)}, u32[]{:S(2)}) %collective-permute-start.10) | collective-permute-done | bytes 278560 | tf_op jit(solution)/shard_map/ppermute | solution.py:743
  62.1 8.8 %self_attend.1 = (bf16[256,512]{1,0:T(8,128)(2,1)}, bf16[1024,512]{1,0:T(8,128)(2,1)}, bf16[512,1024]{1,0:T(8,128)(2,1)}, bf16[512,256]{1,0:T(8,128)(2,1)}, f32[...) custom-call(s32[2]{0:T(128)S(1)} %pad_add_fusion.pos.refs_0_, ...), custom_call_target="tpu_custom_call" | custom-call | flops 12000000000 | bytes 20000000 | tf_op jit(solution)/shard_map/self_attend/pallas_call | solution.py:308
  71.0 4.9 %collective-permute-done.9.refs_0_ = bf16[256,512]{1,0:T(8,128)(2,1)S(1)} collective-permute-done((bf16[256,512]{1,0:T(8,128)(2,1)}, bf16[256,512]{1,0:T(8,128)(2,1)S(1)}, u32[]{:S(2)}, u32[]{:S(2)}) %collective-permute-start.9) | collective-permute-done | bytes 262176 | tf_op jit(solution)/shard_map/ppermute | solution.py:743
  76.9 13.3 %collective-permute-done.12.refs_3_.refs_5_ = bf16[256,512]{1,0:T(8,128)(2,1)S(1)} collective-permute-done((bf16[256,512]{1,0:T(8,128)(2,1)S(1)}, bf16[256,512]{1,0:T(8,128)(2,1)S(1)}, u32[]{:S(2)}, u32[]{:S(2)}) %collective-permute-start.12) | collective-permute-done | bytes 262176 | tf_op jit(solution)/shard_map/ppermute | solution.py:743
  91.4 10.1 %cross_attend.1 = (f32[8,512]{1,0:T(8,128)}, f32[256,512]{1,0:T(8,128)}, f32[256,128]{1,0:T(8,128)}, bf16[256,512]{1,0:T(8,128)(2,1)}, bf16[1024,512]{1,0:T(8,12...) custom-call(s32[2]{0:T(128)S(1)} %pad_add_fusion.pos.refs_0_, ...), custom_call_target="tpu_custom_call" | custom-call | flops 14000000000 | bytes 20000000 | tf_op jit(solution)/shard_map/cross_attend/pallas_call | solution.py:308
  101.5 6.6 %feed.1 = (bf16[256,512]{1,0:T(8,128)(2,1)}, f32[256,512]{1,0:T(8,128)S(1)}, f32[8,512]{1,0:T(8,128)S(1)}, bf16[4,4,16,4096]{3,2,1,0:T(8,128)(2,1)S(1)}, bf16[4,4,16,4096]{3,2,1,0:T(8,128)(2,1)S(1)}) custom-call(s32[2]{0:T(128)S(1)} %pad_add_fusion.pos.refs_0_, f32[256,512]{1,0:T(8,128)S(1)} %get-tuple-element.98.unit_in, ...), custom_call_target="tpu_custom_call" | custom-call | flops 6000000000 | bytes 20000000 | tf_op jit(solution)/shard_map/feed/pallas_call | solution.py:308
  108.1 4.2 %collective-permute-done.17.away = bf16[4,4,16,4096]{3,2,1,0:T(8,128)(2,1)S(1)} collective-permute-done((bf16[4,4,16,4096]{3,2,1,0:T(8,128)(2,1)S(1)}, bf16[4,4,16,4096]{3,2,1,0:T(8,128)(2,1)S(1)}, u32[]{:S(2)}, u32[]{:S(2)}) %collective-permute-start.17) | collective-permute-done | bytes 2097184 | tf_op jit(solution)/shard_map/ppermute | solution.py:743
  112.7 1.5 collective-permute-start.19
  114.2 13.2 %cross_back.1 = (f32[256,512]{1,0:T(8,128)S(1)}, bf16[512,256]{1,0:T(8,128)(2,1)S(1)}, bf16[4,4,16,2688]{3,2,1,0:T(8,128)(2,1)S(1)}, bf16[4,4,16,2688]{3,2,1,0:T(8,128)(2,1)S(1)}, bf16[1024,512]{1,0:T(8,128)(2,1)}) custom-call(s32[2]{0:T(128)S(1)} %pad_add_fusion.pos.refs_0_, s32[1]{0:T(128)} %bitcast.1.refs_1_, ...), custom_call_target="tpu_custom_call" | custom-call | flops 15000000512 | bytes 20000000 | tf_op jit(solution)/shard_map/cross_back/pallas_call | solution.py:308
  127.9 1.2 add_mid.2
  129.1 0.7 copy-done.6
  130.0 0.8 copy-done.7
  130.8 1.5 collective-permute-start.21
  132.3 0.8 collective-permute-start.22
  133.1 1.3 copy-done.14
  134.8 1.7 collective-permute-start.23
  137.1 0.9 copy-done.20
  138.1 9.5 %self_back.1 = (f32[256,512]{1,0:T(8,128)}, bf16[512,256]{1,0:T(8,128)(2,1)S(1)}, bf16[1024,1024]{1,0:T(8,128)(2,1)S(1)}, bf16[1024,512]{1,0:T(8,128)(2,1)}) custom-call(s32[2]{0:T(128)S(1)} %pad_add_fusion.pos.refs_0_, s32[1]{0:T(128)} %bitcast.1.refs_1_, f32[256,512]{1,0:T(8,128)S(1)} %copy-done.16, bf16[512,256]{1,0:T(8,128)(2,1)S(1)} %copy-done.20, ...), custom_call_target="tpu_custom_call" | custom-call | flops 12000000000 | bytes 20000000 | tf_op jit(solution)/shard_map/self_back/pallas_call | solution.py:308
  147.6 1.3 add_near.2
  149.0 0.9 add_mid.3
  149.9 2.7 %self_grads.1 = (bf16[4,4,16,1536]{3,2,1,0:T(8,128)(2,1)S(1)}, bf16[4,4,16,1536]{3,2,1,0:T(8,128)(2,1)S(1)}) custom-call(s32[2]{0:T(128)S(1)} %pad_add_fusion.pos.refs_0_, bf16[272,512]{1,0:T(8,128)(2,1)} %get-tuple-element.92.refs_0_.refs_8_.refs_1_, bf16[272,512]{1,0:T(8,128)(2,1)} %copy-done.11, bf16[272,512]{1,0:T(8,128)(2,1)} %copy-done.5, ...), custom_call_target="tpu_custom_call" | custom-call | flops 5000000000 | bytes 8000000 | tf_op jit(solution)/shard_map/self_grads/pallas_call | solution.py:308
  152.6 0.9 copy-done.17
  153.5 1.5 collective-permute-start.36
  155.0 0.9 collective-permute-start.32
  155.9 1.4 collective-permute-start.33
  157.4 1.8 bitcast_convert_fusion
  159.2 1.1 copy-done.18
  161.2 1.2 collective-permute-done.33.refs_0_
  162.3 1.2 add_near.3
  163.6 1.2 collective-permute-start.34
  165.3 1.3 collective-permute-start.27
  166.6 1.7 collective-permute-start.28
  168.3 1.2 collective-permute-start.37
  169.4 3.0 %collective-permute-done.26.first = bf16[4,16,1536]{2,1,0:T(8,128)(2,1)S(1)} collective-permute-done((bf16[4,16,1536]{2,1,0:T(8,128)(2,1)S(1)}, bf16[4,16,1536]{2,1,0:T(8,128)(2,1)S(1)}, u32[]{:S(2)}, u32[]{:S(2)}) %collective-permute-start.26) | collective-permute-done | bytes 196640 | tf_op jit(solution)/shard_map/ppermute | solution.py:743
  172.5 2.6 %collective-permute-done.27.second = bf16[4,16,1536]{2,1,0:T(8,128)(2,1)S(1)} collective-permute-done((bf16[4,16,1536]{2,1,0:T(8,128)(2,1)S(1)}, bf16[4,16,1536]{2,1,0:T(8,128)(2,1)S(1)}, u32[]{:S(2)}, u32[]{:S(2)}) %collective-permute-start.27) | collective-permute-done | bytes 196640 | tf_op jit(solution)/shard_map/ppermute | solution.py:743
  175.8 1.5 collective-permute-start.29
  177.9 2.4 %collective-permute-start.31 = (bf16[16,1536]{1,0:T(8,128)(2,1)S(1)}, bf16[16,1536]{1,0:T(8,128)(2,1)S(1)}, u32[]{:S(2)}, u32[]{:S(2)}) collective-permute-start(bf16[16,1536]{1,0:T(8,128)(2,1)S(1)} %get-tuple-element.152), channel_id=1, source_target_pairs={{0,3},{1,2},{2,1},{3,0},{4,7},{5,6},{6,5},{7,4},{8,11},{9,10},{10,... | collective-permute-start | bytes 147464 | tf_op jit(solution)/shard_map/ppermute | solution.py:743
  180.2 1.0 collective-permute-done.34.refs_0_
  181.3 6.1 %collective-permute-done.37.refs_0_ = bf16[16,4096]{1,0:T(8,128)(2,1)S(1)} collective-permute-done((bf16[16,4096]{1,0:T(8,128)(2,1)S(1)}, bf16[16,4096]{1,0:T(8,128)(2,1)S(1)}, u32[]{:S(2)}, u32[]{:S(2)}) %collective-permute-start.37) | collective-permute-done | bytes 131104 | tf_op jit(solution)/shard_map/ppermute | solution.py:743
  188.7 0.9 fusion.1
  190.3 2.0 collective-permute-done.30
  192.3 0.9 convert_add_fusion.4
  194.5 1.8 collective-permute-done.35
  196.4 0.8 slice_reduce_fusion
  197.8 1.8 add_bitcast_fusion
  (126 shorter events, 13.5 us)
Async XLA Ops:
  7.2 83.0 %all-gather.2.cloned.1.call-start = ((), (), s32[]{:S(2)}) async-start(), calls=%async_computation.2 | async-start | bytes 4325376 | tf_op jit(solution)/shard_map/all_gather | solution.py:1009
  9.6 147.8 %reduce-scatter.5.cloned.1.call-start = ((), (), s32[]{:S(2)}) async-start(), calls=%async_computation.4 | async-start | bytes 1310720 | tf_op jit(solution)/shard_map/reduce_scatter | solution.py:1114
  9.6 23.2 %collective-permute-start.3 = (bf16[272,512]{1,0:T(8,128)(2,1)}, bf16[272,512]{1,0:T(8,128)(2,1)S(1)}, u32[]{:S(2)}, u32[]{:S(2)}) collective-permute-start(bf16[272,512]{1,0:T(8,128)(2,1)} %get-tuple-element.92.refs_0_.refs_8_.refs_1_), channel_id=1, source_target_pairs={{0,1},{1,0},{2,3},{3,2},{4,5},{5,4},{6,7},{7,6},{8,9},{9,8},{10,11... | collective-permute-start | bytes 835592 | tf_op jit(solution)/shard_map/ppermute | solution.py:743
  12.7 13.2 %collective-permute-start.2 = (bf16[16,4224]{1,0:T(8,128)(2,1)}, bf16[16,4224]{1,0:T(8,128)(2,1)S(1)}, u32[]{:S(2)}, u32[]{:S(2)}) collective-permute-start(bf16[16,4224]{1,0:T(8,128)(2,1)} %get-tuple-element.91.refs_0_), channel_id=1, source_target_pairs={{0,3},{1,2},{2,1},{3,0},{4,7},{5,6},{6,5},{7,4},{8,11},{9,10},{10,... | collective-permute-start | bytes 405512 | tf_op jit(solution)/shard_map/ppermute | solution.py:743
  15.2 14.3 %collective-permute-start.1 = (bf16[16,4224]{1,0:T(8,128)(2,1)}, bf16[16,4224]{1,0:T(8,128)(2,1)S(1)}, u32[]{:S(2)}, u32[]{:S(2)}) collective-permute-start(bf16[16,4224]{1,0:T(8,128)(2,1)} %get-tuple-element.91.refs_0_), channel_id=1, source_target_pairs={{0,2},{1,3},{2,0},{3,1},{4,6},{5,7},{6,4},{7,5},{8,10},{9,11},{10,... | collective-permute-start | bytes 405512 | tf_op jit(solution)/shard_map/ppermute | solution.py:743
  15.3 17.6 %collective-permute-start = (bf16[16,4224]{1,0:T(8,128)(2,1)}, bf16[16,4224]{1,0:T(8,128)(2,1)S(1)}, u32[]{:S(2)}, u32[]{:S(2)}) collective-permute-start(bf16[16,4224]{1,0:T(8,128)(2,1)} %get-tuple-element.91.refs_0_), channel_id=1, source_target_pairs={{0,1},{1,0},{2,3},{3,2},{4,5},{5,4},{6,7},{7,6},{8,9},{9,8},{10,11... | collective-permute-start | bytes 405512 | tf_op jit(solution)/shard_map/ppermute | solution.py:743
  17.1 25.2 %collective-permute-start.7 = (bf16[272,512]{1,0:T(8,128)(2,1)}, bf16[272,512]{1,0:T(8,128)(2,1)S(1)}, u32[]{:S(2)}, u32[]{:S(2)}) collective-permute-start(bf16[272,512]{1,0:T(8,128)(2,1)} %get-tuple-element.92.refs_0_.refs_8_.refs_1_), channel_id=1, source_target_pairs={{0,2},{1,3},{2,0},{3,1},{4,6},{5,7},{6,4},{7,5},{8,10},{9,11},{10,... | collective-permute-start | bytes 835592 | tf_op jit(solution)/shard_map/ppermute | solution.py:743
  32.9 0.9 copy-start.12
  33.8 0.7 copy-start.11
  34.5 10.4 %copy-start.25 = (bf16[256,512]{1,0:T(8,128)(2,1)S(1)}, bf16[256,512]{1,0:T(8,128)(2,1)}, u32[]{:S(2)}) copy-start(bf16[256,512]{1,0:T(8,128)(2,1)} %get-tuple-element.90.refs_0_.refs_2_) | copy-start | bytes 786436
  34.5 7.8 %collective-permute-start.6 = (bf16[4,16,1536]{2,1,0:T(8,128)(2,1)S(1)}, bf16[4,16,1536]{2,1,0:T(8,128)(2,1)S(1)}, u32[]{:S(2)}, u32[]{:S(2)}) collective-permute-start(bf16[4,16,1536]{2,1,0:T(8,128)(2,1)S(1)} %get-tuple-element.93.refs_0_), channel_id=1, source_target_pairs={{0,24},{4,28},{8,16},{12,20},{16,8},{20,12},{24,0},{28,4},{1,25},{... | collective-permute-start | bytes 589832 | tf_op jit(solution)/shard_map/ppermute | solution.py:743
  37.4 5.8 %collective-permute-start.5 = (bf16[4,16,1536]{2,1,0:T(8,128)(2,1)S(1)}, bf16[4,16,1536]{2,1,0:T(8,128)(2,1)S(1)}, u32[]{:S(2)}, u32[]{:S(2)}) collective-permute-start(bf16[4,16,1536]{2,1,0:T(8,128)(2,1)S(1)} %get-tuple-element.93.refs_0_), channel_id=1, source_target_pairs={{0,16},{4,20},{8,24},{12,28},{16,0},{20,4},{24,8},{28,12},{1,17},{... | collective-permute-start | bytes 589832 | tf_op jit(solution)/shard_map/ppermute | solution.py:743
  37.8 5.8 %collective-permute-start.4 = (bf16[4,16,1536]{2,1,0:T(8,128)(2,1)S(1)}, bf16[4,16,1536]{2,1,0:T(8,128)(2,1)S(1)}, u32[]{:S(2)}, u32[]{:S(2)}) collective-permute-start(bf16[4,16,1536]{2,1,0:T(8,128)(2,1)S(1)} %get-tuple-element.93.refs_0_), channel_id=1, source_target_pairs={{0,8},{4,12},{8,0},{12,4},{16,24},{20,28},{24,16},{28,20},{1,9},{5... | collective-permute-start | bytes 589832 | tf_op jit(solution)/shard_map/ppermute | solution.py:743
  43.7 0.9 copy-start.4
  43.7 5.5 %collective-permute-start.8 = (bf16[4,4,16,1536]{3,2,1,0:T(8,128)(2,1)S(1)}, bf16[4,4,16,1536]{3,2,1,0:T(8,128)(2,1)S(1)}, u32[]{:S(2)}, u32[]{:S(2)}) collective-permute-start(bf16[4,4,16,1536]{3,2,1,0:T(8,128)(2,1)S(1)} %join.2.refs_1_.refs_4_.refs_9_), channel_id=1, source_target_pairs={{0,4},{4,0},{8,12},{12,8},{16,20},{20,16},{24,28},{28,24},{1,5},{5... | collective-permute-start | bytes 2359304 | tf_op jit(solution)/shard_map/ppermute | solution.py:743
  44.5 17.5 %copy-start.5 = (bf16[272,512]{1,0:T(8,128)(2,1)}, bf16[272,512]{1,0:T(8,128)(2,1)S(1)}, u32[]{:S(2)}) copy-start(bf16[272,512]{1,0:T(8,128)(2,1)S(1)} %hold.14.refs_2_.refs_3_) | copy-start | bytes 835588
  44.5 17.5 %collective-permute-start.10 = (bf16[272,512]{1,0:T(8,128)(2,1)S(1)}, bf16[272,512]{1,0:T(8,128)(2,1)}, u32[]{:S(2)}, u32[]{:S(2)}) collective-permute-start(bf16[272,512]{1,0:T(8,128)(2,1)S(1)} %hold.14.refs_2_.refs_3_), channel_id=1, source_target_pairs={{0,1},{1,0},{2,3},{3,2},{4,5},{5,4},{6,7},{7,6},{8,9},{9,8},{10,11... | collective-permute-start | bytes 835592 | tf_op jit(solution)/shard_map/ppermute | solution.py:743
  45.6 30.2 %collective-permute-start.15 = (bf16[4,16,2688]{2,1,0:T(8,128)(2,1)S(1)}, bf16[4,16,2688]{2,1,0:T(8,128)(2,1)S(1)}, u32[]{:S(2)}, u32[]{:S(2)}) collective-permute-start(bf16[4,16,2688]{2,1,0:T(8,128)(2,1)S(1)} %get-tuple-element.95.refs_0_), channel_id=1, source_target_pairs={{0,24},{4,28},{8,16},{12,20},{16,8},{20,12},{24,0},{28,4},{1,25},{... | collective-permute-start | bytes 1032200 | tf_op jit(solution)/shard_map/ppermute | solution.py:743
  47.1 28.8 %collective-permute-start.14 = (bf16[4,16,2688]{2,1,0:T(8,128)(2,1)S(1)}, bf16[4,16,2688]{2,1,0:T(8,128)(2,1)S(1)}, u32[]{:S(2)}, u32[]{:S(2)}) collective-permute-start(bf16[4,16,2688]{2,1,0:T(8,128)(2,1)S(1)} %get-tuple-element.95.refs_0_), channel_id=1, source_target_pairs={{0,16},{4,20},{8,24},{12,28},{16,0},{20,4},{24,8},{28,12},{1,17},{... | collective-permute-start | bytes 1032200 | tf_op jit(solution)/shard_map/ppermute | solution.py:743
  48.5 27.5 %collective-permute-start.13 = (bf16[4,16,2688]{2,1,0:T(8,128)(2,1)S(1)}, bf16[4,16,2688]{2,1,0:T(8,128)(2,1)S(1)}, u32[]{:S(2)}, u32[]{:S(2)}) collective-permute-start(bf16[4,16,2688]{2,1,0:T(8,128)(2,1)S(1)} %get-tuple-element.95.refs_0_), channel_id=1, source_target_pairs={{0,8},{4,12},{8,0},{12,4},{16,24},{20,28},{24,16},{28,20},{1,9},{5... | collective-permute-start | bytes 1032200 | tf_op jit(solution)/shard_map/ppermute | solution.py:743
  49.1 0.9 copy-start.22
  50.0 20.9 %collective-permute-start.11 = (bf16[256,512]{1,0:T(8,128)(2,1)}, bf16[256,512]{1,0:T(8,128)(2,1)S(1)}, u32[]{:S(2)}, u32[]{:S(2)}) collective-permute-start(bf16[256,512]{1,0:T(8,128)(2,1)} %hold.13), channel_id=1, source_target_pairs={{0,2},{1,3},{2,0},{3,1},{4,6},{5,7},{6,4},{7,5},{8,10},{9,11},{10,... | collective-permute-start | bytes 786440 | tf_op jit(solution)/shard_map/ppermute | solution.py:743
  62.1 13.8 %collective-permute-start.9 = (bf16[256,512]{1,0:T(8,128)(2,1)}, bf16[256,512]{1,0:T(8,128)(2,1)S(1)}, u32[]{:S(2)}, u32[]{:S(2)}) collective-permute-start(bf16[256,512]{1,0:T(8,128)(2,1)} %hold.13), channel_id=1, source_target_pairs={{0,1},{1,0},{2,3},{3,2},{4,5},{5,4},{6,7},{7,6},{8,9},{9,8},{10,11... | collective-permute-start | bytes 786440 | tf_op jit(solution)/shard_map/ppermute | solution.py:743
  71.0 4.9 %copy-start = (bf16[256,512]{1,0:T(8,128)(2,1)}, bf16[256,512]{1,0:T(8,128)(2,1)S(1)}, u32[]{:S(2)}) copy-start(bf16[256,512]{1,0:T(8,128)(2,1)S(1)} %hold.16.refs_1_.refs_2_.refs_4_) | copy-start | bytes 786436
  75.9 1.0 copy-start.1
  76.6 13.6 %copy-start.10 = (bf16[4,4,16,2688]{3,2,1,0:T(8,128)(2,1)}, bf16[4,4,16,2688]{3,2,1,0:T(8,128)(2,1)S(1)}, u32[]{:S(2)}) copy-start(bf16[4,4,16,2688]{3,2,1,0:T(8,128)(2,1)S(1)} %join.3.refs_4_.refs_6_) | copy-start | bytes 4128772
  76.6 13.6 %collective-permute-start.16 = (bf16[4,4,16,2688]{3,2,1,0:T(8,128)(2,1)S(1)}, bf16[4,4,16,2688]{3,2,1,0:T(8,128)(2,1)S(1)}, u32[]{:S(2)}, u32[]{:S(2)}) collective-permute-start(bf16[4,4,16,2688]{3,2,1,0:T(8,128)(2,1)S(1)} %join.3.refs_4_.refs_6_), channel_id=1, source_target_pairs={{0,4},{4,0},{8,12},{12,8},{16,20},{20,16},{24,28},{28,24},{1,5},{5... | collective-permute-start | bytes 4128776 | tf_op jit(solution)/shard_map/ppermute | solution.py:743
  76.9 13.3 %collective-permute-start.12 = (bf16[256,512]{1,0:T(8,128)(2,1)S(1)}, bf16[256,512]{1,0:T(8,128)(2,1)S(1)}, u32[]{:S(2)}, u32[]{:S(2)}) collective-permute-start(bf16[256,512]{1,0:T(8,128)(2,1)S(1)} %copy-done.1), channel_id=1, source_target_pairs={{0,1},{1,0},{2,3},{3,2},{4,5},{5,4},{6,7},{7,6},{8,9},{9,8},{10,11... | collective-permute-start | bytes 786440 | tf_op jit(solution)/shard_map/ppermute | solution.py:743
  90.2 1.2 copy-start.27
  108.1 4.6 %copy-start.21 = (f32[8,512]{1,0:T(8,128)}, f32[8,512]{1,0:T(8,128)S(1)}, u32[]{:S(2)}) copy-start(f32[8,512]{1,0:T(8,128)S(1)} %get-tuple-element.112.refs_18_) | copy-start | bytes 49156
  108.1 4.2 %collective-permute-start.17 = (bf16[4,4,16,4096]{3,2,1,0:T(8,128)(2,1)S(1)}, bf16[4,4,16,4096]{3,2,1,0:T(8,128)(2,1)S(1)}, u32[]{:S(2)}, u32[]{:S(2)}) collective-permute-start(bf16[4,4,16,4096]{3,2,1,0:T(8,128)(2,1)S(1)} %get-tuple-element.115), channel_id=1, source_target_pairs={{0,4},{4,0},{8,12},{12,8},{16,20},{20,16},{24,28},{28,24},{1,5},{5... | collective-permute-start | bytes 6291464 | tf_op jit(solution)/shard_map/ppermute | solution.py:743
  112.7 14.7 %collective-permute-start.19 = (bf16[2,4,16,2048]{3,2,1,0:T(8,128)(2,1)S(1)}, bf16[2,4,16,2048]{3,2,1,0:T(8,128)(2,1)S(1)}, u32[]{:S(2)}, u32[]{:S(2)}) collective-permute-start(bf16[2,4,16,2048]{3,2,1,0:T(8,128)(2,1)S(1)} %get-tuple-element.127), channel_id=1, source_target_pairs={{0,16},{4,20},{8,24},{12,28},{16,0},{20,4},{24,8},{28,12},{1,17},{... | collective-permute-start | bytes 1572872 | tf_op jit(solution)/shard_map/ppermute | solution.py:743
  114.2 13.7 %collective-permute-start.18 = (bf16[2,4,16,2048]{3,2,1,0:T(8,128)(2,1)S(1)}, bf16[2,4,16,2048]{3,2,1,0:T(8,128)(2,1)S(1)}, u32[]{:S(2)}, u32[]{:S(2)}) collective-permute-start(bf16[2,4,16,2048]{3,2,1,0:T(8,128)(2,1)S(1)} %get-tuple-element.116.refs_21_), channel_id=1, source_target_pairs={{0,8},{4,12},{8,0},{12,4},{16,24},{20,28},{24,16},{28,20},{1,9},{5... | collective-permute-start | bytes 1572872 | tf_op jit(solution)/shard_map/ppermute | solution.py:743
  127.4 2.4 %copy-start.13 = (bf16[4,4,16,2688]{3,2,1,0:T(8,128)(2,1)}, bf16[4,4,16,2688]{3,2,1,0:T(8,128)(2,1)S(1)}, u32[]{:S(2)}) copy-start(bf16[4,4,16,2688]{3,2,1,0:T(8,128)(2,1)S(1)} %get-tuple-element.123.keep) | copy-start | bytes 4128772
  127.4 2.4 %copy-start.15 = (f32[256,512]{1,0:T(8,128)}, f32[256,512]{1,0:T(8,128)S(1)}, u32[]{:S(2)}) copy-start(f32[256,512]{1,0:T(8,128)S(1)} %get-tuple-element.117.refs_4_.refs_2_) | copy-start | bytes 1572868
  127.4 2.4 %copy-start.19 = (bf16[512,256]{1,0:T(8,128)(2,1)}, bf16[512,256]{1,0:T(8,128)(2,1)S(1)}, u32[]{:S(2)}) copy-start(bf16[512,256]{1,0:T(8,128)(2,1)S(1)} %get-tuple-element.118.refs_3_) | copy-start | bytes 786436
  129.1 0.7 copy-start.6
  129.9 1.0 copy-start.7
  129.9 3.2 %collective-permute-start.20 = (bf16[4,4,16,2688]{3,2,1,0:T(8,128)(2,1)S(1)}, bf16[4,4,16,2688]{3,2,1,0:T(8,128)(2,1)S(1)}, u32[]{:S(2)}, u32[]{:S(2)}) collective-permute-start(bf16[4,4,16,2688]{3,2,1,0:T(8,128)(2,1)S(1)} %hold.20), channel_id=1, source_target_pairs={{0,4},{4,0},{8,12},{12,8},{16,20},{20,16},{24,28},{28,24},{1,5},{5... | collective-permute-start | bytes 4128776 | tf_op jit(solution)/shard_map/ppermute | solution.py:743
  130.0 67.8 %reduce-scatter.3.cloned.1.call-start = ((), (), s32[]{:S(2)}) async-start(), calls=%async_computation.3 | async-start | bytes 1310720 | tf_op jit(solution)/shard_map/reduce_scatter | solution.py:1177
  130.8 16.8 %collective-permute-start.21 = (bf16[4,16,2048]{2,1,0:T(8,128)(2,1)S(1)}, bf16[4,16,2048]{2,1,0:T(8,128)(2,1)S(1)}, u32[]{:S(2)}, u32[]{:S(2)}) collective-permute-start(bf16[4,16,2048]{2,1,0:T(8,128)(2,1)S(1)} %copy-done.7), channel_id=1, source_target_pairs={{0,16},{4,20},{8,24},{12,28},{16,0},{20,4},{24,8},{28,12},{1,17},{... | collective-permute-start | bytes 786440 | tf_op jit(solution)/shard_map/ppermute | solution.py:743
  132.3 15.3 %collective-permute-start.22 = (bf16[4,16,2048]{2,1,0:T(8,128)(2,1)S(1)}, bf16[4,16,2048]{2,1,0:T(8,128)(2,1)S(1)}, u32[]{:S(2)}, u32[]{:S(2)}) collective-permute-start(bf16[4,16,2048]{2,1,0:T(8,128)(2,1)S(1)} %get-tuple-element.137), channel_id=1, source_target_pairs={{0,8},{4,12},{8,0},{12,4},{16,24},{20,28},{24,16},{28,20},{1,9},{5... | collective-permute-start | bytes 786440 | tf_op jit(solution)/shard_map/ppermute | solution.py:743
  133.1 1.3 copy-start.14
  134.4 2.7 %copy-start.16 = (f32[256,512]{1,0:T(8,128)S(1)}, f32[256,512]{1,0:T(8,128)}, u32[]{:S(2)}) copy-start(f32[256,512]{1,0:T(8,128)} %copy-done.15) | copy-start | bytes 1572868
  134.8 14.1 %collective-permute-start.23 = (bf16[2,4,16,1280]{3,2,1,0:T(8,128)(2,1)S(1)}, bf16[2,4,16,1280]{3,2,1,0:T(8,128)(2,1)S(1)}, u32[]{:S(2)}, u32[]{:S(2)}) collective-permute-start(bf16[2,4,16,1280]{3,2,1,0:T(8,128)(2,1)S(1)} %get-tuple-element.129.refs_11_), channel_id=1, source_target_pairs={{0,8},{4,12},{8,0},{12,4},{16,24},{20,28},{24,16},{28,20},{1,9},{5... | collective-permute-start | bytes 983048 | tf_op jit(solution)/shard_map/ppermute | solution.py:743
  136.5 12.4 %collective-permute-start.24 = (bf16[2,4,16,1408]{3,2,1,0:T(8,128)(2,1)S(1)}, bf16[2,4,16,1408]{3,2,1,0:T(8,128)(2,1)S(1)}, u32[]{:S(2)}, u32[]{:S(2)}) collective-permute-start(bf16[2,4,16,1408]{3,2,1,0:T(8,128)(2,1)S(1)} %get-tuple-element.141), channel_id=1, source_target_pairs={{0,16},{4,20},{8,24},{12,28},{16,0},{20,4},{24,8},{28,12},{1,17},{... | collective-permute-start | bytes 1081352 | tf_op jit(solution)/shard_map/ppermute | solution.py:743
  137.1 1.0 copy-start.20
  152.6 0.9 copy-start.17
  153.5 5.6 %collective-permute-start.25 = (bf16[4,4,16,1536]{3,2,1,0:T(8,128)(2,1)S(1)}, bf16[4,4,16,1536]{3,2,1,0:T(8,128)(2,1)S(1)}, u32[]{:S(2)}, u32[]{:S(2)}) collective-permute-start(bf16[4,4,16,1536]{3,2,1,0:T(8,128)(2,1)S(1)} %get-tuple-element.144), channel_id=1, source_target_pairs={{0,4},{4,0},{8,12},{12,8},{16,20},{20,16},{24,28},{28,24},{1,5},{5... | collective-permute-start | bytes 2359304 | tf_op jit(solution)/shard_map/ppermute | solution.py:743
  153.5 14.7 %collective-permute-start.36 = (bf16[2,16,4096]{2,1,0:T(8,128)(2,1)S(1)}, bf16[2,16,4096]{2,1,0:T(8,128)(2,1)S(1)}, u32[]{:S(2)}, u32[]{:S(2)}) collective-permute-start(bf16[2,16,4096]{2,1,0:T(8,128)(2,1)S(1)} %get-tuple-element.159), channel_id=1, source_target_pairs={{0,1},{1,0},{2,3},{3,2},{4,5},{5,4},{6,7},{7,6},{8,9},{9,8},{10,11... | collective-permute-start | bytes 786440 | tf_op jit(solution)/shard_map/ppermute | solution.py:743
  155.0 7.3 %collective-permute-start.32 = (bf16[4,16,1280]{2,1,0:T(8,128)(2,1)S(1)}, bf16[4,16,1280]{2,1,0:T(8,128)(2,1)S(1)}, u32[]{:S(2)}, u32[]{:S(2)}) collective-permute-start(bf16[4,16,1280]{2,1,0:T(8,128)(2,1)S(1)} %get-tuple-element.142.refs_8_), channel_id=1, source_target_pairs={{0,16},{4,20},{8,24},{12,28},{16,0},{20,4},{24,8},{28,12},{1,17},{... | collective-permute-start | bytes 491528 | tf_op jit(solution)/shard_map/ppermute | solution.py:743
  155.9 6.4 %collective-permute-start.33 = (bf16[4,16,1408]{2,1,0:T(8,128)(2,1)S(1)}, bf16[4,16,1408]{2,1,0:T(8,128)(2,1)S(1)}, u32[]{:S(2)}, u32[]{:S(2)}) collective-permute-start(bf16[4,16,1408]{2,1,0:T(8,128)(2,1)S(1)} %get-tuple-element.155), channel_id=1, source_target_pairs={{0,8},{4,12},{8,0},{12,4},{16,24},{20,28},{24,16},{28,20},{1,9},{5... | collective-permute-start | bytes 540680 | tf_op jit(solution)/shard_map/ppermute | solution.py:743
  159.2 1.1 copy-start.18
  162.3 12.8 %copy-start.3 = (bf16[4,16,1536]{2,1,0:T(8,128)(2,1)S(1)}, bf16[4,16,1536]{2,1,0:T(8,128)(2,1)}, u32[]{:S(2)}) copy-start(bf16[4,16,1536]{2,1,0:T(8,128)(2,1)} %copy-done.2) | copy-start | bytes 589828
  163.6 17.6 %collective-permute-start.34 = (bf16[2,16,2688]{2,1,0:T(8,128)(2,1)S(1)}, bf16[2,16,2688]{2,1,0:T(8,128)(2,1)S(1)}, u32[]{:S(2)}, u32[]{:S(2)}) collective-permute-start(bf16[2,16,2688]{2,1,0:T(8,128)(2,1)S(1)} %get-tuple-element.157), channel_id=1, source_target_pairs={{0,1},{1,0},{2,3},{3,2},{4,5},{5,4},{6,7},{7,6},{8,9},{9,8},{10,11... | collective-permute-start | bytes 516104 | tf_op jit(solution)/shard_map/ppermute | solution.py:743
  164.8 7.7 %collective-permute-start.26 = (bf16[4,16,1536]{2,1,0:T(8,128)(2,1)S(1)}, bf16[4,16,1536]{2,1,0:T(8,128)(2,1)S(1)}, u32[]{:S(2)}, u32[]{:S(2)}) collective-permute-start(bf16[4,16,1536]{2,1,0:T(8,128)(2,1)S(1)} %get-tuple-element.146), channel_id=1, source_target_pairs={{0,8},{4,12},{8,0},{12,4},{16,24},{20,28},{24,16},{28,20},{1,9},{5... | collective-permute-start | bytes 589832 | tf_op jit(solution)/shard_map/ppermute | solution.py:743
  165.3 9.8 %collective-permute-start.27 = (bf16[4,16,1536]{2,1,0:T(8,128)(2,1)S(1)}, bf16[4,16,1536]{2,1,0:T(8,128)(2,1)S(1)}, u32[]{:S(2)}, u32[]{:S(2)}) collective-permute-start(bf16[4,16,1536]{2,1,0:T(8,128)(2,1)S(1)} %get-tuple-element.147), channel_id=1, source_target_pairs={{0,16},{4,20},{8,24},{12,28},{16,0},{20,4},{24,8},{28,12},{1,17},{... | collective-permute-start | bytes 589832 | tf_op jit(solution)/shard_map/ppermute | solution.py:743
  166.6 8.5 %collective-permute-start.28 = (bf16[4,16,1536]{2,1,0:T(8,128)(2,1)S(1)}, bf16[4,16,1536]{2,1,0:T(8,128)(2,1)S(1)}, u32[]{:S(2)}, u32[]{:S(2)}) collective-permute-start(bf16[4,16,1536]{2,1,0:T(8,128)(2,1)S(1)} %get-tuple-element.148), channel_id=1, source_target_pairs={{0,24},{4,28},{8,16},{12,20},{16,8},{20,12},{24,0},{28,4},{1,25},{... | collective-permute-start | bytes 589832 | tf_op jit(solution)/shard_map/ppermute | solution.py:743
  168.3 19.1 %collective-permute-start.37 = (bf16[16,4096]{1,0:T(8,128)(2,1)S(1)}, bf16[16,4096]{1,0:T(8,128)(2,1)S(1)}, u32[]{:S(2)}, u32[]{:S(2)}) collective-permute-start(bf16[16,4096]{1,0:T(8,128)(2,1)S(1)} %fusion), channel_id=1, source_target_pairs={{0,2},{1,3},{2,0},{3,1},{4,6},{5,7},{6,4},{7,5},{8,10},{9,11},{10,... | collective-permute-start | bytes 393224 | tf_op jit(solution)/shard_map/ppermute | solution.py:743
  175.8 22.0 %copy-start.23 = (f32[256,512]{1,0:T(8,128)S(1)}, f32[256,512]{1,0:T(8,128)}, u32[]{:S(2)}) copy-start(f32[256,512]{1,0:T(8,128)} %get-tuple-element.130) | copy-start | bytes 1572868
  175.8 11.6 %collective-permute-start.29 = (bf16[16,1536]{1,0:T(8,128)(2,1)S(1)}, bf16[16,1536]{1,0:T(8,128)(2,1)S(1)}, u32[]{:S(2)}, u32[]{:S(2)}) collective-permute-start(bf16[16,1536]{1,0:T(8,128)(2,1)S(1)} %get-tuple-element.150), channel_id=1, source_target_pairs={{0,1},{1,0},{2,3},{3,2},{4,5},{5,4},{6,7},{7,6},{8,9},{9,8},{10,11... | collective-permute-start | bytes 147464 | tf_op jit(solution)/shard_map/ppermute | solution.py:743
  177.3 15.0 %collective-permute-start.30 = (bf16[16,1536]{1,0:T(8,128)(2,1)S(1)}, bf16[16,1536]{1,0:T(8,128)(2,1)S(1)}, u32[]{:S(2)}, u32[]{:S(2)}) collective-permute-start(bf16[16,1536]{1,0:T(8,128)(2,1)S(1)} %get-tuple-element.151), channel_id=1, source_target_pairs={{0,2},{1,3},{2,0},{3,1},{4,6},{5,7},{6,4},{7,5},{8,10},{9,11},{10,... | collective-permute-start | bytes 147464 | tf_op jit(solution)/shard_map/ppermute | solution.py:743
  177.9 14.4 %collective-permute-start.31 = (bf16[16,1536]{1,0:T(8,128)(2,1)S(1)}, bf16[16,1536]{1,0:T(8,128)(2,1)S(1)}, u32[]{:S(2)}, u32[]{:S(2)}) collective-permute-start(bf16[16,1536]{1,0:T(8,128)(2,1)S(1)} %get-tuple-element.152), channel_id=1, source_target_pairs={{0,3},{1,2},{2,1},{3,0},{4,7},{5,6},{6,5},{7,4},{8,11},{9,10},{10,... | collective-permute-start | bytes 147464 | tf_op jit(solution)/shard_map/ppermute | solution.py:743
  181.2 15.1 %collective-permute-start.35 = (bf16[16,2688]{1,0:T(8,128)(2,1)S(1)}, bf16[16,2688]{1,0:T(8,128)(2,1)S(1)}, u32[]{:S(2)}, u32[]{:S(2)}) collective-permute-start(bf16[16,2688]{1,0:T(8,128)(2,1)S(1)} %fusion.2), channel_id=1, source_target_pairs={{0,2},{1,3},{2,0},{3,1},{4,6},{5,7},{6,4},{7,5},{8,10},{9,11},{10,... | collective-permute-start | bytes 258056 | tf_op jit(solution)/shard_map/ppermute | solution.py:743
  (6 other events, 4.0 us)
Sparse Core Ops, SparseCore 0:
  11.6 77.5 all-gather.1
  130.1 25.6 reduce-scatter.4
  158.2 35.8 reduce-scatter.2
